TPU v7x, 512 devices: a whole 4x4x16 slice. The times are simulated.
512 devices in a mesh: dp: 8 (over y, core), fsdp: 64 (over x, z).
Axes of the slice: x: 4, y: 4, z: 16, core: 2. Of those that a mesh axis runs over, the one named last changes fastest.
Arguments:
- grads: bfloat16 [8, 64, 2048, 768], P('dp', None, 'fsdp'), as said below
- momentum: float32 [64, 2048, 768], P(None, ('fsdp', 'dp')), as said below
- slot_matrix: int32 [64], replicated, may hold values from 0 to 63, each once
Outputs:
- update: bfloat16 [64, 2048, 768], P(None, ('fsdp', 'dp'))
- new_momentum: float32 [64, 2048, 768], P(None, ('fsdp', 'dp'))
Inputs may be any that keep to these rules, and one draw needn't show every extreme that they name: `slot_matrix`: every matrix index appears in exactly one slot. `grads`: finite values. `momentum`: finite values.
All inputs are finite; a program needn't handle non-finite values.
Results may differ from a plain program's by a relative error of at most 0.025.
Values may be sent and summed in bfloat16 or wider, within the bound.
No kernel may reach another device: no remote copies, remote signals or barrier semaphores. Data moves between devices by JAX's collectives and lax.ppermute only.
A program may use at most 64 MiB of HBM per device.

v0:
```python
import math

import jax
import jax.numpy as jnp
from jax import lax
from jax.sharding import PartitionSpec as P

R = 2048
C = 768
ITERS = 2


coef_one = 3.4445
coef_two = -4.775
coef_three = 2.0315
decay_rate = 0.95


def polish(gram_total):
    trace_sum = jnp.trace(gram_total, axis1=1, axis2=2)
    inv_norm = 1.0 / (jnp.sqrt(trace_sum) + 1e-07)
    level_now = gram_total * (inv_norm * inv_norm)[:, None, None]
    identity = jnp.eye(gram_total.shape[1], dtype=jnp.float32)[None]
    total_now = None
    for step in range(ITERS):
        level_low = level_now.astype(jnp.bfloat16)
        square = jnp.einsum(
            "mij,mjk->mik", level_low, level_low, preferred_element_type=jnp.float32
        )
        poly_now = coef_one * identity + coef_two * level_now + coef_three * square
        poly_low = poly_now.astype(jnp.bfloat16)
        if step == 0:
            total_now = poly_now
        else:
            total_now = jnp.einsum(
                "mij,mjk->mik",
                total_now.astype(jnp.bfloat16),
                poly_low,
                preferred_element_type=jnp.float32,
            )
        if step + 1 < ITERS:
            left_half = jnp.einsum(
                "mij,mjk->mik", poly_low, level_low, preferred_element_type=jnp.float32
            ).astype(jnp.bfloat16)
            level_now = jnp.einsum(
                "mij,mjk->mik", left_half, poly_low, preferred_element_type=jnp.float32
            )
    return (inv_norm, total_now.astype(jnp.bfloat16))


def shards(grads, momentum, slot_matrix):
    summed = lax.psum_scatter(grads[0], "dp", scatter_dimension=1, tiled=True).astype(jnp.float32)
    gradient = jnp.zeros_like(summed).at[slot_matrix].set(summed)
    new_momentum = decay_rate * momentum + gradient
    nesterov = (gradient + decay_rate * new_momentum).astype(jnp.bfloat16)
    owned_rows = lax.all_to_all(nesterov, "fsdp", split_axis=0, concat_axis=1, tiled=True)
    piece = lax.all_gather(owned_rows, "dp", axis=1, tiled=True)
    gram_total = jnp.einsum("mrc,mrd->mcd", piece, piece, preferred_element_type=jnp.float32)
    inv_norm, total_low = polish(gram_total)
    factor = math.sqrt(max(R, C)) * inv_norm
    product = jnp.einsum("mrc,mcd->mrd", owned_rows, total_low, preferred_element_type=jnp.float32)
    update_rows = (product * factor[:, None, None]).astype(jnp.bfloat16)
    update = lax.all_to_all(update_rows, "fsdp", split_axis=1, concat_axis=0, tiled=True)
    return (update, new_momentum)


def solution(mesh):
    in_specs = (P("dp", None, "fsdp", None), P(None, ("fsdp", "dp"), None), P())
    out_specs = (P(None, ("fsdp", "dp"), None), P(None, ("fsdp", "dp"), None))
    return jax.shard_map(shards, mesh=mesh, in_specs=in_specs, out_specs=out_specs, check_vma=False)
```

profile of v0, /device:TPU:6, one launch (start us, length us, event | category | flops | bytes accessed | tf_op | source)
XLA Modules:
  0.0 210.7 jit_solution(9034453453086099385)
XLA Ops:
  7.2 0.0 reduce-scatter.2.cloned.1.call-start
  7.2 5.3 %copy.14 = bf16[1,64,32,768]{3,1,2,0:T(8,128)(2,1)} copy(bf16[1,64,32,768]{3,2,1,0:T(8,128)(2,1)} %param.3) | data formatting | bytes 6291456 | tf_op args[0]
  12.5 0.0 copy-start.1
  12.5 0.0 reduce-scatter.2.cloned.1.call-update
  12.5 0.0 copy-start
  12.5 0.0 all-gather.2.cloned.1.call-start
  12.6 0.6 copy-done.1
  13.2 47.3 %reduce-scatter.2.cloned.1.call-done = bf16[64,4,768]{2,0,1:T(8,128)(2,1)} async-done(((bf16[64,32,768]{2,0,1:T(8,128)(2,1)}), bf16[64,4,768]{2,0,1:T(8,128)(2,1)}) %reduce-scatter.2.cloned.1.call-update) | async-done | bytes 393232 | tf_op jit(solution)/shard_map/reduce_scatter | solution.py:52
  60.5 1.3 copy.9
  61.8 0.1 broadcast_in_dim.14
  61.9 2.5 %scatter_fusion = f32[64,4,768]{2,1,0:T(4,128)S(1)} fusion(f32[64,4,768]{2,1,0:T(4,128)S(1)} %broadcast_in_dim.14, s32[64]{0:T(128)S(1)} %compare_select_fusion, f32[64,4,768]{2,1,0:T(4,128)S(1)} %copy.9), kind=kCustom, calls=%fused_computation | custom fusion | bytes 2359552 | tf_op jit(solution)/shard_map/scatter | solution.py:53
  64.4 0.0 copy-done
  64.4 1.3 add_convert_fusion
  65.7 39.1 %all_to_all.24 = bf16[64,4,768]{2,1,0:T(4,128)(2,1)S(1)} all-to-all(bf16[64,4,768]{2,1,0:T(4,128)(2,1)S(1)} %get-tuple-element.2), channel_id=1, replica_groups=mesh['dp'=8,'fsdp'=64] {'fsdp'}, dimensions={0} | all-to-all | bytes 786432 | tf_op jit(solution)/shard_map/all_to_all | solution.py:56
  104.8 0.8 all_to_all.9
  105.7 0.0 all-gather.2.cloned.1.call-update
  105.7 0.1 reshape.83
  105.8 27.8 %all-gather.2.cloned.1.call-done = bf16[1,2048,768]{2,1,0:T(8,128)(2,1)} async-done(((bf16[1,256,768]{2,1,0:T(8,128)(2,1)}), bf16[1,2048,768]{2,1,0:T(8,128)(2,1)}) %all-gather.2.cloned.1.call-update) | async-done | bytes 3145744 | tf_op jit(solution)/shard_map/all_gather | solution.py:57
  133.6 6.1 %select_reduce_fusion = (f32[]{:T(128)}, f32[768,768]{1,0:T(8,128)S(1)}) fusion(bf16[1,2048,768]{2,1,0:T(8,128)(2,1)} %all-gather.2.cloned.1.call-done), kind=kOutput, calls=%fused_computation.10 | convolution fusion | flops 2417688576 | bytes 5505028 | tf_op jit(solution)/shard_map/mrc,mrd->mcd/dot_general | solution.py:58
  140.4 2.2 %fusion.3 = bf16[768,768]{1,0:T(8,128)(2,1)} fusion(f32[768,768]{1,0:T(8,128)S(1)} %get-tuple-element.5, f32[]{:T(128)S(6)} %mul.58), kind=kOutput, calls=%fused_computation.7 | convolution fusion | flops 911867904 | bytes 3538948 | tf_op jit(solution)/shard_map/mij,mjk->mik/dot_general | solution.py:27
  142.6 5.2 %fusion.9 = f32[768,768]{1,0:T(8,128)} fusion(bf16[768,768]{1,0:T(8,128)(2,1)} %fusion.3, f32[768,768]{1,0:T(8,128)S(1)} %get-tuple-element.5, f32[]{:T(128)S(6)} %mul.58), kind=kOutput, calls=%fused_computation.19 | convolution fusion | flops 1813708800 | bytes 5898244 | tf_op jit(solution)/shard_map/mij,mjk->mik/dot_general | solution.py:45
  147.8 0.0 copy-start.2
  147.8 4.3 %fusion.5 = bf16[768,768]{1,0:T(8,128)(2,1)S(1)} fusion(f32[768,768]{1,0:T(8,128)} %fusion.9), kind=kOutput, calls=%fused_computation.9 | convolution fusion | flops 910688256 | bytes 3538944 | tf_op jit(solution)/shard_map/mij,mjk->mik/dot_general | solution.py:27
  152.1 0.0 copy-done.2
  152.1 1.6 fusion.7
  153.7 0.6 copy.15
  154.3 0.5 broadcast.45
  154.8 3.0 %reduce.4 = bf16[256,768]{1,0:T(8,128)(2,1)S(1)} reduce(bf16[256,1,768]{2,1,0:T(2,128)(2,1)S(1)} %bitcast.21, bf16[]{:T(256)} %broadcast.45), dimensions={1}, to_apply=%bitcast.19.reduce_sub_computation | reduce | bytes 786434
  157.8 0.2 reshape.95
  158.1 42.3 %all_to_all.25 = bf16[64,2,1536]{2,1,0:T(2,128)(2,1)S(1)} all-to-all(bf16[64,2,1536]{2,1,0:T(2,128)(2,1)S(1)} %reshape.95), channel_id=1, replica_groups=mesh['dp'=8,'fsdp'=64] {'fsdp'}, dimensions={0} | all-to-all | bytes 786432 | tf_op jit(solution)/shard_map/all_to_all | solution.py:63
  200.4 0.3 reshape.96
  200.8 2.3 %bitcast_reduce_fusion = bf16[256,768]{1,0:T(8,128)(2,1)S(1)} fusion(bf16[256,1,768]{2,1,0:T(2,128)(2,1)S(1)} %reshape.96), kind=kLoop, calls=%fused_computation.23 | loop fusion | bytes 786432 | tf_op jit(solution)/shard_map/all_to_all | solution.py:63
  203.0 0.8 all_to_all.21
  (1 shorter events, 0.0 us)
Async XLA Ops:
  7.2 53.3 %reduce-scatter.2.cloned.1.call-start = ((), (), s32[]{:S(2)}) async-start(), calls=%async_computation.3 | async-start | bytes 3538944 | tf_op jit(solution)/shard_map/reduce_scatter | solution.py:52
  12.5 0.7 copy-start.1
  12.5 51.9 %copy-start = (f32[64,4,768]{2,1,0:T(4,128)S(1)}, f32[64,4,768]{2,1,0:T(4,128)}, u32[]{:S(2)}) copy-start(f32[64,4,768]{2,1,0:T(4,128)} %param.4) | copy-start | bytes 2359300
  12.5 121.0 %all-gather.2.cloned.1.call-start = ((), (), s32[]{:S(2)}) async-start(), calls=%async_computation.4 | async-start | bytes 3538944 | tf_op jit(solution)/shard_map/all_gather | solution.py:57
  147.8 4.3 %copy-start.2 = (bf16[768,768]{1,0:T(8,128)(2,1)S(1)}, bf16[768,768]{1,0:T(8,128)(2,1)}, u32[]{:S(2)}) copy-start(bf16[768,768]{1,0:T(8,128)(2,1)} %fusion.3) | copy-start | bytes 3538948
Sparse Core Ops, SparseCore 0:
  12.7 47.8 reduce-scatter.1
  105.8 27.6 all-gather.1
where the time goes:
time: 211 us
  blocking collectives  81.4 us (39%)
  waiting for transfers between devices  75.1 us (36%)
  matrix products  19.4 us (9%)
  local copies, waits for them, and re-layouts  15.5 us (7%)
  between operations  14.9 us (7%)
  other arithmetic  4.29 us (2%)
    reduce_scatter x1, waiting for transfers between devices, shards(): lax.psum_scatter(grads[0], 'dp', scatter_dimension=1, tiled=True)  47.3 us
    all_to_all x1, blocking collectives, shards(): lax.all_to_all(update_rows, 'fsdp', split_axis=1, concat_axis=0, tiled=True)  42.3 us
    all_to_all x1, blocking collectives, shards(): lax.all_to_all(nesterov, 'fsdp', split_axis=0, concat_axis=1, tiled=True)  39.1 us
    all_gather x1, waiting for transfers between devices, shards(): piece = lax.all_gather(owned_rows, 'dp', axis=1, tiled=True)  27.8 us
    unnamed x10, local copies, waits for them, and re-layouts  6.96 us
    dot_general x2, matrix products, polish(): jnp.einsum('mij,mjk->mik', level_low, level_low, preferred_element_type=j...  6.53 us
    dot_general x1, matrix products, shards(): jnp.einsum('mrc,mrd->mcd', piece, piece, preferred_element_type=jnp.float32)  6.11 us
    dot_general x1, matrix products, polish(): jnp.einsum('mij,mjk->mik', left_half, poly_low, preferred_element_type=jn...  5.16 us
  transfers between devices with their start and end apart: 2, of which 2 were waited for; matrix products, arithmetic and copies ran while one was open for 0% of the time, Pallas kernels for 0%

commit v1 on v0

v1 whole, which is shorter than its diff:
```python
import functools
import math

import jax
import jax.numpy as jnp
from jax import lax
from jax.experimental import pallas as pl
from jax.experimental.pallas import tpu as pltpu
from jax.sharding import PartitionSpec as P

NY = 4
NX = 4
COEF_A = 3.4445
COEF_B = -4.775
COEF_C = 2.0315
DECAY = 0.95
BF = jnp.bfloat16
F32 = jnp.float32
SMEM = pltpu.SMEM


def sds(shape, dtype):
    return jax.ShapeDtypeStruct(shape, dtype)


def params(mib=16):
    return pltpu.CompilerParams(vmem_limit_bytes=mib * 1024 * 1024)


def whole(n):
    return [pl.BlockSpec(memory_space=pltpu.VMEM)] * n


def split_kernel(pos, g_ref, send2, send013, keep2, keep013, scr):
    y = pos[0]
    c = pos[1]
    scr[...] = g_ref[0].astype(F32)

    def emit(low):
        slot = 0
        for rel in range(NY):
            yy = lax.rem(y + rel, NY)
            both = scr[:, pl.ds(pl.multiple_of(8 * yy, 8), 8), :]
            own = both[:, 4 * low : 4 * low + 4, :].astype(BF)
            other = both[:, 4 - 4 * low : 8 - 4 * low, :].astype(BF)
            if rel == 2:
                send2[...] = other
                keep2[...] = own
            else:
                send013[slot] = other
                keep013[slot] = own
                slot += 1

    pl.when(c == 0)(lambda: emit(0))
    pl.when(c == 1)(lambda: emit(1))


def split_rows(pos, grads, mb):
    _, m, rows, cols = grads.shape
    one = pl.BlockSpec((mb, 4, cols), lambda i: (i, 0, 0))
    three = pl.BlockSpec((3, mb, 4, cols), lambda i: (0, i, 0, 0))
    return pl.pallas_call(
        split_kernel,
        grid=(m // mb,),
        in_specs=[
            pl.BlockSpec(memory_space=SMEM),
            pl.BlockSpec((1, mb, rows, cols), lambda i: (0, i, 0, 0)),
        ],
        out_specs=[one, three, one, three],
        out_shape=[
            sds((m, 4, cols), BF),
            sds((3, m, 4, cols), BF),
            sds((m, 4, cols), BF),
            sds((3, m, 4, cols), BF),
        ],
        scratch_shapes=[pltpu.VMEM((mb, rows, cols), F32)],
        compiler_params=params(),
        name="split_rows",
    )(pos, grads)


def momentum_kernel(nz, pos, slots, own, dir_a, rel_a, dir_b, rel_b, mom, n0, n1, n2, n3, new_mom, total, inv):
    x = pos[2]
    m = mom.shape[0]
    h = m // 2

    def invert(j, carry):
        inv[slots[j]] = j
        return carry

    lax.fori_loop(0, m, invert, 0)

    def add_up(j, carry):
        total[j] = own[j] + dir_a[j].astype(F32) + rel_a[j].astype(F32)
        total[h + j] = own[h + j] + dir_b[j].astype(F32) + rel_b[j].astype(F32)
        return carry

    lax.fori_loop(0, h, add_up, 0, unroll=min(4, h))
    for rel, out in enumerate((n0, n1, n2, n3)):
        base = lax.rem(x + rel, NX) * nz

        def step(z, carry, out=out, base=base):
            mat = base + z
            gradient = total[inv[mat]]
            new = DECAY * mom[mat] + gradient
            new_mom[mat] = new
            out[z] = (gradient + DECAY * new).astype(BF)
            return carry

        lax.fori_loop(0, nz, step, 0, unroll=min(4, nz))


def momentum_step(nz, pos, slots, own, dir_a, rel_a, dir_b, rel_b, mom):
    m, _, cols = mom.shape
    return pl.pallas_call(
        functools.partial(momentum_kernel, nz),
        in_specs=[pl.BlockSpec(memory_space=SMEM)] * 2 + whole(6),
        out_specs=whole(5),
        out_shape=[sds((nz, 4, cols), BF)] * 4 + [sds((m, 4, cols), F32)],
        scratch_shapes=[pltpu.VMEM((m, 4, cols), F32), pltpu.SMEM((m,), jnp.int32)],
        compiler_params=params(),
        name="momentum_step",
    )(pos, slots, own, dir_a, rel_a, dir_b, rel_b, mom)


def pack_z_kernel(a0, a1, a2, a3, out):
    nz = a0.shape[0]
    for rel, ref in enumerate((a0, a1, a2, a3)):
        for z in range(nz):
            out[NX * z + rel] = ref[z]


def pack_z(parts):
    nz, _, cols = parts[0].shape
    return pl.pallas_call(
        pack_z_kernel,
        in_specs=whole(4),
        out_specs=whole(1)[0],
        out_shape=sds((NX * nz, 4, cols), BF),
        compiler_params=params(),
        name="pack_z",
    )(*parts)


def pack_x_kernel(*refs):
    ins, outs = refs[:-4], refs[-4:]
    for rel, out in enumerate(outs):
        for k, ref in enumerate(ins):
            out[k] = ref[rel]


def pack_x(parts):
    nz = len(parts)
    cols = parts[0].shape[2]
    return pl.pallas_call(
        pack_x_kernel,
        in_specs=whole(nz),
        out_specs=whole(4),
        out_shape=[sds((nz, 4, cols), BF)] * 4,
        compiler_params=params(),
        name="pack_x",
    )(*parts)


def place_kernel(pos, q0, q1, q2, q3, out):
    x = pos[2]
    z = pos[3]
    nz = q0.shape[0]
    for rel, ref in enumerate((q0, q1, q2, q3)):
        base = lax.rem(x + rel, NX) * nz
        for k in range(nz):
            out[base + lax.rem(z - k + nz, nz)] = ref[k]


def place(pos, parts):
    nz, _, cols = parts[0].shape
    return pl.pallas_call(
        place_kernel,
        in_specs=[pl.BlockSpec(memory_space=SMEM)] + whole(4),
        out_specs=whole(1)[0],
        out_shape=sds((NX * nz, 4, cols), BF),
        compiler_params=params(),
        name="place",
    )(pos, *parts)


def blocks_of(cols):
    n = cols // 128
    return [(i, j) for i in range(n) for j in range(i, n)]


def gram_kernel(pos, a_ref, rows_ref, send, keep, slabs):
    c = pos[1]
    count, _, cols = a_ref.shape
    for g in range(count // 4):
        four = [a_ref[4 * g + i].astype(F32) for i in range(4)]
        rows_ref[16 * g : 16 * g + 16, :] = jnp.concatenate(four, axis=0).astype(BF)
    n = cols // 128
    b = 0
    for i in range(n):
        strip = lax.dot_general(
            rows_ref[:, 128 * i : 128 * i + 128],
            rows_ref[:, 128 * i :],
            (((0,), (0,)), ((), ())),
            preferred_element_type=F32,
        )
        for j in range(i, n):
            block = strip[:, 128 * (j - i) : 128 * (j - i) + 128]
            for q in range(4):
                slabs[q, b] = block[32 * q : 32 * q + 32, :]
            b += 1
    send[...] = slabs[pl.ds(2 * (1 - c), 2)].astype(BF)
    keep[...] = slabs[pl.ds(2 * c, 2)]


def partial_gram(pos, a):
    count, _, cols = a.shape
    nb = len(blocks_of(cols))
    return pl.pallas_call(
        gram_kernel,
        in_specs=[pl.BlockSpec(memory_space=SMEM)] + whole(1),
        out_specs=whole(3),
        out_shape=[
            sds((4 * count, cols), BF),
            sds((2, nb, 32, 128), BF),
            sds((2, nb, 32, 128), F32),
        ],
        scratch_shapes=[pltpu.VMEM((4, nb, 32, 128), F32)],
        compiler_params=params(),
        name="partial_gram",
    )(pos, a)


def polish_kernel(nz, scale, pos, own, other, rows_ref, *rest):
    outs = rest[:nz]
    slabs, level, low, poly, high, result = rest[nz:]
    c = pos[1]
    z = pos[3]
    count, cols = rows_ref.shape
    n = cols // 128
    slabs[pl.ds(2 * c, 2)] = own[...].astype(F32)
    slabs[pl.ds(2 * (1 - c), 2)] = other[...].astype(F32)

    eye = (
        lax.broadcasted_iota(jnp.int32, (128, 128), 0) == lax.broadcasted_iota(jnp.int32, (128, 128), 1)
    )
    diag = jnp.zeros((128, 128), F32)
    for b, (i, j) in enumerate(blocks_of(cols)):
        if i == j:
            diag += slabs[:, b].reshape(128, 128)
    trace = jnp.sum(jnp.where(eye, diag, 0.0))
    inv_norm = 1.0 / (jnp.sqrt(jnp.full((1, 1), trace)) + 1e-7)
    square = inv_norm * inv_norm
    for b, (i, j) in enumerate(blocks_of(cols)):
        block = slabs[:, b].reshape(128, 128) * square
        level[128 * i : 128 * i + 128, 128 * j : 128 * j + 128] = block
        low[128 * i : 128 * i + 128, 128 * j : 128 * j + 128] = block.astype(BF)
        if i != j:
            block = block.T
            level[128 * j : 128 * j + 128, 128 * i : 128 * i + 128] = block
            low[128 * j : 128 * j + 128, 128 * i : 128 * i + 128] = block.astype(BF)

    step = 256 if cols % 256 == 0 else 128
    for r in range(0, cols, step):
        part = jnp.dot(low[r : r + step, :], low[...], preferred_element_type=F32)
        poly[r : r + step, :] = (COEF_B * level[r : r + step, :] + COEF_C * part).astype(BF)
    for r in range(0, cols, step):
        part = jnp.dot(poly[r : r + step, :], low[...], preferred_element_type=F32)
        left_now = COEF_A * level[r : r + step, :] + part
        left_low = left_now.astype(BF)
        high[r : r + step, :] = (
            COEF_A * left_now + jnp.dot(left_low, poly[...], preferred_element_type=F32)
        ).astype(BF)
    rows = rows_ref[...]
    y0 = COEF_A * rows.astype(F32) + jnp.dot(rows, poly[...], preferred_element_type=F32)
    result[...] = COEF_A * y0
    y1 = jnp.dot(y0.astype(BF), high[...], preferred_element_type=F32)
    result[...] += COEF_B * y1
    y2 = jnp.dot(y1.astype(BF), high[...], preferred_element_type=F32)
    result[...] = (result[...] + COEF_C * y2) * (scale * inv_norm)
    for k in range(nz):
        start = pl.multiple_of(16 * lax.rem(z + k, nz), 16)
        group = result[pl.ds(start, 16), :]
        for i in range(4):
            outs[k][i] = group[4 * i : 4 * i + 4, :].astype(BF)


def polish(nz, scale, pos, own, other, rows):
    count, cols = rows.shape
    nb = own.shape[1]
    return pl.pallas_call(
        functools.partial(polish_kernel, nz, scale),
        in_specs=[pl.BlockSpec(memory_space=SMEM)] + whole(3),
        out_specs=whole(nz),
        out_shape=[sds((4, 4, cols), BF)] * nz,
        scratch_shapes=[
            pltpu.VMEM((4, nb, 32, 128), F32),
            pltpu.VMEM((cols, cols), F32),
            pltpu.VMEM((cols, cols), BF),
            pltpu.VMEM((cols, cols), BF),
            pltpu.VMEM((cols, cols), BF),
            pltpu.VMEM((count, cols), F32),
        ],
        compiler_params=params(32),
        name="polish",
    )(pos, own, other, rows)


def shards(n_rows, grads, momentum, slot_matrix):
    m = grads.shape[1]
    cols = grads.shape[3]
    nf = m
    nz = nf // NX
    d = lax.axis_index("dp")
    f = lax.axis_index("fsdp")
    pos = jnp.stack([d // 2, d % 2, f // nz, f % nz]).astype(jnp.int32)
    h = m // 2

    def core_swap(v):
        return lax.ppermute(v, "dp", [(i, i ^ 1) for i in range(2 * NY)])

    def y_shift(v, by):
        return lax.ppermute(v, "dp", [(i, (i + 2 * by) % (2 * NY)) for i in range(2 * NY)])

    def y_pair(v, odd):
        perm = []
        for y in range(NY):
            to = (y ^ 1) if not odd else ((y + 1) % NY if y % 2 else (y - 1) % NY)
            perm += [(2 * y, 2 * to), (2 * y + 1, 2 * to + 1)]
        return lax.ppermute(v, "dp", perm)

    def x_shift(v, by):
        return lax.ppermute(v, "fsdp", [(i, (i + nz * by) % nf) for i in range(nf)])

    def z_shift(v, by):
        return lax.ppermute(v, "fsdp", [(i, i // nz * nz + (i % nz + by) % nz) for i in range(nf)])

    send2, send013, keep2, keep013 = split_rows(pos, grads, min(8, m))
    sum2 = keep2.astype(F32) + core_swap(send2).astype(F32)
    sum2 = sum2.astype(BF)
    relay_a = y_shift(sum2[:h], 1)
    relay_b = y_shift(sum2[h:], -1)
    sums = keep013.astype(F32) + core_swap(send013).astype(F32)
    dir_b = y_shift(sums[1, h:].astype(BF), 1)
    dir_a = y_shift(sums[2, :h].astype(BF), -1)
    rel_a = y_shift((sums[1, :h] + relay_a.astype(F32)).astype(BF), 1)
    rel_b = y_shift((sums[2, h:] + relay_b.astype(F32)).astype(BF), -1)
    parts = momentum_step(nz, pos, slot_matrix, sums[0], dir_a, rel_a, dir_b, rel_b, momentum)
    new_momentum = parts[4]

    arrived = [parts[0]] + [x_shift(parts[rel], rel) for rel in range(1, NX)]
    groups = [[nz * x + z for z in range(nz)] for x in range(NX)]
    mine = lax.all_to_all(
        pack_z(arrived), "fsdp", split_axis=0, concat_axis=0, axis_index_groups=groups, tiled=True
    )

    rows, gram_send, gram_keep = partial_gram(pos, mine)
    gram = gram_keep + core_swap(gram_send).astype(F32)
    one, two = gram[0], gram[1]
    one_in, two_in = y_pair(one.astype(BF), False), y_pair(two.astype(BF), True)
    one = one + one_in.astype(F32)
    two = two + two_in.astype(F32)
    one_in, two_in = y_pair(one.astype(BF), True), y_pair(two.astype(BF), False)
    one = one + one_in.astype(F32)
    two = two + two_in.astype(F32)
    own = jnp.stack([one, two]).astype(BF)
    other = core_swap(own)

    pieces = polish(nz, math.sqrt(max(n_rows, cols)), pos, own, other, rows)
    back = [pieces[0]] + [z_shift(pieces[k], k) for k in range(1, nz)]
    packed = pack_x(back)
    home = [packed[0]] + [x_shift(packed[rel], -rel) for rel in range(1, NX)]
    return (place(pos, home), new_momentum)


def solution(mesh):
    in_specs = (P("dp", None, "fsdp", None), P(None, ("fsdp", "dp"), None), P())
    out_specs = (P(None, ("fsdp", "dp"), None), P(None, ("fsdp", "dp"), None))

    def run(grads, momentum, slot_matrix):
        body = functools.partial(shards, grads.shape[2])
        return jax.shard_map(body, mesh=mesh, in_specs=in_specs, out_specs=out_specs, check_vma=False)(
            grads, momentum, slot_matrix
        )

    return run
```

time: 211 us -> 227 us (1.076)
  starting transfers between devices: 0.08 us -> 136 us
  blocking collectives: 81.4 us -> 35 us
  waiting for transfers between devices: 75.1 us -> 36.4 us
  matrix products: 19.4 us -> 0 us
  between operations: 14.9 us -> 1.21 us
  local copies, waits for them, and re-layouts: 15.5 us -> 2.29 us
  Pallas kernels: 0 us -> 12 us
  other arithmetic: 4.29 us -> 1.67 us
    ppermute x0 -> x35, starting transfers between devices: none -> 136 us  [the longest x15 75.4 us: z_shift(): lax.ppermute(v, 'fsdp', [(i, i // nz * nz + (i % nz + by) % nz) for i in...]
    reduce_scatter x1 -> x0, waiting for transfers between devices: 47.3 us -> none  [shards(): lax.psum_scatter(grads[0], 'dp', scatter_dimension=1, tiled=True)]
    all_to_all x2 -> x1, blocking collectives: 81.4 us -> 35 us  [shards(): lax.all_to_all(pack_z(arrived), 'fsdp', split_axis=0, concat_axis=0, axis...]
    ppermute x0 -> x35, waiting for transfers between devices: none -> 36.4 us  [the longest x6 10.2 us: y_shift(): lax.ppermute(v, 'dp', [(i, (i + 2 * by) % (2 * NY)) for i in range(2 * NY)])]
    all_gather x1 -> x0, waiting for transfers between devices: 27.8 us -> none  [shards(): piece = lax.all_gather(owned_rows, 'dp', axis=1, tiled=True)]
    dot_general x5 -> x0, matrix products: 19.4 us -> none  [the longest x2 6.53 us: polish(): jnp.einsum('mij,mjk->mik', level_low, level_low, preferred_element_type=j...]
    pallas_call x0 -> x7, Pallas kernels: none -> 12 us  [the longest x1 5.11 us: polish(): pl.pallas_call(functools.partial(polish_kernel, nz, scale), in_specs=[pl....]
    unnamed x10 -> x6, local copies, waits for them, and re-layouts: 6.96 us -> 1.9 us
  transfers between devices with their start and end apart: 2 -> 35, of which waited for: 2 -> 17; matrix products, arithmetic and copies ran while one was open for 0% -> 1% of each run, Pallas kernels for 0% -> 0%
where the time goes in v1:
time: 227 us; the launch traced here: 225 us
  starting transfers between devices  136 us (60%)
  waiting for transfers between devices  36.4 us (16%)
  blocking collectives  35 us (15%)
  Pallas kernels  12 us (5%)
  local copies, waits for them, and re-layouts  2.29 us (1%)
    ppermute x15, starting transfers between devices, z_shift(): lax.ppermute(v, 'fsdp', [(i, i // nz * nz + (i % nz + by) % nz) for i in...  75.4 us
    all_to_all x1, blocking collectives, shards(): lax.all_to_all(pack_z(arrived), 'fsdp', split_axis=0, concat_axis=0, axis...  35 us
    ppermute x6, starting transfers between devices, y_shift(): lax.ppermute(v, 'dp', [(i, (i + 2 * by) % (2 * NY)) for i in range(2 * NY)])  19.9 us
    ppermute x6, starting transfers between devices, x_shift(): return lax.ppermute(v, 'fsdp', [(i, (i + nz * by) % nf) for i in range(nf)])  18.7 us
    ppermute x4, starting transfers between devices, y_pair(): return lax.ppermute(v, 'dp', perm)  14 us
    ppermute x6, waiting for transfers between devices, y_shift(): lax.ppermute(v, 'dp', [(i, (i + 2 * by) % (2 * NY)) for i in range(2 * NY)])  10.2 us
    ppermute x4, waiting for transfers between devices, y_pair(): return lax.ppermute(v, 'dp', perm)  10 us
    ppermute x6, waiting for transfers between devices, x_shift(): return lax.ppermute(v, 'fsdp', [(i, (i + nz * by) % nf) for i in range(nf)])  8.36 us
  transfers between devices with their start and end apart: 35, of which 17 were waited for; matrix products, arithmetic and copies ran while one was open for 1% of the time, Pallas kernels for 0%

profile of v1, /device:TPU:6, one launch (start us, length us, event | category | flops | bytes accessed | tf_op | source)
XLA Modules:
  0.0 224.7 jit_solution(17242500161550112500)
XLA Ops:
  0.7 1.9 copy-done
  2.6 1.9 split_rows.1
  4.5 1.9 collective-permute-start
  6.4 2.4 %collective-permute-start.2 = (bf16[64,4,768]{2,1,0:T(4,128)(2,1)S(1)}, bf16[64,4,768]{2,1,0:T(4,128)(2,1)S(1)}, u32[]{:S(2)}, u32[]{:S(2)}) collective-permute-start(bf16[64,4,768]{2,1,0:T(4,128)(2,1)S(1)} %get-tuple-element.37), channel_id=1, source_target_pairs={{0,64},{64,0},{128,192},{192,128},{256,320},{320,256},{384,448},{4... | collective-permute-start | bytes 1179656 | tf_op jit(solution)/shard_map/ppermute | solution.py:320
  10.5 4.9 %collective-permute-start.6 = (bf16[32,4,768]{2,1,0:T(4,128)(2,1)S(1)}, bf16[32,4,768]{2,1,0:T(4,128)(2,1)S(1)}, u32[]{:S(2)}, u32[]{:S(2)}) collective-permute-start(bf16[32,4,768]{2,1,0:T(4,128)(2,1)S(1)} %get-tuple-element.78), channel_id=1, source_target_pairs={{0,384},{64,448},{128,0},{192,64},{256,128},{320,192},{384,256},{4... | collective-permute-start | bytes 589832 | tf_op jit(solution)/shard_map/ppermute | solution.py:323
  15.5 1.9 collective-permute-start.3
  20.1 5.3 %collective-permute-done.3 = bf16[32,4,768]{2,1,0:T(4,128)(2,1)S(1)} collective-permute-done((bf16[32,4,768]{2,1,0:T(4,128)(2,1)S(1)}, bf16[32,4,768]{2,1,0:T(4,128)(2,1)S(1)}, u32[]{:S(2)}, u32[]{:S(2)}) %collective-permute-start.3) | collective-permute-done | bytes 196640 | tf_op jit(solution)/shard_map/ppermute | solution.py:323
  25.7 2.1 collective-permute-start.7
  27.8 3.9 %collective-permute-start.4 = (bf16[32,4,768]{2,1,0:T(4,128)(2,1)S(1)}, bf16[32,4,768]{2,1,0:T(4,128)(2,1)S(1)}, u32[]{:S(2)}, u32[]{:S(2)}) collective-permute-start(bf16[32,4,768]{2,1,0:T(4,128)(2,1)S(1)} %get-tuple-element.67), channel_id=1, source_target_pairs={{0,128},{64,192},{128,256},{192,320},{256,384},{320,448},{384,0},{... | collective-permute-start | bytes 589832 | tf_op jit(solution)/shard_map/ppermute | solution.py:323
  31.7 1.9 collective-permute-start.5
  33.6 5.1 %collective-permute-start.1 = (bf16[32,4,768]{2,1,0:T(4,128)(2,1)S(1)}, bf16[32,4,768]{2,1,0:T(4,128)(2,1)S(1)}, u32[]{:S(2)}, u32[]{:S(2)}) collective-permute-start(bf16[32,4,768]{2,1,0:T(4,128)(2,1)S(1)} %get-tuple-element.71), channel_id=1, source_target_pairs={{0,384},{64,448},{128,0},{192,64},{256,128},{320,192},{384,256},{4... | collective-permute-start | bytes 589832 | tf_op jit(solution)/shard_map/ppermute | solution.py:323
  38.8 2.3 %collective-permute-done.5.dir_b = bf16[32,4,768]{2,1,0:T(4,128)(2,1)S(1)} collective-permute-done((bf16[32,4,768]{2,1,0:T(4,128)(2,1)S(1)}, bf16[32,4,768]{2,1,0:T(4,128)(2,1)S(1)}, u32[]{:S(2)}, u32[]{:S(2)}) %collective-permute-start.5) | collective-permute-done | bytes 196640 | tf_op jit(solution)/shard_map/ppermute | solution.py:323
  41.9 2.5 %momentum_step.1 = (bf16[16,4,768]{2,1,0:T(4,128)(2,1)S(1)}, bf16[16,4,768]{2,1,0:T(4,128)(2,1)S(1)}, bf16[16,4,768]{2,1,0:T(4,128)(2,1)S(1)}, bf16[16,4,768]{2,1,0:T(4,128)(2,1)S(1)}, f32[64,4,768]{2,1,0:T(4,128)}) custom-call(s32[4]{0:T(128)S(1)} %pad_add_fusion.pos, s32[64]{0:T(128)S(1)} %copy-done.2, f32[64,4,768]{2,1,0:T(4,128)S(1)} %slice_bitcast_fusion.own, ...), custom_call_target="tpu_custom_call" | custom-call | tf_op jit(solution)/shard_map/momentum_step/pallas_call | solution.py:115
  44.4 5.0 %collective-permute-start.8 = (bf16[16,4,768]{2,1,0:T(4,128)(2,1)S(1)}, bf16[16,4,768]{2,1,0:T(4,128)(2,1)S(1)}, u32[]{:S(2)}, u32[]{:S(2)}) collective-permute-start(bf16[16,4,768]{2,1,0:T(4,128)(2,1)S(1)} %get-tuple-element.39), channel_id=1, source_target_pairs={{0,16},{1,17},{2,18},{3,19},{4,20},{5,21},{6,22},{7,23},{8,24},{9,... | collective-permute-start | bytes 294920 | tf_op jit(solution)/shard_map/ppermute | solution.py:333
  49.5 1.9 collective-permute-start.9
  51.4 2.8 %collective-permute-start.10 = (bf16[16,4,768]{2,1,0:T(4,128)(2,1)S(1)}, bf16[16,4,768]{2,1,0:T(4,128)(2,1)S(1)}, u32[]{:S(2)}, u32[]{:S(2)}) collective-permute-start(bf16[16,4,768]{2,1,0:T(4,128)(2,1)S(1)} %get-tuple-element.41), channel_id=1, source_target_pairs={{0,48},{1,49},{2,50},{3,51},{4,52},{5,53},{6,54},{7,55},{8,56},{9,... | collective-permute-start | bytes 294920 | tf_op jit(solution)/shard_map/ppermute | solution.py:333
  54.2 3.5 %collective-permute-done.9.a2 = bf16[16,4,768]{2,1,0:T(4,128)(2,1)S(1)} collective-permute-done((bf16[16,4,768]{2,1,0:T(4,128)(2,1)S(1)}, bf16[16,4,768]{2,1,0:T(4,128)(2,1)S(1)}, u32[]{:S(2)}, u32[]{:S(2)}) %collective-permute-start.9) | collective-permute-done | bytes 98336 | tf_op jit(solution)/shard_map/ppermute | solution.py:333
  59.2 35.0 %all_to_all.5.a_ref = bf16[64,4,768]{2,1,0:T(4,128)(2,1)S(1)} all-to-all(bf16[64,4,768]{2,1,0:T(4,128)(2,1)S(1)} %pack_z.1), channel_id=1, replica_groups={{0,1,2,3,4,5,6,7,8,9,10,11,12,13,14,15},{16,17,18,19,20,21,22,23,24,25,..., dimensions={0} | all-to-all | bytes 786432 | tf_op jit(solution)/shard_map/all_to_all | solution.py:353
  95.2 1.9 collective-permute-start.11
  98.9 1.9 collective-permute-start.12
  100.9 5.3 %collective-permute-start.14 = (bf16[21,32,128]{2,1,0:T(8,128)(2,1)S(1)}, bf16[21,32,128]{2,1,0:T(8,128)(2,1)S(1)}, u32[]{:S(2)}, u32[]{:S(2)}) collective-permute-start(bf16[21,32,128]{2,1,0:T(8,128)(2,1)S(1)} %get-tuple-element.77), channel_id=1, source_target_pairs={{0,384},{64,448},{128,256},{192,320},{256,128},{320,192},{384,0},{... | collective-permute-start | bytes 516104 | tf_op jit(solution)/shard_map/ppermute | solution.py:330
  107.2 3.6 %collective-permute-done.14 = bf16[21,32,128]{2,1,0:T(8,128)(2,1)S(1)} collective-permute-done((bf16[21,32,128]{2,1,0:T(8,128)(2,1)S(1)}, bf16[21,32,128]{2,1,0:T(8,128)(2,1)S(1)}, u32[]{:S(2)}, u32[]{:S(2)}) %collective-permute-start.14) | collective-permute-done | bytes 172064 | tf_op jit(solution)/shard_map/ppermute | solution.py:330
  110.9 4.9 %collective-permute-start.13 = (bf16[21,32,128]{2,1,0:T(8,128)(2,1)S(1)}, bf16[21,32,128]{2,1,0:T(8,128)(2,1)S(1)}, u32[]{:S(2)}, u32[]{:S(2)}) collective-permute-start(bf16[21,32,128]{2,1,0:T(8,128)(2,1)S(1)} %get-tuple-element.74), channel_id=1, source_target_pairs={{0,384},{64,448},{128,256},{192,320},{256,128},{320,192},{384,0},{... | collective-permute-start | bytes 516104 | tf_op jit(solution)/shard_map/ppermute | solution.py:330
  115.8 1.9 collective-permute-start.15
  117.7 2.2 collective-permute-done.13
  120.0 3.1 %collective-permute-done.15 = bf16[21,32,128]{2,1,0:T(8,128)(2,1)S(1)} collective-permute-done((bf16[21,32,128]{2,1,0:T(8,128)(2,1)S(1)}, bf16[21,32,128]{2,1,0:T(8,128)(2,1)S(1)}, u32[]{:S(2)}, u32[]{:S(2)}) %collective-permute-start.15) | collective-permute-done | bytes 172064 | tf_op jit(solution)/shard_map/ppermute | solution.py:330
  123.3 1.9 collective-permute-start.16
  126.8 5.1 %polish.1 = (bf16[4,4,768]{2,1,0:T(4,128)(2,1)S(1)}, bf16[4,4,768]{2,1,0:T(4,128)(2,1)S(1)}, bf16[4,4,768]{2,1,0:T(4,128)(2,1)S(1)}, bf16[4,4,768]{2,1,0:T(4,128...) custom-call(s32[4]{0:T(128)S(1)} %pad_add_fusion.pos, ...), custom_call_target="tpu_custom_call" | custom-call | tf_op jit(solution)/shard_map/polish/pallas_call | solution.py:291
  132.0 4.2 %collective-permute-start.17 = (bf16[4,4,768]{2,1,0:T(4,128)(2,1)S(1)}, bf16[4,4,768]{2,1,0:T(4,128)(2,1)S(1)}, u32[]{:S(2)}, u32[]{:S(2)}) collective-permute-start(bf16[4,4,768]{2,1,0:T(4,128)(2,1)S(1)} %get-tuple-element.46), channel_id=1, source_target_pairs={{0,1},{1,2},{2,3},{3,4},{4,5},{5,6},{6,7},{7,8},{8,9},{9,10},{10,1... | collective-permute-start | bytes 73736 | tf_op jit(solution)/shard_map/ppermute | solution.py:336
  136.2 4.0 %collective-permute-start.18 = (bf16[4,4,768]{2,1,0:T(4,128)(2,1)S(1)}, bf16[4,4,768]{2,1,0:T(4,128)(2,1)S(1)}, u32[]{:S(2)}, u32[]{:S(2)}) collective-permute-start(bf16[4,4,768]{2,1,0:T(4,128)(2,1)S(1)} %get-tuple-element.47), channel_id=1, source_target_pairs={{0,2},{1,3},{2,4},{3,5},{4,6},{5,7},{6,8},{7,9},{8,10},{9,11},{10,... | collective-permute-start | bytes 73736 | tf_op jit(solution)/shard_map/ppermute | solution.py:336
  140.2 2.9 %collective-permute-start.19 = (bf16[4,4,768]{2,1,0:T(4,128)(2,1)S(1)}, bf16[4,4,768]{2,1,0:T(4,128)(2,1)S(1)}, u32[]{:S(2)}, u32[]{:S(2)}) collective-permute-start(bf16[4,4,768]{2,1,0:T(4,128)(2,1)S(1)} %get-tuple-element.48), channel_id=1, source_target_pairs={{0,3},{1,4},{2,5},{3,6},{4,7},{5,8},{6,9},{7,10},{8,11},{9,12},{10... | collective-permute-start | bytes 73736 | tf_op jit(solution)/shard_map/ppermute | solution.py:336
  143.1 5.3 %collective-permute-start.20 = (bf16[4,4,768]{2,1,0:T(4,128)(2,1)S(1)}, bf16[4,4,768]{2,1,0:T(4,128)(2,1)S(1)}, u32[]{:S(2)}, u32[]{:S(2)}) collective-permute-start(bf16[4,4,768]{2,1,0:T(4,128)(2,1)S(1)} %get-tuple-element.49), channel_id=1, source_target_pairs={{0,4},{1,5},{2,6},{3,7},{4,8},{5,9},{6,10},{7,11},{8,12},{9,13},{1... | collective-permute-start | bytes 73736 | tf_op jit(solution)/shard_map/ppermute | solution.py:336
  148.3 5.7 %collective-permute-start.21 = (bf16[4,4,768]{2,1,0:T(4,128)(2,1)S(1)}, bf16[4,4,768]{2,1,0:T(4,128)(2,1)S(1)}, u32[]{:S(2)}, u32[]{:S(2)}) collective-permute-start(bf16[4,4,768]{2,1,0:T(4,128)(2,1)S(1)} %get-tuple-element.50), channel_id=1, source_target_pairs={{0,5},{1,6},{2,7},{3,8},{4,9},{5,10},{6,11},{7,12},{8,13},{9,14},{... | collective-permute-start | bytes 73736 | tf_op jit(solution)/shard_map/ppermute | solution.py:336
  154.0 6.6 %collective-permute-start.22 = (bf16[4,4,768]{2,1,0:T(4,128)(2,1)S(1)}, bf16[4,4,768]{2,1,0:T(4,128)(2,1)S(1)}, u32[]{:S(2)}, u32[]{:S(2)}) collective-permute-start(bf16[4,4,768]{2,1,0:T(4,128)(2,1)S(1)} %get-tuple-element.51), channel_id=1, source_target_pairs={{0,6},{1,7},{2,8},{3,9},{4,10},{5,11},{6,12},{7,13},{8,14},{9,15},... | collective-permute-start | bytes 73736 | tf_op jit(solution)/shard_map/ppermute | solution.py:336
  160.6 7.0 %collective-permute-start.23 = (bf16[4,4,768]{2,1,0:T(4,128)(2,1)S(1)}, bf16[4,4,768]{2,1,0:T(4,128)(2,1)S(1)}, u32[]{:S(2)}, u32[]{:S(2)}) collective-permute-start(bf16[4,4,768]{2,1,0:T(4,128)(2,1)S(1)} %get-tuple-element.52), channel_id=1, source_target_pairs={{0,7},{1,8},{2,9},{3,10},{4,11},{5,12},{6,13},{7,14},{8,15},{9,0},... | collective-permute-start | bytes 73736 | tf_op jit(solution)/shard_map/ppermute | solution.py:336
  167.6 6.8 %collective-permute-start.24 = (bf16[4,4,768]{2,1,0:T(4,128)(2,1)S(1)}, bf16[4,4,768]{2,1,0:T(4,128)(2,1)S(1)}, u32[]{:S(2)}, u32[]{:S(2)}) collective-permute-start(bf16[4,4,768]{2,1,0:T(4,128)(2,1)S(1)} %get-tuple-element.53), channel_id=1, source_target_pairs={{0,8},{1,9},{2,10},{3,11},{4,12},{5,13},{6,14},{7,15},{8,0},{9,1},... | collective-permute-start | bytes 73736 | tf_op jit(solution)/shard_map/ppermute | solution.py:336
  174.4 8.0 %collective-permute-start.25 = (bf16[4,4,768]{2,1,0:T(4,128)(2,1)S(1)}, bf16[4,4,768]{2,1,0:T(4,128)(2,1)S(1)}, u32[]{:S(2)}, u32[]{:S(2)}) collective-permute-start(bf16[4,4,768]{2,1,0:T(4,128)(2,1)S(1)} %get-tuple-element.54), channel_id=1, source_target_pairs={{0,9},{1,10},{2,11},{3,12},{4,13},{5,14},{6,15},{7,0},{8,1},{9,2},... | collective-permute-start | bytes 73736 | tf_op jit(solution)/shard_map/ppermute | solution.py:336
  182.5 5.1 %collective-permute-start.26 = (bf16[4,4,768]{2,1,0:T(4,128)(2,1)S(1)}, bf16[4,4,768]{2,1,0:T(4,128)(2,1)S(1)}, u32[]{:S(2)}, u32[]{:S(2)}) collective-permute-start(bf16[4,4,768]{2,1,0:T(4,128)(2,1)S(1)} %get-tuple-element.55), channel_id=1, source_target_pairs={{0,10},{1,11},{2,12},{3,13},{4,14},{5,15},{6,0},{7,1},{8,2},{9,3},... | collective-permute-start | bytes 73736 | tf_op jit(solution)/shard_map/ppermute | solution.py:336
  187.6 6.2 %collective-permute-start.27 = (bf16[4,4,768]{2,1,0:T(4,128)(2,1)S(1)}, bf16[4,4,768]{2,1,0:T(4,128)(2,1)S(1)}, u32[]{:S(2)}, u32[]{:S(2)}) collective-permute-start(bf16[4,4,768]{2,1,0:T(4,128)(2,1)S(1)} %get-tuple-element.56), channel_id=1, source_target_pairs={{0,11},{1,12},{2,13},{3,14},{4,15},{5,0},{6,1},{7,2},{8,3},{9,4},{... | collective-permute-start | bytes 73736 | tf_op jit(solution)/shard_map/ppermute | solution.py:336
  193.8 4.3 %collective-permute-start.28 = (bf16[4,4,768]{2,1,0:T(4,128)(2,1)S(1)}, bf16[4,4,768]{2,1,0:T(4,128)(2,1)S(1)}, u32[]{:S(2)}, u32[]{:S(2)}) collective-permute-start(bf16[4,4,768]{2,1,0:T(4,128)(2,1)S(1)} %get-tuple-element.57), channel_id=1, source_target_pairs={{0,12},{1,13},{2,14},{3,15},{4,0},{5,1},{6,2},{7,3},{8,4},{9,5},{1... | collective-permute-start | bytes 73736 | tf_op jit(solution)/shard_map/ppermute | solution.py:336
  198.1 3.8 %collective-permute-start.29 = (bf16[4,4,768]{2,1,0:T(4,128)(2,1)S(1)}, bf16[4,4,768]{2,1,0:T(4,128)(2,1)S(1)}, u32[]{:S(2)}, u32[]{:S(2)}) collective-permute-start(bf16[4,4,768]{2,1,0:T(4,128)(2,1)S(1)} %get-tuple-element.58), channel_id=1, source_target_pairs={{0,13},{1,14},{2,15},{3,0},{4,1},{5,2},{6,3},{7,4},{8,5},{9,6},{10... | collective-permute-start | bytes 73736 | tf_op jit(solution)/shard_map/ppermute | solution.py:336
  202.0 3.1 %collective-permute-start.30 = (bf16[4,4,768]{2,1,0:T(4,128)(2,1)S(1)}, bf16[4,4,768]{2,1,0:T(4,128)(2,1)S(1)}, u32[]{:S(2)}, u32[]{:S(2)}) collective-permute-start(bf16[4,4,768]{2,1,0:T(4,128)(2,1)S(1)} %get-tuple-element.59), channel_id=1, source_target_pairs={{0,14},{1,15},{2,0},{3,1},{4,2},{5,3},{6,4},{7,5},{8,6},{9,7},{10,... | collective-permute-start | bytes 73736 | tf_op jit(solution)/shard_map/ppermute | solution.py:336
  205.1 2.5 %collective-permute-start.31 = (bf16[4,4,768]{2,1,0:T(4,128)(2,1)S(1)}, bf16[4,4,768]{2,1,0:T(4,128)(2,1)S(1)}, u32[]{:S(2)}, u32[]{:S(2)}) collective-permute-start(bf16[4,4,768]{2,1,0:T(4,128)(2,1)S(1)} %get-tuple-element.60), channel_id=1, source_target_pairs={{0,15},{1,0},{2,1},{3,2},{4,3},{5,4},{6,5},{7,6},{8,7},{9,8},{10,9... | collective-permute-start | bytes 73736 | tf_op jit(solution)/shard_map/ppermute | solution.py:336
  208.6 2.2 collective-permute-done.31.refs_15_
  210.9 1.9 collective-permute-start.32
  212.8 4.0 %collective-permute-start.33 = (bf16[16,4,768]{2,1,0:T(4,128)(2,1)S(1)}, bf16[16,4,768]{2,1,0:T(4,128)(2,1)S(1)}, u32[]{:S(2)}, u32[]{:S(2)}) collective-permute-start(bf16[16,4,768]{2,1,0:T(4,128)(2,1)S(1)} %get-tuple-element.63), channel_id=1, source_target_pairs={{0,32},{1,33},{2,34},{3,35},{4,36},{5,37},{6,38},{7,39},{8,40},{9,... | collective-permute-start | bytes 294920 | tf_op jit(solution)/shard_map/ppermute | solution.py:333
  216.8 3.1 %collective-permute-start.34 = (bf16[16,4,768]{2,1,0:T(4,128)(2,1)S(1)}, bf16[16,4,768]{2,1,0:T(4,128)(2,1)S(1)}, u32[]{:S(2)}, u32[]{:S(2)}) collective-permute-start(bf16[16,4,768]{2,1,0:T(4,128)(2,1)S(1)} %get-tuple-element.64), channel_id=1, source_target_pairs={{0,16},{1,17},{2,18},{3,19},{4,20},{5,21},{6,22},{7,23},{8,24},{9,... | collective-permute-start | bytes 294920 | tf_op jit(solution)/shard_map/ppermute | solution.py:333
  220.8 2.5 %collective-permute-done.34.q3 = bf16[16,4,768]{2,1,0:T(4,128)(2,1)S(1)} collective-permute-done((bf16[16,4,768]{2,1,0:T(4,128)(2,1)S(1)}, bf16[16,4,768]{2,1,0:T(4,128)(2,1)S(1)}, u32[]{:S(2)}, u32[]{:S(2)}) %collective-permute-start.34) | collective-permute-done | bytes 98336 | tf_op jit(solution)/shard_map/ppermute | solution.py:333
  (48 shorter events, 16.2 us)
Async XLA Ops:
  0.7 1.9 copy-start
  4.5 12.9 %collective-permute-start = (bf16[3,64,4,768]{3,2,1,0:T(4,128)(2,1)S(1)}, bf16[3,64,4,768]{3,2,1,0:T(4,128)(2,1)S(1)}, u32[]{:S(2)}, u32[]{:S(2)}) collective-permute-start(bf16[3,64,4,768]{3,2,1,0:T(4,128)(2,1)S(1)} %get-tuple-element.35), channel_id=1, source_target_pairs={{0,64},{64,0},{128,192},{192,128},{256,320},{320,256},{384,448},{4... | collective-permute-start | bytes 3538952 | tf_op jit(solution)/shard_map/ppermute | solution.py:320
  6.4 3.7 %collective-permute-start.2 = (bf16[64,4,768]{2,1,0:T(4,128)(2,1)S(1)}, bf16[64,4,768]{2,1,0:T(4,128)(2,1)S(1)}, u32[]{:S(2)}, u32[]{:S(2)}) collective-permute-start(bf16[64,4,768]{2,1,0:T(4,128)(2,1)S(1)} %get-tuple-element.37), channel_id=1, source_target_pairs={{0,64},{64,0},{128,192},{192,128},{256,320},{320,256},{384,448},{4... | collective-permute-start | bytes 1179656 | tf_op jit(solution)/shard_map/ppermute | solution.py:320
  10.5 9.6 %collective-permute-start.6 = (bf16[32,4,768]{2,1,0:T(4,128)(2,1)S(1)}, bf16[32,4,768]{2,1,0:T(4,128)(2,1)S(1)}, u32[]{:S(2)}, u32[]{:S(2)}) collective-permute-start(bf16[32,4,768]{2,1,0:T(4,128)(2,1)S(1)} %get-tuple-element.78), channel_id=1, source_target_pairs={{0,384},{64,448},{128,0},{192,64},{256,128},{320,192},{384,256},{4... | collective-permute-start | bytes 589832 | tf_op jit(solution)/shard_map/ppermute | solution.py:323
  15.5 10.0 %collective-permute-start.3 = (bf16[32,4,768]{2,1,0:T(4,128)(2,1)S(1)}, bf16[32,4,768]{2,1,0:T(4,128)(2,1)S(1)}, u32[]{:S(2)}, u32[]{:S(2)}) collective-permute-start(bf16[32,4,768]{2,1,0:T(4,128)(2,1)S(1)} %get-tuple-element.79), channel_id=1, source_target_pairs={{0,128},{64,192},{128,256},{192,320},{256,384},{320,448},{384,0},{... | collective-permute-start | bytes 589832 | tf_op jit(solution)/shard_map/ppermute | solution.py:323
  25.7 16.3 %copy-start.1 = (f32[64,4,768]{2,1,0:T(4,128)S(1)}, f32[64,4,768]{2,1,0:T(4,128)}, u32[]{:S(2)}) copy-start(f32[64,4,768]{2,1,0:T(4,128)} %mom.1) | copy-start | bytes 2359300
  25.7 16.2 %copy-start.2 = (s32[64]{0:T(128)S(1)}, s32[64]{0:T(128)}, u32[]{:S(2)}) copy-start(s32[64]{0:T(128)} %slots.1) | copy-start | bytes 772
  25.7 13.1 %collective-permute-start.7 = (bf16[32,4,768]{2,1,0:T(4,128)(2,1)S(1)}, bf16[32,4,768]{2,1,0:T(4,128)(2,1)S(1)}, u32[]{:S(2)}, u32[]{:S(2)}) collective-permute-start(bf16[32,4,768]{2,1,0:T(4,128)(2,1)S(1)} %get-tuple-element.66), channel_id=1, source_target_pairs={{0,384},{64,448},{128,0},{192,64},{256,128},{320,192},{384,256},{4... | collective-permute-start | bytes 589832 | tf_op jit(solution)/shard_map/ppermute | solution.py:323
  27.8 11.1 %collective-permute-start.4 = (bf16[32,4,768]{2,1,0:T(4,128)(2,1)S(1)}, bf16[32,4,768]{2,1,0:T(4,128)(2,1)S(1)}, u32[]{:S(2)}, u32[]{:S(2)}) collective-permute-start(bf16[32,4,768]{2,1,0:T(4,128)(2,1)S(1)} %get-tuple-element.67), channel_id=1, source_target_pairs={{0,128},{64,192},{128,256},{192,320},{256,384},{320,448},{384,0},{... | collective-permute-start | bytes 589832 | tf_op jit(solution)/shard_map/ppermute | solution.py:323
  31.7 9.4 %collective-permute-start.5 = (bf16[32,4,768]{2,1,0:T(4,128)(2,1)S(1)}, bf16[32,4,768]{2,1,0:T(4,128)(2,1)S(1)}, u32[]{:S(2)}, u32[]{:S(2)}) collective-permute-start(bf16[32,4,768]{2,1,0:T(4,128)(2,1)S(1)} %get-tuple-element.70), channel_id=1, source_target_pairs={{0,128},{64,192},{128,256},{192,320},{256,384},{320,448},{384,0},{... | collective-permute-start | bytes 589832 | tf_op jit(solution)/shard_map/ppermute | solution.py:323
  33.6 8.3 %collective-permute-start.1 = (bf16[32,4,768]{2,1,0:T(4,128)(2,1)S(1)}, bf16[32,4,768]{2,1,0:T(4,128)(2,1)S(1)}, u32[]{:S(2)}, u32[]{:S(2)}) collective-permute-start(bf16[32,4,768]{2,1,0:T(4,128)(2,1)S(1)} %get-tuple-element.71), channel_id=1, source_target_pairs={{0,384},{64,448},{128,0},{192,64},{256,128},{320,192},{384,256},{4... | collective-permute-start | bytes 589832 | tf_op jit(solution)/shard_map/ppermute | solution.py:323
  44.4 9.7 %collective-permute-start.8 = (bf16[16,4,768]{2,1,0:T(4,128)(2,1)S(1)}, bf16[16,4,768]{2,1,0:T(4,128)(2,1)S(1)}, u32[]{:S(2)}, u32[]{:S(2)}) collective-permute-start(bf16[16,4,768]{2,1,0:T(4,128)(2,1)S(1)} %get-tuple-element.39), channel_id=1, source_target_pairs={{0,16},{1,17},{2,18},{3,19},{4,20},{5,21},{6,22},{7,23},{8,24},{9,... | collective-permute-start | bytes 294920 | tf_op jit(solution)/shard_map/ppermute | solution.py:333
  49.5 8.2 %collective-permute-start.9 = (bf16[16,4,768]{2,1,0:T(4,128)(2,1)S(1)}, bf16[16,4,768]{2,1,0:T(4,128)(2,1)S(1)}, u32[]{:S(2)}, u32[]{:S(2)}) collective-permute-start(bf16[16,4,768]{2,1,0:T(4,128)(2,1)S(1)} %get-tuple-element.40), channel_id=1, source_target_pairs={{0,32},{1,33},{2,34},{3,35},{4,36},{5,37},{6,38},{7,39},{8,40},{9,... | collective-permute-start | bytes 294920 | tf_op jit(solution)/shard_map/ppermute | solution.py:333
  51.4 7.7 %collective-permute-start.10 = (bf16[16,4,768]{2,1,0:T(4,128)(2,1)S(1)}, bf16[16,4,768]{2,1,0:T(4,128)(2,1)S(1)}, u32[]{:S(2)}, u32[]{:S(2)}) collective-permute-start(bf16[16,4,768]{2,1,0:T(4,128)(2,1)S(1)} %get-tuple-element.41), channel_id=1, source_target_pairs={{0,48},{1,49},{2,50},{3,51},{4,52},{5,53},{6,54},{7,55},{8,56},{9,... | collective-permute-start | bytes 294920 | tf_op jit(solution)/shard_map/ppermute | solution.py:333
  95.2 3.5 %collective-permute-start.11 = (bf16[2,21,32,128]{3,2,1,0:T(8,128)(2,1)S(1)}, bf16[2,21,32,128]{3,2,1,0:T(8,128)(2,1)S(1)}, u32[]{:S(2)}, u32[]{:S(2)}) collective-permute-start(bf16[2,21,32,128]{3,2,1,0:T(8,128)(2,1)S(1)} %get-tuple-element.43), channel_id=1, source_target_pairs={{0,64},{64,0},{128,192},{192,128},{256,320},{320,256},{384,448},{4... | collective-permute-start | bytes 1032200 | tf_op jit(solution)/shard_map/ppermute | solution.py:320
  98.9 8.3 %collective-permute-start.12 = (bf16[21,32,128]{2,1,0:T(8,128)(2,1)S(1)}, bf16[21,32,128]{2,1,0:T(8,128)(2,1)S(1)}, u32[]{:S(2)}, u32[]{:S(2)}) collective-permute-start(bf16[21,32,128]{2,1,0:T(8,128)(2,1)S(1)} %get-tuple-element.76), channel_id=1, source_target_pairs={{0,128},{64,192},{128,0},{192,64},{256,384},{320,448},{384,256},{4... | collective-permute-start | bytes 516104 | tf_op jit(solution)/shard_map/ppermute | solution.py:330
  100.9 10.0 %collective-permute-start.14 = (bf16[21,32,128]{2,1,0:T(8,128)(2,1)S(1)}, bf16[21,32,128]{2,1,0:T(8,128)(2,1)S(1)}, u32[]{:S(2)}, u32[]{:S(2)}) collective-permute-start(bf16[21,32,128]{2,1,0:T(8,128)(2,1)S(1)} %get-tuple-element.77), channel_id=1, source_target_pairs={{0,384},{64,448},{128,256},{192,320},{256,128},{320,192},{384,0},{... | collective-permute-start | bytes 516104 | tf_op jit(solution)/shard_map/ppermute | solution.py:330
  110.9 9.0 %collective-permute-start.13 = (bf16[21,32,128]{2,1,0:T(8,128)(2,1)S(1)}, bf16[21,32,128]{2,1,0:T(8,128)(2,1)S(1)}, u32[]{:S(2)}, u32[]{:S(2)}) collective-permute-start(bf16[21,32,128]{2,1,0:T(8,128)(2,1)S(1)} %get-tuple-element.74), channel_id=1, source_target_pairs={{0,384},{64,448},{128,256},{192,320},{256,128},{320,192},{384,0},{... | collective-permute-start | bytes 516104 | tf_op jit(solution)/shard_map/ppermute | solution.py:330
  115.8 7.3 %collective-permute-start.15 = (bf16[21,32,128]{2,1,0:T(8,128)(2,1)S(1)}, bf16[21,32,128]{2,1,0:T(8,128)(2,1)S(1)}, u32[]{:S(2)}, u32[]{:S(2)}) collective-permute-start(bf16[21,32,128]{2,1,0:T(8,128)(2,1)S(1)} %get-tuple-element.75), channel_id=1, source_target_pairs={{0,128},{64,192},{128,0},{192,64},{256,384},{320,448},{384,256},{4... | collective-permute-start | bytes 516104 | tf_op jit(solution)/shard_map/ppermute | solution.py:330
  123.3 3.5 %collective-permute-start.16 = (bf16[2,21,32,128]{3,2,1,0:T(8,128)(2,1)S(1)}, bf16[2,21,32,128]{3,2,1,0:T(8,128)(2,1)S(1)}, u32[]{:S(2)}, u32[]{:S(2)}) collective-permute-start(bf16[2,21,32,128]{3,2,1,0:T(8,128)(2,1)S(1)} %pad_maximum_fusion.own), channel_id=1, source_target_pairs={{0,64},{64,0},{128,192},{192,128},{256,320},{320,256},{384,448},{4... | collective-permute-start | bytes 1032200 | tf_op jit(solution)/shard_map/ppermute | solution.py:320
  132.0 22.1 %collective-permute-start.17 = (bf16[4,4,768]{2,1,0:T(4,128)(2,1)S(1)}, bf16[4,4,768]{2,1,0:T(4,128)(2,1)S(1)}, u32[]{:S(2)}, u32[]{:S(2)}) collective-permute-start(bf16[4,4,768]{2,1,0:T(4,128)(2,1)S(1)} %get-tuple-element.46), channel_id=1, source_target_pairs={{0,1},{1,2},{2,3},{3,4},{4,5},{5,6},{6,7},{7,8},{8,9},{9,10},{10,1... | collective-permute-start | bytes 73736 | tf_op jit(solution)/shard_map/ppermute | solution.py:336
  136.2 24.5 %collective-permute-start.18 = (bf16[4,4,768]{2,1,0:T(4,128)(2,1)S(1)}, bf16[4,4,768]{2,1,0:T(4,128)(2,1)S(1)}, u32[]{:S(2)}, u32[]{:S(2)}) collective-permute-start(bf16[4,4,768]{2,1,0:T(4,128)(2,1)S(1)} %get-tuple-element.47), channel_id=1, source_target_pairs={{0,2},{1,3},{2,4},{3,5},{4,6},{5,7},{6,8},{7,9},{8,10},{9,11},{10,... | collective-permute-start | bytes 73736 | tf_op jit(solution)/shard_map/ppermute | solution.py:336
  140.2 27.5 %collective-permute-start.19 = (bf16[4,4,768]{2,1,0:T(4,128)(2,1)S(1)}, bf16[4,4,768]{2,1,0:T(4,128)(2,1)S(1)}, u32[]{:S(2)}, u32[]{:S(2)}) collective-permute-start(bf16[4,4,768]{2,1,0:T(4,128)(2,1)S(1)} %get-tuple-element.48), channel_id=1, source_target_pairs={{0,3},{1,4},{2,5},{3,6},{4,7},{5,8},{6,9},{7,10},{8,11},{9,12},{10... | collective-permute-start | bytes 73736 | tf_op jit(solution)/shard_map/ppermute | solution.py:336
  143.1 31.4 %collective-permute-start.20 = (bf16[4,4,768]{2,1,0:T(4,128)(2,1)S(1)}, bf16[4,4,768]{2,1,0:T(4,128)(2,1)S(1)}, u32[]{:S(2)}, u32[]{:S(2)}) collective-permute-start(bf16[4,4,768]{2,1,0:T(4,128)(2,1)S(1)} %get-tuple-element.49), channel_id=1, source_target_pairs={{0,4},{1,5},{2,6},{3,7},{4,8},{5,9},{6,10},{7,11},{8,12},{9,13},{1... | collective-permute-start | bytes 73736 | tf_op jit(solution)/shard_map/ppermute | solution.py:336
  148.3 34.2 %collective-permute-start.21 = (bf16[4,4,768]{2,1,0:T(4,128)(2,1)S(1)}, bf16[4,4,768]{2,1,0:T(4,128)(2,1)S(1)}, u32[]{:S(2)}, u32[]{:S(2)}) collective-permute-start(bf16[4,4,768]{2,1,0:T(4,128)(2,1)S(1)} %get-tuple-element.50), channel_id=1, source_target_pairs={{0,5},{1,6},{2,7},{3,8},{4,9},{5,10},{6,11},{7,12},{8,13},{9,14},{... | collective-permute-start | bytes 73736 | tf_op jit(solution)/shard_map/ppermute | solution.py:336
  154.0 33.6 %collective-permute-start.22 = (bf16[4,4,768]{2,1,0:T(4,128)(2,1)S(1)}, bf16[4,4,768]{2,1,0:T(4,128)(2,1)S(1)}, u32[]{:S(2)}, u32[]{:S(2)}) collective-permute-start(bf16[4,4,768]{2,1,0:T(4,128)(2,1)S(1)} %get-tuple-element.51), channel_id=1, source_target_pairs={{0,6},{1,7},{2,8},{3,9},{4,10},{5,11},{6,12},{7,13},{8,14},{9,15},... | collective-permute-start | bytes 73736 | tf_op jit(solution)/shard_map/ppermute | solution.py:336
  160.6 33.2 %collective-permute-start.23 = (bf16[4,4,768]{2,1,0:T(4,128)(2,1)S(1)}, bf16[4,4,768]{2,1,0:T(4,128)(2,1)S(1)}, u32[]{:S(2)}, u32[]{:S(2)}) collective-permute-start(bf16[4,4,768]{2,1,0:T(4,128)(2,1)S(1)} %get-tuple-element.52), channel_id=1, source_target_pairs={{0,7},{1,8},{2,9},{3,10},{4,11},{5,12},{6,13},{7,14},{8,15},{9,0},... | collective-permute-start | bytes 73736 | tf_op jit(solution)/shard_map/ppermute | solution.py:336
  167.6 30.5 %collective-permute-start.24 = (bf16[4,4,768]{2,1,0:T(4,128)(2,1)S(1)}, bf16[4,4,768]{2,1,0:T(4,128)(2,1)S(1)}, u32[]{:S(2)}, u32[]{:S(2)}) collective-permute-start(bf16[4,4,768]{2,1,0:T(4,128)(2,1)S(1)} %get-tuple-element.53), channel_id=1, source_target_pairs={{0,8},{1,9},{2,10},{3,11},{4,12},{5,13},{6,14},{7,15},{8,0},{9,1},... | collective-permute-start | bytes 73736 | tf_op jit(solution)/shard_map/ppermute | solution.py:336
  174.4 27.5 %collective-permute-start.25 = (bf16[4,4,768]{2,1,0:T(4,128)(2,1)S(1)}, bf16[4,4,768]{2,1,0:T(4,128)(2,1)S(1)}, u32[]{:S(2)}, u32[]{:S(2)}) collective-permute-start(bf16[4,4,768]{2,1,0:T(4,128)(2,1)S(1)} %get-tuple-element.54), channel_id=1, source_target_pairs={{0,9},{1,10},{2,11},{3,12},{4,13},{5,14},{6,15},{7,0},{8,1},{9,2},... | collective-permute-start | bytes 73736 | tf_op jit(solution)/shard_map/ppermute | solution.py:336
  182.5 22.6 %collective-permute-start.26 = (bf16[4,4,768]{2,1,0:T(4,128)(2,1)S(1)}, bf16[4,4,768]{2,1,0:T(4,128)(2,1)S(1)}, u32[]{:S(2)}, u32[]{:S(2)}) collective-permute-start(bf16[4,4,768]{2,1,0:T(4,128)(2,1)S(1)} %get-tuple-element.55), channel_id=1, source_target_pairs={{0,10},{1,11},{2,12},{3,13},{4,14},{5,15},{6,0},{7,1},{8,2},{9,3},... | collective-permute-start | bytes 73736 | tf_op jit(solution)/shard_map/ppermute | solution.py:336
  187.6 19.9 %collective-permute-start.27 = (bf16[4,4,768]{2,1,0:T(4,128)(2,1)S(1)}, bf16[4,4,768]{2,1,0:T(4,128)(2,1)S(1)}, u32[]{:S(2)}, u32[]{:S(2)}) collective-permute-start(bf16[4,4,768]{2,1,0:T(4,128)(2,1)S(1)} %get-tuple-element.56), channel_id=1, source_target_pairs={{0,11},{1,12},{2,13},{3,14},{4,15},{5,0},{6,1},{7,2},{8,3},{9,4},{... | collective-permute-start | bytes 73736 | tf_op jit(solution)/shard_map/ppermute | solution.py:336
  193.8 13.7 %collective-permute-start.28 = (bf16[4,4,768]{2,1,0:T(4,128)(2,1)S(1)}, bf16[4,4,768]{2,1,0:T(4,128)(2,1)S(1)}, u32[]{:S(2)}, u32[]{:S(2)}) collective-permute-start(bf16[4,4,768]{2,1,0:T(4,128)(2,1)S(1)} %get-tuple-element.57), channel_id=1, source_target_pairs={{0,12},{1,13},{2,14},{3,15},{4,0},{5,1},{6,2},{7,3},{8,4},{9,5},{1... | collective-permute-start | bytes 73736 | tf_op jit(solution)/shard_map/ppermute | solution.py:336
  198.1 9.5 %collective-permute-start.29 = (bf16[4,4,768]{2,1,0:T(4,128)(2,1)S(1)}, bf16[4,4,768]{2,1,0:T(4,128)(2,1)S(1)}, u32[]{:S(2)}, u32[]{:S(2)}) collective-permute-start(bf16[4,4,768]{2,1,0:T(4,128)(2,1)S(1)} %get-tuple-element.58), channel_id=1, source_target_pairs={{0,13},{1,14},{2,15},{3,0},{4,1},{5,2},{6,3},{7,4},{8,5},{9,6},{10... | collective-permute-start | bytes 73736 | tf_op jit(solution)/shard_map/ppermute | solution.py:336
  202.0 6.6 %collective-permute-start.30 = (bf16[4,4,768]{2,1,0:T(4,128)(2,1)S(1)}, bf16[4,4,768]{2,1,0:T(4,128)(2,1)S(1)}, u32[]{:S(2)}, u32[]{:S(2)}) collective-permute-start(bf16[4,4,768]{2,1,0:T(4,128)(2,1)S(1)} %get-tuple-element.59), channel_id=1, source_target_pairs={{0,14},{1,15},{2,0},{3,1},{4,2},{5,3},{6,4},{7,5},{8,6},{9,7},{10,... | collective-permute-start | bytes 73736 | tf_op jit(solution)/shard_map/ppermute | solution.py:336
  205.1 5.7 %collective-permute-start.31 = (bf16[4,4,768]{2,1,0:T(4,128)(2,1)S(1)}, bf16[4,4,768]{2,1,0:T(4,128)(2,1)S(1)}, u32[]{:S(2)}, u32[]{:S(2)}) collective-permute-start(bf16[4,4,768]{2,1,0:T(4,128)(2,1)S(1)} %get-tuple-element.60), channel_id=1, source_target_pairs={{0,15},{1,0},{2,1},{3,2},{4,3},{5,4},{6,5},{7,6},{8,7},{9,8},{10,9... | collective-permute-start | bytes 73736 | tf_op jit(solution)/shard_map/ppermute | solution.py:336
  210.9 9.0 %collective-permute-start.32 = (bf16[16,4,768]{2,1,0:T(4,128)(2,1)S(1)}, bf16[16,4,768]{2,1,0:T(4,128)(2,1)S(1)}, u32[]{:S(2)}, u32[]{:S(2)}) collective-permute-start(bf16[16,4,768]{2,1,0:T(4,128)(2,1)S(1)} %get-tuple-element.62), channel_id=1, source_target_pairs={{0,48},{1,49},{2,50},{3,51},{4,52},{5,53},{6,54},{7,55},{8,56},{9,... | collective-permute-start | bytes 294920 | tf_op jit(solution)/shard_map/ppermute | solution.py:333
  212.8 8.0 %collective-permute-start.33 = (bf16[16,4,768]{2,1,0:T(4,128)(2,1)S(1)}, bf16[16,4,768]{2,1,0:T(4,128)(2,1)S(1)}, u32[]{:S(2)}, u32[]{:S(2)}) collective-permute-start(bf16[16,4,768]{2,1,0:T(4,128)(2,1)S(1)} %get-tuple-element.63), channel_id=1, source_target_pairs={{0,32},{1,33},{2,34},{3,35},{4,36},{5,37},{6,38},{7,39},{8,40},{9,... | collective-permute-start | bytes 294920 | tf_op jit(solution)/shard_map/ppermute | solution.py:333
  216.8 6.5 %collective-permute-start.34 = (bf16[16,4,768]{2,1,0:T(4,128)(2,1)S(1)}, bf16[16,4,768]{2,1,0:T(4,128)(2,1)S(1)}, u32[]{:S(2)}, u32[]{:S(2)}) collective-permute-start(bf16[16,4,768]{2,1,0:T(4,128)(2,1)S(1)} %get-tuple-element.64), channel_id=1, source_target_pairs={{0,16},{1,17},{2,18},{3,19},{4,20},{5,21},{6,22},{7,23},{8,24},{9,... | collective-permute-start | bytes 294920 | tf_op jit(solution)/shard_map/ppermute | solution.py:333

commit v2 on v0

v2 whole, which is shorter than its diff:
```python
import functools
import math

import jax
import jax.numpy as jnp
from jax import lax
from jax.experimental import pallas as pl
from jax.experimental.pallas import tpu as pltpu
from jax.sharding import PartitionSpec as P

NY = 4
COEF_A = 3.4445
COEF_B = -4.775
COEF_C = 2.0315
DECAY = 0.95
BF = jnp.bfloat16
F32 = jnp.float32
SMEM = pltpu.SMEM


def sds(shape, dtype):
    return jax.ShapeDtypeStruct(shape, dtype)


def params(mib=16):
    return pltpu.CompilerParams(vmem_limit_bytes=mib * 1024 * 1024)


def whole(n):
    return [pl.BlockSpec(memory_space=pltpu.VMEM)] * n


def place_of():
    d = lax.axis_index("dp")
    y, c = lax.div(d, 2), lax.rem(d, 2)
    flip, turn = y + 1 - 2 * lax.rem(y, 2), NY - 1 - y
    near = jnp.where(c == 0, flip, turn)
    far = jnp.where(c == 0, turn, flip)
    return y, c, near, far, lax.rem(y + 2, NY)


def split_kernel(g_ref, send_a, send_b, keep_a, keep_b, scr):
    y, c, near, far, across = place_of()
    scr[...] = g_ref[0].astype(F32)

    def emit(low):
        def rows(yy, core):
            both = scr[:, pl.ds(pl.multiple_of(8 * yy, 8), 8), :]
            return both[:, 4 * core : 4 * core + 4, :].astype(BF)

        send_a[0] = rows(far, 1 - low)
        send_a[1] = rows(across, 1 - low)
        send_b[0] = rows(y, 1 - low)
        send_b[1] = rows(near, 1 - low)
        keep_a[0] = rows(near, low)
        keep_a[1] = rows(across, low)
        keep_b[0] = rows(y, low)
        keep_b[1] = rows(far, low)

    pl.when(c == 0)(lambda: emit(0))
    pl.when(c == 1)(lambda: emit(1))


def split_rows(grads, mb):
    _, m, rows, cols = grads.shape
    two = pl.BlockSpec((2, mb, 4, cols), lambda i: (0, i, 0, 0))
    return pl.pallas_call(
        split_kernel,
        grid=(m // mb,),
        in_specs=[pl.BlockSpec((1, mb, rows, cols), lambda i: (0, i, 0, 0))],
        out_specs=[two] * 4,
        out_shape=[sds((2, m, 4, cols), BF)] * 4,
        scratch_shapes=[pltpu.VMEM((mb, rows, cols), F32)],
        compiler_params=params(),
        name="split_rows",
    )(grads)


def momentum_kernel(slots, keep, swapped, first, second, mom, nesterov, new_mom):
    m = mom.shape[0]

    def step(j, carry):
        mat = slots[j]
        gradient = (keep[0, j].astype(F32) + swapped[0, j].astype(F32)) + (
            first[0, j].astype(F32) + second[j].astype(F32)
        )
        new = DECAY * mom[mat] + gradient
        new_mom[mat] = new
        nesterov[mat] = (gradient + DECAY * new).astype(BF)
        return carry

    lax.fori_loop(0, m, step, 0, unroll=min(8, m))


def momentum_step(slots, keep, swapped, first, second, mom):
    m, _, cols = mom.shape
    return pl.pallas_call(
        momentum_kernel,
        in_specs=[pl.BlockSpec(memory_space=SMEM)] + whole(5),
        out_specs=whole(2),
        out_shape=[sds((m, 4, cols), BF), sds((m, 4, cols), F32)],
        compiler_params=params(),
        name="momentum_step",
    )(slots, keep, swapped, first, second, mom)


def blocks_of(cols):
    n = cols // 128
    return [(i, j) for i in range(n) for j in range(i, n)]


def gram_kernel(a_ref, rows_ref, send, keep, slabs):
    c = lax.rem(lax.axis_index("dp"), 2)
    count, _, cols = a_ref.shape
    for g in range(count // 4):
        four = [a_ref[4 * g + i].astype(F32) for i in range(4)]
        rows_ref[16 * g : 16 * g + 16, :] = jnp.concatenate(four, axis=0).astype(BF)
    n = cols // 128
    b = 0
    for i in range(n):
        strip = lax.dot_general(
            rows_ref[:, 128 * i : 128 * i + 128],
            rows_ref[:, 128 * i :],
            (((0,), (0,)), ((), ())),
            preferred_element_type=F32,
        )
        for j in range(i, n):
            block = strip[:, 128 * (j - i) : 128 * (j - i) + 128]
            slabs[0, b] = block[:64, :]
            slabs[1, b] = block[64:, :]
            b += 1
    send[...] = slabs[1 - c].astype(BF)
    keep[...] = slabs[c]


def partial_gram(a):
    count, _, cols = a.shape
    nb = len(blocks_of(cols))
    return pl.pallas_call(
        gram_kernel,
        in_specs=whole(1),
        out_specs=whole(3),
        out_shape=[
            sds((4 * count, cols), BF),
            sds((nb, 64, 128), BF),
            sds((nb, 64, 128), F32),
        ],
        scratch_shapes=[pltpu.VMEM((2, nb, 64, 128), F32)],
        compiler_params=params(),
        name="partial_gram",
    )(a)


def polish_kernel(scale, own, other, rows_ref, out, slabs, level, low, poly, high):
    c = lax.rem(lax.axis_index("dp"), 2)
    count, cols = rows_ref.shape
    n = cols // 128
    slabs[c] = own[...].astype(F32)
    slabs[1 - c] = other[...].astype(F32)

    eye = (
        lax.broadcasted_iota(jnp.int32, (128, 128), 0) == lax.broadcasted_iota(jnp.int32, (128, 128), 1)
    )
    diag = jnp.zeros((128, 128), F32)
    for b, (i, j) in enumerate(blocks_of(cols)):
        if i == j:
            diag += slabs[:, b].reshape(128, 128)
    trace = jnp.sum(jnp.where(eye, diag, 0.0))
    inv_norm = 1.0 / (jnp.sqrt(jnp.full((1, 1), trace)) + 1e-7)
    square = inv_norm * inv_norm
    for b, (i, j) in enumerate(blocks_of(cols)):
        block = slabs[:, b].reshape(128, 128) * square
        level[128 * i : 128 * i + 128, 128 * j : 128 * j + 128] = block
        low[128 * i : 128 * i + 128, 128 * j : 128 * j + 128] = block.astype(BF)
        if i != j:
            block = block.T
            level[128 * j : 128 * j + 128, 128 * i : 128 * i + 128] = block
            low[128 * j : 128 * j + 128, 128 * i : 128 * i + 128] = block.astype(BF)

    step = 256 if cols % 256 == 0 else 128
    for r in range(0, cols, step):
        part = jnp.dot(low[r : r + step, :], low[...], preferred_element_type=F32)
        poly[r : r + step, :] = (COEF_B * level[r : r + step, :] + COEF_C * part).astype(BF)
    for r in range(0, cols, step):
        part = jnp.dot(poly[r : r + step, :], low[...], preferred_element_type=F32)
        left_now = COEF_A * level[r : r + step, :] + part
        left_low = left_now.astype(BF)
        high[r : r + step, :] = (
            COEF_A * left_now + jnp.dot(left_low, poly[...], preferred_element_type=F32)
        ).astype(BF)
    rows = rows_ref[...]
    y0 = COEF_A * rows.astype(F32) + jnp.dot(rows, poly[...], preferred_element_type=F32)
    y1 = jnp.dot(y0.astype(BF), high[...], preferred_element_type=F32)
    y2 = jnp.dot(y1.astype(BF), high[...], preferred_element_type=F32)
    result = (COEF_A * y0 + COEF_B * y1 + COEF_C * y2) * (scale * inv_norm)
    for i in range(count // 4):
        out[i] = result[4 * i : 4 * i + 4, :].astype(BF)


def polish(scale, own, other, rows):
    count, cols = rows.shape
    nb = own.shape[0]
    return pl.pallas_call(
        functools.partial(polish_kernel, scale),
        in_specs=whole(3),
        out_specs=whole(1)[0],
        out_shape=sds((count // 4, 4, cols), BF),
        scratch_shapes=[
            pltpu.VMEM((2, nb, 64, 128), F32),
            pltpu.VMEM((cols, cols), F32),
            pltpu.VMEM((cols, cols), BF),
            pltpu.VMEM((cols, cols), BF),
            pltpu.VMEM((cols, cols), BF),
        ],
        compiler_params=params(32),
        name="polish",
    )(own, other, rows)


def core_swap(v):
    return lax.ppermute(v, "dp", [(i, i ^ 1) for i in range(2 * NY)])


def y_swap(v, second):
    perm = []
    for y in range(NY):
        for c in range(2):
            to = (y ^ 1) if c == second else NY - 1 - y
            perm.append((2 * y + c, 2 * to + c))
    return lax.ppermute(v, "dp", perm)


def shards(n_rows, grads, momentum, slot_matrix):
    m = grads.shape[1]
    cols = grads.shape[3]

    send_a, send_b, keep_a, keep_b = split_rows(grads, min(8, m))
    swapped_a = core_swap(send_a)
    swapped_b = core_swap(send_b)
    first = y_swap((keep_a.astype(F32) + swapped_a.astype(F32)).astype(BF), 0)
    far = (keep_b[1].astype(F32) + swapped_b[1].astype(F32)) + first[1].astype(F32)
    second = y_swap(far.astype(BF), 1)
    nesterov, new_momentum = momentum_step(slot_matrix, keep_b, swapped_b, first, second, momentum)

    mine = lax.all_to_all(nesterov, "fsdp", split_axis=0, concat_axis=0, tiled=True)

    rows, gram_send, gram_keep = partial_gram(mine)
    gram = gram_keep + core_swap(gram_send).astype(F32)
    gram = gram + y_swap(gram.astype(BF), 0).astype(F32)
    gram = gram + y_swap(gram.astype(BF), 1).astype(F32)
    own = gram.astype(BF)
    other = core_swap(own)

    update = polish(math.sqrt(max(n_rows, cols)), own, other, rows)
    update = lax.all_to_all(update, "fsdp", split_axis=0, concat_axis=0, tiled=True)
    return (update, new_momentum)


def solution(mesh):
    in_specs = (P("dp", None, "fsdp", None), P(None, ("fsdp", "dp"), None), P())
    out_specs = (P(None, ("fsdp", "dp"), None), P(None, ("fsdp", "dp"), None))

    def run(grads, momentum, slot_matrix):
        body = functools.partial(shards, grads.shape[2])
        return jax.shard_map(body, mesh=mesh, in_specs=in_specs, out_specs=out_specs, check_vma=False)(
            grads, momentum, slot_matrix
        )

    return run
```

time: 211 us -> 145 us (0.69)
  waiting for transfers between devices: 75.1 us -> 31.7 us
  starting transfers between devices: 0.08 us -> 23.9 us
  matrix products: 19.4 us -> 0 us
  between operations: 14.9 us -> 0.79 us
  local copies, waits for them, and re-layouts: 15.5 us -> 2.64 us
  Pallas kernels: 0 us -> 8.37 us
  blocking collectives: 81.4 us -> 76.1 us
  other arithmetic: 4.29 us -> 1.14 us
    reduce_scatter x1 -> x0, waiting for transfers between devices: 47.3 us -> none  [shards(): lax.psum_scatter(grads[0], 'dp', scatter_dimension=1, tiled=True)]
    ppermute x0 -> x8, waiting for transfers between devices: none -> 31.7 us  [the longest x4 28.5 us: y_swap(): return lax.ppermute(v, 'dp', perm)]
    all_gather x1 -> x0, waiting for transfers between devices: 27.8 us -> none  [shards(): piece = lax.all_gather(owned_rows, 'dp', axis=1, tiled=True)]
    ppermute x0 -> x8, starting transfers between devices: none -> 23.9 us  [the longest x4 15.7 us: y_swap(): return lax.ppermute(v, 'dp', perm)]
    dot_general x5 -> x0, matrix products: 19.4 us -> none  [the longest x2 6.53 us: polish(): jnp.einsum('mij,mjk->mik', level_low, level_low, preferred_element_type=j...]
    pallas_call x0 -> x4, Pallas kernels: none -> 8.37 us  [the longest x1 4.48 us: polish(): pl.pallas_call(functools.partial(polish_kernel, scale), in_specs=whole(3)...]
    all_to_all x2, blocking collectives: 81.4 us -> 76.1 us  [the longest x1 43.1 us: shards(): lax.all_to_all(nesterov, 'fsdp', split_axis=0, concat_axis=0, tiled=True)]
    unnamed x10 -> x7, local copies, waits for them, and re-layouts: 6.96 us -> 2.64 us
  transfers between devices with their start and end apart: 2 -> 8, of which waited for: 2 -> 6; matrix products, arithmetic and copies ran while one was open for 0% -> 0% of each run, Pallas kernels for 0% -> 0%
where the time goes in v2:
time: 145 us
  blocking collectives  76.1 us (52%)
  waiting for transfers between devices  31.7 us (22%)
  starting transfers between devices  23.9 us (16%)
  Pallas kernels  8.37 us (6%)
  local copies, waits for them, and re-layouts  2.64 us (2%)
    all_to_all x1, blocking collectives, shards(): lax.all_to_all(nesterov, 'fsdp', split_axis=0, concat_axis=0, tiled=True)  43.1 us
    all_to_all x1, blocking collectives, shards(): lax.all_to_all(update, 'fsdp', split_axis=0, concat_axis=0, tiled=True)  33 us
    ppermute x4, waiting for transfers between devices, y_swap(): return lax.ppermute(v, 'dp', perm)  28.5 us
    ppermute x4, starting transfers between devices, y_swap(): return lax.ppermute(v, 'dp', perm)  15.7 us
    ppermute x4, starting transfers between devices, core_swap(): return lax.ppermute(v, 'dp', [(i, i ^ 1) for i in range(2 * NY)])  8.17 us
    pallas_call x1, Pallas kernels, polish(): pl.pallas_call(functools.partial(polish_kernel, scale), in_specs=whole(3)...  4.48 us
    ppermute x4, waiting for transfers between devices, core_swap(): return lax.ppermute(v, 'dp', [(i, i ^ 1) for i in range(2 * NY)])  3.24 us
  transfers between devices with their start and end apart: 8, of which 6 were waited for; matrix products, arithmetic and copies ran while one was open for 0% of the time, Pallas kernels for 0%

profile of v2, /device:TPU:6, one launch (start us, length us, event | category | flops | bytes accessed | tf_op | source)
XLA Modules:
  0.0 144.7 jit_solution(13495441678408803268)
XLA Ops:
  0.6 0.0 copy-start
  0.6 1.9 %copy-done = bf16[1,64,32,768]{3,2,1,0:T(8,128)(2,1)S(1)} copy-done((bf16[1,64,32,768]{3,2,1,0:T(8,128)(2,1)S(1)}, bf16[1,64,32,768]{3,2,1,0:T(8,128)(2,1)}, u32[]{:S(2)}) %copy-start) | copy-done | bytes 3145752
  2.5 1.4 split_rows.1
  3.9 1.9 %collective-permute-start.1 = (bf16[2,64,4,768]{3,2,1,0:T(4,128)(2,1)S(1)}, bf16[2,64,4,768]{3,2,1,0:T(4,128)(2,1)S(1)}, u32[]{:S(2)}, u32[]{:S(2)}) collective-permute-start(bf16[2,64,4,768]{3,2,1,0:T(4,128)(2,1)S(1)} %get-tuple-element.14), channel_id=1, source_target_pairs={{0,64},{64,0},{128,192},{192,128},{256,320},{320,256},{384,448},{4... | collective-permute-start | bytes 2359304 | tf_op jit(solution)/shard_map/ppermute | solution.py:221
  5.9 2.4 %collective-permute-start = (bf16[2,64,4,768]{3,2,1,0:T(4,128)(2,1)S(1)}, bf16[2,64,4,768]{3,2,1,0:T(4,128)(2,1)S(1)}, u32[]{:S(2)}, u32[]{:S(2)}) collective-permute-start(bf16[2,64,4,768]{3,2,1,0:T(4,128)(2,1)S(1)} %get-tuple-element.12), channel_id=1, source_target_pairs={{0,64},{64,0},{128,192},{192,128},{256,320},{320,256},{384,448},{4... | collective-permute-start | bytes 2359304 | tf_op jit(solution)/shard_map/ppermute | solution.py:221
  8.3 0.0 collective-permute-done.1
  8.3 0.0 copy-start.1
  8.3 0.0 copy-start.2
  8.3 0.4 add_convert_fusion
  8.7 3.5 %collective-permute-start.2 = (bf16[2,64,4,768]{3,2,1,0:T(4,128)(2,1)S(1)}, bf16[2,64,4,768]{3,2,1,0:T(4,128)(2,1)S(1)}, u32[]{:S(2)}, u32[]{:S(2)}) collective-permute-start(bf16[2,64,4,768]{3,2,1,0:T(4,128)(2,1)S(1)} %add_convert_fusion), channel_id=1, source_target_pairs={{0,128},{64,448},{128,0},{192,320},{256,384},{320,192},{384,256},{... | collective-permute-start | bytes 2359304 | tf_op jit(solution)/shard_map/ppermute | solution.py:230
  12.2 0.0 collective-permute-done.swapped
  12.2 10.4 %collective-permute-done.2.first = bf16[2,64,4,768]{3,2,1,0:T(4,128)(2,1)S(1)} collective-permute-done((bf16[2,64,4,768]{3,2,1,0:T(4,128)(2,1)S(1)}, bf16[2,64,4,768]{3,2,1,0:T(4,128)(2,1)S(1)}, u32[]{:S(2)}, u32[]{:S(2)}) %collective-permute-start.2) | collective-permute-done | bytes 786464 | tf_op jit(solution)/shard_map/ppermute | solution.py:230
  22.6 0.3 fusion.1
  22.9 4.9 %collective-permute-start.3 = (bf16[64,4,768]{2,1,0:T(4,128)(2,1)S(1)}, bf16[64,4,768]{2,1,0:T(4,128)(2,1)S(1)}, u32[]{:S(2)}, u32[]{:S(2)}) collective-permute-start(bf16[64,4,768]{2,1,0:T(4,128)(2,1)S(1)} %fusion.1), channel_id=1, source_target_pairs={{0,384},{64,192},{128,256},{192,64},{256,128},{320,448},{384,0},{4... | collective-permute-start | bytes 1179656 | tf_op jit(solution)/shard_map/ppermute | solution.py:230
  27.9 6.0 %collective-permute-done.3.second = bf16[64,4,768]{2,1,0:T(4,128)(2,1)S(1)} collective-permute-done((bf16[64,4,768]{2,1,0:T(4,128)(2,1)S(1)}, bf16[64,4,768]{2,1,0:T(4,128)(2,1)S(1)}, u32[]{:S(2)}, u32[]{:S(2)}) %collective-permute-start.3) | collective-permute-done | bytes 393248 | tf_op jit(solution)/shard_map/ppermute | solution.py:230
  33.8 0.0 copy-done.1
  33.8 0.0 copy-done.2
  33.8 1.9 %momentum_step.1 = (bf16[64,4,768]{2,1,0:T(4,128)(2,1)S(1)}, f32[64,4,768]{2,1,0:T(4,128)}) custom-call(s32[64]{0:T(128)S(1)} %copy-done.2, bf16[2,64,4,768]{3,2,1,0:T(4,128)(2,1)S(1)} %get-tuple-element.11.keep, bf16[2,64,4,768]{3,2,1,0:T(4,128)(2,1)S(1)} %collective-permute-done.swapped, bf16[2,64,4,768]{3,2,1,0:T(4,128)(2,1)S(1)} %collective-permute-done.2.first, ...), custom_call_target="tpu_custom_call" | custom-call | tf_op jit(solution)/shard_map/momentum_step/pallas_call | solution.py:97
  35.7 43.1 %all_to_all.10.a_ref = bf16[64,4,768]{2,1,0:T(4,128)(2,1)S(1)} all-to-all(bf16[64,4,768]{2,1,0:T(4,128)(2,1)S(1)} %get-tuple-element.15), channel_id=1, replica_groups=mesh['dp'=8,'fsdp'=64] {'fsdp'}, dimensions={0} | all-to-all | bytes 786432 | tf_op jit(solution)/shard_map/all_to_all | solution.py:245
  78.8 0.6 partial_gram.1
  79.4 1.9 %collective-permute-start.4 = (bf16[21,64,128]{2,1,0:T(8,128)(2,1)S(1)}, bf16[21,64,128]{2,1,0:T(8,128)(2,1)S(1)}, u32[]{:S(2)}, u32[]{:S(2)}) collective-permute-start(bf16[21,64,128]{2,1,0:T(8,128)(2,1)S(1)} %get-tuple-element.17), channel_id=1, source_target_pairs={{0,64},{64,0},{128,192},{192,128},{256,320},{320,256},{384,448},{4... | collective-permute-start | bytes 1032200 | tf_op jit(solution)/shard_map/ppermute | solution.py:221
  81.4 1.6 %collective-permute-done.4 = bf16[21,64,128]{2,1,0:T(8,128)(2,1)S(1)} collective-permute-done((bf16[21,64,128]{2,1,0:T(8,128)(2,1)S(1)}, bf16[21,64,128]{2,1,0:T(8,128)(2,1)S(1)}, u32[]{:S(2)}, u32[]{:S(2)}) %collective-permute-start.4) | collective-permute-done | bytes 344096 | tf_op jit(solution)/shard_map/ppermute | solution.py:221
  83.0 0.1 fusion
  83.1 2.5 %collective-permute-start.5 = (bf16[21,64,128]{2,1,0:T(8,128)(2,1)S(1)}, bf16[21,64,128]{2,1,0:T(8,128)(2,1)S(1)}, u32[]{:S(2)}, u32[]{:S(2)}) collective-permute-start(bf16[21,64,128]{2,1,0:T(8,128)(2,1)S(1)} %fusion), channel_id=1, source_target_pairs={{0,128},{64,448},{128,0},{192,320},{256,384},{320,192},{384,256},{... | collective-permute-start | bytes 1032200 | tf_op jit(solution)/shard_map/ppermute | solution.py:230
  85.5 6.7 %collective-permute-done.5 = bf16[21,64,128]{2,1,0:T(8,128)(2,1)S(1)} collective-permute-done((bf16[21,64,128]{2,1,0:T(8,128)(2,1)S(1)}, bf16[21,64,128]{2,1,0:T(8,128)(2,1)S(1)}, u32[]{:S(2)}, u32[]{:S(2)}) %collective-permute-start.5) | collective-permute-done | bytes 344096 | tf_op jit(solution)/shard_map/ppermute | solution.py:230
  92.2 0.1 fusion.2
  92.4 4.9 %collective-permute-start.6 = (bf16[21,64,128]{2,1,0:T(8,128)(2,1)S(1)}, bf16[21,64,128]{2,1,0:T(8,128)(2,1)S(1)}, u32[]{:S(2)}, u32[]{:S(2)}) collective-permute-start(bf16[21,64,128]{2,1,0:T(8,128)(2,1)S(1)} %fusion.2), channel_id=1, source_target_pairs={{0,384},{64,192},{128,256},{192,64},{256,128},{320,448},{384,0},{4... | collective-permute-start | bytes 1032200 | tf_op jit(solution)/shard_map/ppermute | solution.py:230
  97.2 5.5 %collective-permute-done.6 = bf16[21,64,128]{2,1,0:T(8,128)(2,1)S(1)} collective-permute-done((bf16[21,64,128]{2,1,0:T(8,128)(2,1)S(1)}, bf16[21,64,128]{2,1,0:T(8,128)(2,1)S(1)}, u32[]{:S(2)}, u32[]{:S(2)}) %collective-permute-start.6) | collective-permute-done | bytes 344096 | tf_op jit(solution)/shard_map/ppermute | solution.py:230
  102.7 0.2 add_convert_fusion.2.own
  102.9 1.9 %collective-permute-start.7 = (bf16[21,64,128]{2,1,0:T(8,128)(2,1)S(1)}, bf16[21,64,128]{2,1,0:T(8,128)(2,1)S(1)}, u32[]{:S(2)}, u32[]{:S(2)}) collective-permute-start(bf16[21,64,128]{2,1,0:T(8,128)(2,1)S(1)} %add_convert_fusion.2.own), channel_id=1, source_target_pairs={{0,64},{64,0},{128,192},{192,128},{256,320},{320,256},{384,448},{4... | collective-permute-start | bytes 1032200 | tf_op jit(solution)/shard_map/ppermute | solution.py:221
  104.8 1.6 %collective-permute-done.7.other = bf16[21,64,128]{2,1,0:T(8,128)(2,1)S(1)} collective-permute-done((bf16[21,64,128]{2,1,0:T(8,128)(2,1)S(1)}, bf16[21,64,128]{2,1,0:T(8,128)(2,1)S(1)}, u32[]{:S(2)}, u32[]{:S(2)}) %collective-permute-start.7) | collective-permute-done | bytes 344096 | tf_op jit(solution)/shard_map/ppermute | solution.py:221
  106.5 4.5 %polish.1 = bf16[64,4,768]{2,1,0:T(4,128)(2,1)S(1)} custom-call(bf16[21,64,128]{2,1,0:T(8,128)(2,1)S(1)} %add_convert_fusion.2.own, bf16[21,64,128]{2,1,0:T(8,128)(2,1)S(1)} %collective-permute-done.7.other, bf16[256,768]{1,0:T(8,128)(2,1)S(1)} %get-tuple-element.18.rows_ref), custom_call_target="tpu_custom_call" | custom-call | tf_op jit(solution)/shard_map/polish/pallas_call | solution.py:203
  111.0 33.0 %all_to_all.11 = bf16[64,4,768]{2,1,0:T(4,128)(2,1)S(1)} all-to-all(bf16[64,4,768]{2,1,0:T(4,128)(2,1)S(1)} %polish.1), channel_id=1, replica_groups=mesh['dp'=8,'fsdp'=64] {'fsdp'}, dimensions={0} | all-to-all | bytes 786432 | tf_op jit(solution)/shard_map/all_to_all | solution.py:255
  143.9 0.7 copy.6
Async XLA Ops:
  0.6 1.9 %copy-start = (bf16[1,64,32,768]{3,2,1,0:T(8,128)(2,1)S(1)}, bf16[1,64,32,768]{3,2,1,0:T(8,128)(2,1)}, u32[]{:S(2)}) copy-start(bf16[1,64,32,768]{3,2,1,0:T(8,128)(2,1)} %g_ref.1) | copy-start | bytes 9437188
  3.9 4.3 %collective-permute-start.1 = (bf16[2,64,4,768]{3,2,1,0:T(4,128)(2,1)S(1)}, bf16[2,64,4,768]{3,2,1,0:T(4,128)(2,1)S(1)}, u32[]{:S(2)}, u32[]{:S(2)}) collective-permute-start(bf16[2,64,4,768]{3,2,1,0:T(4,128)(2,1)S(1)} %get-tuple-element.14), channel_id=1, source_target_pairs={{0,64},{64,0},{128,192},{192,128},{256,320},{320,256},{384,448},{4... | collective-permute-start | bytes 2359304 | tf_op jit(solution)/shard_map/ppermute | solution.py:221
  5.9 6.4 %collective-permute-start = (bf16[2,64,4,768]{3,2,1,0:T(4,128)(2,1)S(1)}, bf16[2,64,4,768]{3,2,1,0:T(4,128)(2,1)S(1)}, u32[]{:S(2)}, u32[]{:S(2)}) collective-permute-start(bf16[2,64,4,768]{3,2,1,0:T(4,128)(2,1)S(1)} %get-tuple-element.12), channel_id=1, source_target_pairs={{0,64},{64,0},{128,192},{192,128},{256,320},{320,256},{384,448},{4... | collective-permute-start | bytes 2359304 | tf_op jit(solution)/shard_map/ppermute | solution.py:221
  8.3 25.5 %copy-start.1 = (f32[64,4,768]{2,1,0:T(4,128)S(1)}, f32[64,4,768]{2,1,0:T(4,128)}, u32[]{:S(2)}) copy-start(f32[64,4,768]{2,1,0:T(4,128)} %mom.1) | copy-start | bytes 2359300
  8.3 25.5 %copy-start.2 = (s32[64]{0:T(128)S(1)}, s32[64]{0:T(128)}, u32[]{:S(2)}) copy-start(s32[64]{0:T(128)} %slots.1) | copy-start | bytes 772
  8.7 13.9 %collective-permute-start.2 = (bf16[2,64,4,768]{3,2,1,0:T(4,128)(2,1)S(1)}, bf16[2,64,4,768]{3,2,1,0:T(4,128)(2,1)S(1)}, u32[]{:S(2)}, u32[]{:S(2)}) collective-permute-start(bf16[2,64,4,768]{3,2,1,0:T(4,128)(2,1)S(1)} %add_convert_fusion), channel_id=1, source_target_pairs={{0,128},{64,448},{128,0},{192,320},{256,384},{320,192},{384,256},{... | collective-permute-start | bytes 2359304 | tf_op jit(solution)/shard_map/ppermute | solution.py:230
  22.9 10.9 %collective-permute-start.3 = (bf16[64,4,768]{2,1,0:T(4,128)(2,1)S(1)}, bf16[64,4,768]{2,1,0:T(4,128)(2,1)S(1)}, u32[]{:S(2)}, u32[]{:S(2)}) collective-permute-start(bf16[64,4,768]{2,1,0:T(4,128)(2,1)S(1)} %fusion.1), channel_id=1, source_target_pairs={{0,384},{64,192},{128,256},{192,64},{256,128},{320,448},{384,0},{4... | collective-permute-start | bytes 1179656 | tf_op jit(solution)/shard_map/ppermute | solution.py:230
  79.4 3.5 %collective-permute-start.4 = (bf16[21,64,128]{2,1,0:T(8,128)(2,1)S(1)}, bf16[21,64,128]{2,1,0:T(8,128)(2,1)S(1)}, u32[]{:S(2)}, u32[]{:S(2)}) collective-permute-start(bf16[21,64,128]{2,1,0:T(8,128)(2,1)S(1)} %get-tuple-element.17), channel_id=1, source_target_pairs={{0,64},{64,0},{128,192},{192,128},{256,320},{320,256},{384,448},{4... | collective-permute-start | bytes 1032200 | tf_op jit(solution)/shard_map/ppermute | solution.py:221
  83.1 9.1 %collective-permute-start.5 = (bf16[21,64,128]{2,1,0:T(8,128)(2,1)S(1)}, bf16[21,64,128]{2,1,0:T(8,128)(2,1)S(1)}, u32[]{:S(2)}, u32[]{:S(2)}) collective-permute-start(bf16[21,64,128]{2,1,0:T(8,128)(2,1)S(1)} %fusion), channel_id=1, source_target_pairs={{0,128},{64,448},{128,0},{192,320},{256,384},{320,192},{384,256},{... | collective-permute-start | bytes 1032200 | tf_op jit(solution)/shard_map/ppermute | solution.py:230
  92.4 10.4 %collective-permute-start.6 = (bf16[21,64,128]{2,1,0:T(8,128)(2,1)S(1)}, bf16[21,64,128]{2,1,0:T(8,128)(2,1)S(1)}, u32[]{:S(2)}, u32[]{:S(2)}) collective-permute-start(bf16[21,64,128]{2,1,0:T(8,128)(2,1)S(1)} %fusion.2), channel_id=1, source_target_pairs={{0,384},{64,192},{128,256},{192,64},{256,128},{320,448},{384,0},{4... | collective-permute-start | bytes 1032200 | tf_op jit(solution)/shard_map/ppermute | solution.py:230
  102.9 3.5 %collective-permute-start.7 = (bf16[21,64,128]{2,1,0:T(8,128)(2,1)S(1)}, bf16[21,64,128]{2,1,0:T(8,128)(2,1)S(1)}, u32[]{:S(2)}, u32[]{:S(2)}) collective-permute-start(bf16[21,64,128]{2,1,0:T(8,128)(2,1)S(1)} %add_convert_fusion.2.own), channel_id=1, source_target_pairs={{0,64},{64,0},{128,192},{192,128},{256,320},{320,256},{384,448},{4... | collective-permute-start | bytes 1032200 | tf_op jit(solution)/shard_map/ppermute | solution.py:221

commit v3 on v2

--- a/solution.py
+++ b/solution.py
@@ -71,7 +71,7 @@
         out_specs=[two] * 4,
         out_shape=[sds((2, m, 4, cols), BF)] * 4,
         scratch_shapes=[pltpu.VMEM((mb, rows, cols), F32)],
-        compiler_params=params(),
+        compiler_params=params(48),
         name="split_rows",
     )(grads)
 
@@ -109,8 +109,7 @@
     return [(i, j) for i in range(n) for j in range(i, n)]
 
 
-def gram_kernel(a_ref, rows_ref, send, keep, slabs):
-    c = lax.rem(lax.axis_index("dp"), 2)
+def gram_kernel(a_ref, rows_ref, gram):
     count, _, cols = a_ref.shape
     for g in range(count // 4):
         four = [a_ref[4 * g + i].astype(F32) for i in range(4)]
@@ -125,12 +124,8 @@
             preferred_element_type=F32,
         )
         for j in range(i, n):
-            block = strip[:, 128 * (j - i) : 128 * (j - i) + 128]
-            slabs[0, b] = block[:64, :]
-            slabs[1, b] = block[64:, :]
+            gram[128 * b : 128 * b + 128, :] = strip[:, 128 * (j - i) : 128 * (j - i) + 128].astype(BF)
             b += 1
-    send[...] = slabs[1 - c].astype(BF)
-    keep[...] = slabs[c]
 
 
 def partial_gram(a):
@@ -139,24 +134,19 @@
     return pl.pallas_call(
         gram_kernel,
         in_specs=whole(1),
-        out_specs=whole(3),
-        out_shape=[
-            sds((4 * count, cols), BF),
-            sds((nb, 64, 128), BF),
-            sds((nb, 64, 128), F32),
-        ],
-        scratch_shapes=[pltpu.VMEM((2, nb, 64, 128), F32)],
+        out_specs=whole(2),
+        out_shape=[sds((4 * count, cols), BF), sds((nb * 128, 128), BF)],
         compiler_params=params(),
         name="partial_gram",
     )(a)
 
 
-def polish_kernel(scale, own, other, rows_ref, out, slabs, level, low, poly, high):
-    c = lax.rem(lax.axis_index("dp"), 2)
+def polish_kernel(scale, gram, rows_ref, out, level, low, poly, high):
     count, cols = rows_ref.shape
     n = cols // 128
-    slabs[c] = own[...].astype(F32)
-    slabs[1 - c] = other[...].astype(F32)
+
+    def block_of(b):
+        return gram[128 * b : 128 * b + 128, :].astype(F32)
 
     eye = (
         lax.broadcasted_iota(jnp.int32, (128, 128), 0) == lax.broadcasted_iota(jnp.int32, (128, 128), 1)
@@ -164,12 +154,12 @@
     diag = jnp.zeros((128, 128), F32)
     for b, (i, j) in enumerate(blocks_of(cols)):
         if i == j:
-            diag += slabs[:, b].reshape(128, 128)
+            diag += block_of(b)
     trace = jnp.sum(jnp.where(eye, diag, 0.0))
     inv_norm = 1.0 / (jnp.sqrt(jnp.full((1, 1), trace)) + 1e-7)
     square = inv_norm * inv_norm
     for b, (i, j) in enumerate(blocks_of(cols)):
-        block = slabs[:, b].reshape(128, 128) * square
+        block = block_of(b) * square
         level[128 * i : 128 * i + 128, 128 * j : 128 * j + 128] = block
         low[128 * i : 128 * i + 128, 128 * j : 128 * j + 128] = block.astype(BF)
         if i != j:
@@ -197,16 +187,14 @@
         out[i] = result[4 * i : 4 * i + 4, :].astype(BF)
 
 
-def polish(scale, own, other, rows):
+def polish(scale, gram, rows):
     count, cols = rows.shape
-    nb = own.shape[0]
     return pl.pallas_call(
         functools.partial(polish_kernel, scale),
-        in_specs=whole(3),
+        in_specs=whole(2),
         out_specs=whole(1)[0],
         out_shape=sds((count // 4, 4, cols), BF),
         scratch_shapes=[
-            pltpu.VMEM((2, nb, 64, 128), F32),
             pltpu.VMEM((cols, cols), F32),
             pltpu.VMEM((cols, cols), BF),
             pltpu.VMEM((cols, cols), BF),
@@ -214,7 +202,7 @@
         ],
         compiler_params=params(32),
         name="polish",
-    )(own, other, rows)
+    )(gram, rows)
 
 
 def core_swap(v):
@@ -244,14 +232,10 @@
 
     mine = lax.all_to_all(nesterov, "fsdp", split_axis=0, concat_axis=0, tiled=True)
 
-    rows, gram_send, gram_keep = partial_gram(mine)
-    gram = gram_keep + core_swap(gram_send).astype(F32)
-    gram = gram + y_swap(gram.astype(BF), 0).astype(F32)
-    gram = gram + y_swap(gram.astype(BF), 1).astype(F32)
-    own = gram.astype(BF)
-    other = core_swap(own)
-
-    update = polish(math.sqrt(max(n_rows, cols)), own, other, rows)
+    rows, gram = partial_gram(mine)
+    gram = lax.psum(gram, "dp")
+
+    update = polish(math.sqrt(max(n_rows, cols)), gram, rows)
     update = lax.all_to_all(update, "fsdp", split_axis=0, concat_axis=0, tiled=True)
     return (update, new_momentum)
 

time: 145 us -> 211 us (1.46)
  waiting for transfers between devices: 31.7 us -> 85.5 us
  between operations: 0.79 us -> 14.1 us
  starting transfers between devices: 23.9 us -> 12.8 us
  blocking collectives: 76.1 us -> 82.6 us
  Pallas kernels: 8.37 us -> 12.5 us
    psum x0 -> x1, waiting for transfers between devices: none -> 69.1 us  [shards(): gram = lax.psum(gram, 'dp')]
    ppermute x4 -> x2, waiting for transfers between devices: 28.5 us -> 16.3 us  [y_swap(): return lax.ppermute(v, 'dp', perm)]
    ppermute x4 -> x2, starting transfers between devices: 15.7 us -> 8.41 us  [y_swap(): return lax.ppermute(v, 'dp', perm)]
    all_to_all x1, blocking collectives: 33 us -> 39.5 us  [shards(): lax.all_to_all(update, 'fsdp', split_axis=0, concat_axis=0, tiled=True)]
    ppermute x4 -> x2, starting transfers between devices: 8.17 us -> 4.33 us  [core_swap(): return lax.ppermute(v, 'dp', [(i, i ^ 1) for i in range(2 * NY)])]
    pallas_call x1, Pallas kernels: 1.4 us -> 4.94 us  [split_rows(): pl.pallas_call(split_kernel, grid=(m // mb,), in_specs=[pl.BlockSpec((1,...]
    ppermute x4 -> x2, waiting for transfers between devices: 3.24 us -> 0.01 us  [core_swap(): return lax.ppermute(v, 'dp', [(i, i ^ 1) for i in range(2 * NY)])]
  transfers between devices with their start and end apart: 8 -> 5, of which waited for: 6 -> 3; matrix products, arithmetic and copies ran while one was open for 0% -> 0% of each run, Pallas kernels for 0% -> 0%
where the time goes in v3:
time: 211 us; the launch traced here: 210 us
  waiting for transfers between devices  85.5 us (41%)
  blocking collectives  82.6 us (39%)
  between operations  14.1 us (7%)
  starting transfers between devices  12.8 us (6%)
  Pallas kernels  12.5 us (6%)
    psum x1, waiting for transfers between devices, shards(): gram = lax.psum(gram, 'dp')  69.1 us
    all_to_all x1, blocking collectives, shards(): lax.all_to_all(nesterov, 'fsdp', split_axis=0, concat_axis=0, tiled=True)  43.1 us
    all_to_all x1, blocking collectives, shards(): lax.all_to_all(update, 'fsdp', split_axis=0, concat_axis=0, tiled=True)  39.5 us
    ppermute x2, waiting for transfers between devices, y_swap(): return lax.ppermute(v, 'dp', perm)  16.3 us
    ppermute x2, starting transfers between devices, y_swap(): return lax.ppermute(v, 'dp', perm)  8.41 us
    pallas_call x1, Pallas kernels, split_rows(): pl.pallas_call(split_kernel, grid=(m // mb,), in_specs=[pl.BlockSpec((1,...  4.94 us
    pallas_call x1, Pallas kernels, polish(): pl.pallas_call(functools.partial(polish_kernel, scale), in_specs=whole(2)...  4.4 us
    ppermute x2, starting transfers between devices, core_swap(): return lax.ppermute(v, 'dp', [(i, i ^ 1) for i in range(2 * NY)])  4.33 us
  transfers between devices with their start and end apart: 5, of which 3 were waited for; matrix products, arithmetic and copies ran while one was open for 0% of the time, Pallas kernels for 0%

profile of v3, /device:TPU:6, one launch (start us, length us, event | category | flops | bytes accessed | tf_op | source)
XLA Modules:
  0.0 210.1 jit_solution(13261482712745213850)
XLA Ops:
  7.2 0.0 all-reduce.2.cloned.1.call-start
  7.2 4.9 %split_rows.1 = (bf16[2,64,4,768]{3,2,1,0:T(4,128)(2,1)S(1)}, bf16[2,64,4,768]{3,2,1,0:T(4,128)(2,1)S(1)}, bf16[2,64,4,768]{3,2,1,0:T(4,128)(2,1)S(1)}, bf16[2,64,4,768]{3,2,1,0:T(4,128)(2,1)S(1)}) custom-call(bf16[1,64,32,768]{3,2,1,0:T(8,128)(2,1)} %g_ref.1), custom_call_target="tpu_custom_call" | custom-call | tf_op jit(solution)/shard_map/split_rows/pallas_call | solution.py:67
  12.2 1.9 collective-permute-start.1
  14.1 2.4 %collective-permute-start = (bf16[2,64,4,768]{3,2,1,0:T(4,128)(2,1)S(1)}, bf16[2,64,4,768]{3,2,1,0:T(4,128)(2,1)S(1)}, u32[]{:S(2)}, u32[]{:S(2)}) collective-permute-start(bf16[2,64,4,768]{3,2,1,0:T(4,128)(2,1)S(1)} %get-tuple-element.11), channel_id=1, source_target_pairs={{0,64},{64,0},{128,192},{192,128},{256,320},{320,256},{384,448},{4... | collective-permute-start | bytes 2359304 | tf_op jit(solution)/shard_map/ppermute | solution.py:209
  16.5 0.0 collective-permute-done.1
  16.5 0.0 copy-start
  16.5 0.0 copy-start.2
  16.5 0.4 add_convert_fusion
  16.9 3.5 %collective-permute-start.2 = (bf16[2,64,4,768]{3,2,1,0:T(4,128)(2,1)S(1)}, bf16[2,64,4,768]{3,2,1,0:T(4,128)(2,1)S(1)}, u32[]{:S(2)}, u32[]{:S(2)}) collective-permute-start(bf16[2,64,4,768]{3,2,1,0:T(4,128)(2,1)S(1)} %add_convert_fusion), channel_id=1, source_target_pairs={{0,128},{64,448},{128,0},{192,320},{256,384},{320,192},{384,256},{... | collective-permute-start | bytes 2359304 | tf_op jit(solution)/shard_map/ppermute | solution.py:218
  20.4 0.0 collective-permute-done.swapped
  20.4 10.4 %collective-permute-done.2.first = bf16[2,64,4,768]{3,2,1,0:T(4,128)(2,1)S(1)} collective-permute-done((bf16[2,64,4,768]{3,2,1,0:T(4,128)(2,1)S(1)}, bf16[2,64,4,768]{3,2,1,0:T(4,128)(2,1)S(1)}, u32[]{:S(2)}, u32[]{:S(2)}) %collective-permute-start.2) | collective-permute-done | bytes 786464 | tf_op jit(solution)/shard_map/ppermute | solution.py:218
  30.8 0.3 fusion
  31.1 4.9 %collective-permute-start.3 = (bf16[64,4,768]{2,1,0:T(4,128)(2,1)S(1)}, bf16[64,4,768]{2,1,0:T(4,128)(2,1)S(1)}, u32[]{:S(2)}, u32[]{:S(2)}) collective-permute-start(bf16[64,4,768]{2,1,0:T(4,128)(2,1)S(1)} %fusion), channel_id=1, source_target_pairs={{0,384},{64,192},{128,256},{192,64},{256,128},{320,448},{384,0},{4... | collective-permute-start | bytes 1179656 | tf_op jit(solution)/shard_map/ppermute | solution.py:218
  36.1 6.0 %collective-permute-done.3.second = bf16[64,4,768]{2,1,0:T(4,128)(2,1)S(1)} collective-permute-done((bf16[64,4,768]{2,1,0:T(4,128)(2,1)S(1)}, bf16[64,4,768]{2,1,0:T(4,128)(2,1)S(1)}, u32[]{:S(2)}, u32[]{:S(2)}) %collective-permute-start.3) | collective-permute-done | bytes 393248 | tf_op jit(solution)/shard_map/ppermute | solution.py:218
  42.0 0.0 copy-done
  42.0 0.0 copy-done.2
  42.0 1.9 momentum_step.1
  43.9 43.1 %all_to_all.10.a_ref = bf16[64,4,768]{2,1,0:T(4,128)(2,1)S(1)} all-to-all(bf16[64,4,768]{2,1,0:T(4,128)(2,1)S(1)} %get-tuple-element.14), channel_id=1, replica_groups=mesh['dp'=8,'fsdp'=64] {'fsdp'}, dimensions={0} | all-to-all | bytes 786432 | tf_op jit(solution)/shard_map/all_to_all | solution.py:233
  87.0 1.3 partial_gram.1
  88.3 0.0 all-reduce.2.cloned.1.call-update
  88.4 69.1 %all-reduce.2.cloned.1.call-done.gram = bf16[2688,128]{1,0:T(8,128)(2,1)} async-done(((bf16[2688,128]{1,0:T(8,128)(2,1)}), bf16[2688,128]{1,0:T(8,128)(2,1)}) %all-reduce.2.cloned.1.call-update) | async-done | bytes 688144 | tf_op jit(solution)/shard_map/psum | solution.py:236
  157.5 0.0 copy-start.1
  157.5 1.1 copy-done.1
  158.6 4.4 %polish.1 = bf16[64,4,768]{2,1,0:T(4,128)(2,1)S(1)} custom-call(bf16[2688,128]{1,0:T(8,128)(2,1)S(1)} %copy-done.1, bf16[256,768]{1,0:T(8,128)(2,1)S(1)} %get-tuple-element.16.rows_ref), custom_call_target="tpu_custom_call" | custom-call | tf_op jit(solution)/shard_map/polish/pallas_call | solution.py:192
  163.0 39.5 %all_to_all.11 = bf16[64,4,768]{2,1,0:T(4,128)(2,1)S(1)} all-to-all(bf16[64,4,768]{2,1,0:T(4,128)(2,1)S(1)} %polish.1), channel_id=1, replica_groups=mesh['dp'=8,'fsdp'=64] {'fsdp'}, dimensions={0} | all-to-all | bytes 786432 | tf_op jit(solution)/shard_map/all_to_all | solution.py:239
  202.5 0.7 copy.7
Async XLA Ops:
  7.2 150.3 %all-reduce.2.cloned.1.call-start = ((), (), s32[]{:S(2)}) async-start(), calls=%async_computation.2 | async-start | bytes 1376256 | tf_op jit(solution)/shard_map/psum | solution.py:236
  12.2 4.3 %collective-permute-start.1 = (bf16[2,64,4,768]{3,2,1,0:T(4,128)(2,1)S(1)}, bf16[2,64,4,768]{3,2,1,0:T(4,128)(2,1)S(1)}, u32[]{:S(2)}, u32[]{:S(2)}) collective-permute-start(bf16[2,64,4,768]{3,2,1,0:T(4,128)(2,1)S(1)} %get-tuple-element.13), channel_id=1, source_target_pairs={{0,64},{64,0},{128,192},{192,128},{256,320},{320,256},{384,448},{4... | collective-permute-start | bytes 2359304 | tf_op jit(solution)/shard_map/ppermute | solution.py:209
  14.1 6.4 %collective-permute-start = (bf16[2,64,4,768]{3,2,1,0:T(4,128)(2,1)S(1)}, bf16[2,64,4,768]{3,2,1,0:T(4,128)(2,1)S(1)}, u32[]{:S(2)}, u32[]{:S(2)}) collective-permute-start(bf16[2,64,4,768]{3,2,1,0:T(4,128)(2,1)S(1)} %get-tuple-element.11), channel_id=1, source_target_pairs={{0,64},{64,0},{128,192},{192,128},{256,320},{320,256},{384,448},{4... | collective-permute-start | bytes 2359304 | tf_op jit(solution)/shard_map/ppermute | solution.py:209
  16.5 25.5 %copy-start = (f32[64,4,768]{2,1,0:T(4,128)S(1)}, f32[64,4,768]{2,1,0:T(4,128)}, u32[]{:S(2)}) copy-start(f32[64,4,768]{2,1,0:T(4,128)} %mom.1) | copy-start | bytes 2359300
  16.5 25.5 %copy-start.2 = (s32[64]{0:T(128)S(1)}, s32[64]{0:T(128)}, u32[]{:S(2)}) copy-start(s32[64]{0:T(128)} %slots.1) | copy-start | bytes 772
  16.9 13.9 %collective-permute-start.2 = (bf16[2,64,4,768]{3,2,1,0:T(4,128)(2,1)S(1)}, bf16[2,64,4,768]{3,2,1,0:T(4,128)(2,1)S(1)}, u32[]{:S(2)}, u32[]{:S(2)}) collective-permute-start(bf16[2,64,4,768]{3,2,1,0:T(4,128)(2,1)S(1)} %add_convert_fusion), channel_id=1, source_target_pairs={{0,128},{64,448},{128,0},{192,320},{256,384},{320,192},{384,256},{... | collective-permute-start | bytes 2359304 | tf_op jit(solution)/shard_map/ppermute | solution.py:218
  31.1 10.9 %collective-permute-start.3 = (bf16[64,4,768]{2,1,0:T(4,128)(2,1)S(1)}, bf16[64,4,768]{2,1,0:T(4,128)(2,1)S(1)}, u32[]{:S(2)}, u32[]{:S(2)}) collective-permute-start(bf16[64,4,768]{2,1,0:T(4,128)(2,1)S(1)} %fusion), channel_id=1, source_target_pairs={{0,384},{64,192},{128,256},{192,64},{256,128},{320,448},{384,0},{4... | collective-permute-start | bytes 1179656 | tf_op jit(solution)/shard_map/ppermute | solution.py:218
  157.5 1.1 copy-start.1
Sparse Core Ops, SparseCore 0:
  88.5 68.9 all-reduce.1

commit v4 on v2

--- a/solution.py
+++ b/solution.py
@@ -3,6 +3,7 @@
 
 import jax
 import jax.numpy as jnp
+import numpy as np
 from jax import lax
 from jax.experimental import pallas as pl
 from jax.experimental.pallas import tpu as pltpu
@@ -39,39 +40,56 @@
     return y, c, near, far, lax.rem(y + 2, NY)
 
 
-def split_kernel(g_ref, send_a, send_b, keep_a, keep_b, scr):
+def split_kernel(g_hbm, send_across, send_rest, keep_across, keep_rest, raw, wide, sems):
     y, c, near, far, across = place_of()
-    scr[...] = g_ref[0].astype(F32)
-
-    def emit(low):
+    parts = sems.shape[0]
+    mb = raw.shape[0] // parts
+
+    def fetch(i):
+        return pltpu.make_async_copy(
+            g_hbm.at[0, pl.ds(i * mb, mb)], raw.at[pl.ds(i * mb, mb)], sems.at[i]
+        )
+
+    for i in range(parts):
+        fetch(i).start()
+
+    def emit(i, low):
+        here = pl.ds(i * mb, mb)
+
         def rows(yy, core):
-            both = scr[:, pl.ds(pl.multiple_of(8 * yy, 8), 8), :]
+            both = wide[:, pl.ds(pl.multiple_of(8 * yy, 8), 8), :]
             return both[:, 4 * core : 4 * core + 4, :].astype(BF)
 
-        send_a[0] = rows(far, 1 - low)
-        send_a[1] = rows(across, 1 - low)
-        send_b[0] = rows(y, 1 - low)
-        send_b[1] = rows(near, 1 - low)
-        keep_a[0] = rows(near, low)
-        keep_a[1] = rows(across, low)
-        keep_b[0] = rows(y, low)
-        keep_b[1] = rows(far, low)
-
-    pl.when(c == 0)(lambda: emit(0))
-    pl.when(c == 1)(lambda: emit(1))
-
-
-def split_rows(grads, mb):
+        send_across[here] = rows(across, 1 - low)
+        send_rest[0, here] = rows(y, 1 - low)
+        send_rest[1, here] = rows(near, 1 - low)
+        send_rest[2, here] = rows(far, 1 - low)
+        keep_across[here] = rows(across, low)
+        keep_rest[0, here] = rows(y, low)
+        keep_rest[1, here] = rows(far, low)
+        keep_rest[2, here] = rows(near, low)
+
+    for i in range(parts):
+        fetch(i).wait()
+        wide[...] = raw[i * mb : i * mb + mb].astype(F32)
+        pl.when(c == 0)(functools.partial(emit, i, 0))
+        pl.when(c == 1)(functools.partial(emit, i, 1))
+
+
+def split_rows(grads, parts):
     _, m, rows, cols = grads.shape
-    two = pl.BlockSpec((2, mb, 4, cols), lambda i: (0, i, 0, 0))
+    one, three = sds((m, 4, cols), BF), sds((3, m, 4, cols), BF)
     return pl.pallas_call(
         split_kernel,
-        grid=(m // mb,),
-        in_specs=[pl.BlockSpec((1, mb, rows, cols), lambda i: (0, i, 0, 0))],
-        out_specs=[two] * 4,
-        out_shape=[sds((2, m, 4, cols), BF)] * 4,
-        scratch_shapes=[pltpu.VMEM((mb, rows, cols), F32)],
-        compiler_params=params(),
+        in_specs=[pl.BlockSpec(memory_space=pl.ANY)],
+        out_specs=whole(4),
+        out_shape=[one, three, one, three],
+        scratch_shapes=[
+            pltpu.VMEM((m, rows, cols), BF),
+            pltpu.VMEM((m // parts, rows, cols), F32),
+            pltpu.SemaphoreType.DMA((parts,)),
+        ],
+        compiler_params=params(48),
         name="split_rows",
     )(grads)
 
@@ -82,7 +100,7 @@
     def step(j, carry):
         mat = slots[j]
         gradient = (keep[0, j].astype(F32) + swapped[0, j].astype(F32)) + (
-            first[0, j].astype(F32) + second[j].astype(F32)
+            first[j].astype(F32) + second[j].astype(F32)
         )
         new = DECAY * mom[mat] + gradient
         new_mom[mat] = new
@@ -230,19 +248,26 @@
     return lax.ppermute(v, "dp", perm)
 
 
+def exchange(v):
+    order = np.random.RandomState(7).permutation(v.shape[0])
+    groups = [[int(i) for i in order]]
+    return lax.all_to_all(v, "fsdp", split_axis=0, concat_axis=0, axis_index_groups=groups, tiled=True)
+
+
 def shards(n_rows, grads, momentum, slot_matrix):
     m = grads.shape[1]
     cols = grads.shape[3]
 
-    send_a, send_b, keep_a, keep_b = split_rows(grads, min(8, m))
-    swapped_a = core_swap(send_a)
-    swapped_b = core_swap(send_b)
-    first = y_swap((keep_a.astype(F32) + swapped_a.astype(F32)).astype(BF), 0)
-    far = (keep_b[1].astype(F32) + swapped_b[1].astype(F32)) + first[1].astype(F32)
+    send_across, send_rest, keep_across, keep_rest = split_rows(grads, 8)
+    across = keep_across.astype(F32) + core_swap(send_across).astype(F32)
+    first_far = y_swap(across.astype(BF), 0)
+    swapped = core_swap(send_rest)
+    first_own = y_swap((keep_rest[2].astype(F32) + swapped[2].astype(F32)).astype(BF), 0)
+    far = (keep_rest[1].astype(F32) + swapped[1].astype(F32)) + first_far.astype(F32)
     second = y_swap(far.astype(BF), 1)
-    nesterov, new_momentum = momentum_step(slot_matrix, keep_b, swapped_b, first, second, momentum)
-
-    mine = lax.all_to_all(nesterov, "fsdp", split_axis=0, concat_axis=0, tiled=True)
+    nesterov, new_momentum = momentum_step(slot_matrix, keep_rest, swapped, first_own, second, momentum)
+
+    mine = exchange(nesterov)
 
     rows, gram_send, gram_keep = partial_gram(mine)
     gram = gram_keep + core_swap(gram_send).astype(F32)
@@ -252,8 +277,7 @@
     other = core_swap(own)
 
     update = polish(math.sqrt(max(n_rows, cols)), own, other, rows)
-    update = lax.all_to_all(update, "fsdp", split_axis=0, concat_axis=0, tiled=True)
-    return (update, new_momentum)
+    return (exchange(update), new_momentum)
 
 
 def solution(mesh):

time: 145 us -> 142 us (0.979); the launches traced: 145 us -> 140 us
  waiting for transfers between devices: 31.7 us -> 26.1 us
  starting transfers between devices: 23.9 us -> 26.4 us
  local copies, waits for them, and re-layouts: 2.64 us -> 0.76 us
    ppermute x4 -> x5, waiting for transfers between devices: 28.5 us -> 21.5 us  [y_swap(): return lax.ppermute(v, 'dp', perm)]
    ppermute x4 -> x5, starting transfers between devices: 15.7 us -> 18.2 us  [y_swap(): return lax.ppermute(v, 'dp', perm)]
    unnamed x7 -> x5, local copies, waits for them, and re-layouts: 2.64 us -> 0.76 us
  transfers between devices with their start and end apart: 8 -> 9, of which waited for: 6 -> 7; matrix products, arithmetic and copies ran while one was open for 0% -> 1% of each run, Pallas kernels for 0% -> 0%
where the time goes in v4:
time: 142 us; the launch traced here: 140 us
  blocking collectives  75.9 us (53%)
  starting transfers between devices  26.4 us (19%)
  waiting for transfers between devices  26.1 us (18%)
  Pallas kernels  9 us (6%)
    all_to_all x2, blocking collectives, exchange(): lax.all_to_all(v, 'fsdp', split_axis=0, concat_axis=0, axis_index_groups=...  75.9 us
    ppermute x5, waiting for transfers between devices, y_swap(): return lax.ppermute(v, 'dp', perm)  21.5 us
    ppermute x5, starting transfers between devices, y_swap(): return lax.ppermute(v, 'dp', perm)  18.2 us
    ppermute x4, starting transfers between devices, core_swap(): return lax.ppermute(v, 'dp', [(i, i ^ 1) for i in range(2 * NY)])  8.17 us
    ppermute x4, waiting for transfers between devices, core_swap(): return lax.ppermute(v, 'dp', [(i, i ^ 1) for i in range(2 * NY)])  4.57 us
    pallas_call x1, Pallas kernels, polish(): pl.pallas_call(functools.partial(polish_kernel, scale), in_specs=whole(3)...  4.48 us
  transfers between devices with their start and end apart: 9, of which 7 were waited for; matrix products, arithmetic and copies ran while one was open for 1% of the time, Pallas kernels for 0%

profile of v4, /device:TPU:6, one launch (start us, length us, event | category | flops | bytes accessed | tf_op | source)
XLA Modules:
  0.0 140.0 jit_solution(4399630137756160622)
XLA Ops:
  0.6 2.0 %split_rows.1 = (bf16[64,4,768]{2,1,0:T(4,128)(2,1)S(1)}, bf16[3,64,4,768]{3,2,1,0:T(4,128)(2,1)S(1)}, bf16[64,4,768]{2,1,0:T(4,128)(2,1)S(1)}, bf16[3,64,4,768]{3,2,1,0:T(4,128)(2,1)S(1)}) custom-call(bf16[1,64,32,768]{3,2,1,0:T(8,128)(2,1)} %g_hbm.1), custom_call_target="tpu_custom_call" | custom-call | tf_op jit(solution)/shard_map/split_rows/pallas_call | solution.py:82
  2.7 1.9 %collective-permute-start = (bf16[3,64,4,768]{3,2,1,0:T(4,128)(2,1)S(1)}, bf16[3,64,4,768]{3,2,1,0:T(4,128)(2,1)S(1)}, u32[]{:S(2)}, u32[]{:S(2)}) collective-permute-start(bf16[3,64,4,768]{3,2,1,0:T(4,128)(2,1)S(1)} %get-tuple-element.12), channel_id=1, source_target_pairs={{0,64},{64,0},{128,192},{192,128},{256,320},{320,256},{384,448},{4... | collective-permute-start | bytes 3538952 | tf_op jit(solution)/shard_map/ppermute | solution.py:239
  4.6 2.4 %collective-permute-start.2 = (bf16[64,4,768]{2,1,0:T(4,128)(2,1)S(1)}, bf16[64,4,768]{2,1,0:T(4,128)(2,1)S(1)}, u32[]{:S(2)}, u32[]{:S(2)}) collective-permute-start(bf16[64,4,768]{2,1,0:T(4,128)(2,1)S(1)} %get-tuple-element.14), channel_id=1, source_target_pairs={{0,64},{64,0},{128,192},{192,128},{256,320},{320,256},{384,448},{4... | collective-permute-start | bytes 1179656 | tf_op jit(solution)/shard_map/ppermute | solution.py:239
  7.0 1.3 collective-permute-done.2
  8.3 0.2 add_convert_fusion
  8.5 3.5 %collective-permute-start.3 = (bf16[64,4,768]{2,1,0:T(4,128)(2,1)S(1)}, bf16[64,4,768]{2,1,0:T(4,128)(2,1)S(1)}, u32[]{:S(2)}, u32[]{:S(2)}) collective-permute-start(bf16[64,4,768]{2,1,0:T(4,128)(2,1)S(1)} %add_convert_fusion), channel_id=1, source_target_pairs={{0,128},{64,448},{128,0},{192,320},{256,384},{320,192},{384,256},{... | collective-permute-start | bytes 1179656 | tf_op jit(solution)/shard_map/ppermute | solution.py:248
  12.0 0.0 collective-permute-done.swapped
  12.0 0.0 copy-start
  12.1 0.0 copy-start.1
  12.1 0.2 fusion.2
  12.3 2.5 %collective-permute-start.1 = (bf16[64,4,768]{2,1,0:T(4,128)(2,1)S(1)}, bf16[64,4,768]{2,1,0:T(4,128)(2,1)S(1)}, u32[]{:S(2)}, u32[]{:S(2)}) collective-permute-start(bf16[64,4,768]{2,1,0:T(4,128)(2,1)S(1)} %fusion.2), channel_id=1, source_target_pairs={{0,128},{64,448},{128,0},{192,320},{256,384},{320,192},{384,256},{... | collective-permute-start | bytes 1179656 | tf_op jit(solution)/shard_map/ppermute | solution.py:248
  14.8 3.4 %collective-permute-done.3 = bf16[64,4,768]{2,1,0:T(4,128)(2,1)S(1)} collective-permute-done((bf16[64,4,768]{2,1,0:T(4,128)(2,1)S(1)}, bf16[64,4,768]{2,1,0:T(4,128)(2,1)S(1)}, u32[]{:S(2)}, u32[]{:S(2)}) %collective-permute-start.3) | collective-permute-done | bytes 393248 | tf_op jit(solution)/shard_map/ppermute | solution.py:248
  18.2 0.3 fusion
  18.5 4.9 %collective-permute-start.4 = (bf16[64,4,768]{2,1,0:T(4,128)(2,1)S(1)}, bf16[64,4,768]{2,1,0:T(4,128)(2,1)S(1)}, u32[]{:S(2)}, u32[]{:S(2)}) collective-permute-start(bf16[64,4,768]{2,1,0:T(4,128)(2,1)S(1)} %fusion), channel_id=1, source_target_pairs={{0,384},{64,192},{128,256},{192,64},{256,128},{320,448},{384,0},{4... | collective-permute-start | bytes 1179656 | tf_op jit(solution)/shard_map/ppermute | solution.py:248
  23.5 0.0 collective-permute-done.1.first
  23.5 5.9 %collective-permute-done.4.second = bf16[64,4,768]{2,1,0:T(4,128)(2,1)S(1)} collective-permute-done((bf16[64,4,768]{2,1,0:T(4,128)(2,1)S(1)}, bf16[64,4,768]{2,1,0:T(4,128)(2,1)S(1)}, u32[]{:S(2)}, u32[]{:S(2)}) %collective-permute-start.4) | collective-permute-done | bytes 393248 | tf_op jit(solution)/shard_map/ppermute | solution.py:248
  29.4 0.0 copy-done
  29.4 0.0 copy-done.1
  29.4 1.9 %momentum_step.1 = (bf16[64,4,768]{2,1,0:T(4,128)(2,1)S(1)}, f32[64,4,768]{2,1,0:T(4,128)}) custom-call(s32[64]{0:T(128)S(1)} %copy-done.1, bf16[3,64,4,768]{3,2,1,0:T(4,128)(2,1)S(1)} %get-tuple-element.11.keep, bf16[3,64,4,768]{3,2,1,0:T(4,128)(2,1)S(1)} %collective-permute-done.swapped, bf16[64,4,768]{2,1,0:T(4,128)(2,1)S(1)} %collective-permute-done.1.first, ...), custom_call_target="tpu_custom_call" | custom-call | tf_op jit(solution)/shard_map/momentum_step/pallas_call | solution.py:115
  31.3 42.7 %all_to_all.10.a_ref = bf16[64,4,768]{2,1,0:T(4,128)(2,1)S(1)} all-to-all(bf16[64,4,768]{2,1,0:T(4,128)(2,1)S(1)} %get-tuple-element.15), channel_id=1, replica_groups={{18,2,40,48,17,41,29,21,32,45,15,20,31,51,13,22,27,30,10,43,12,37,36,1,..., dimensions={0} | all-to-all | bytes 786432 | tf_op jit(solution)/shard_map/all_to_all | solution.py:254
  74.0 0.6 partial_gram.1
  74.6 1.9 %collective-permute-start.5 = (bf16[21,64,128]{2,1,0:T(8,128)(2,1)S(1)}, bf16[21,64,128]{2,1,0:T(8,128)(2,1)S(1)}, u32[]{:S(2)}, u32[]{:S(2)}) collective-permute-start(bf16[21,64,128]{2,1,0:T(8,128)(2,1)S(1)} %get-tuple-element.17), channel_id=1, source_target_pairs={{0,64},{64,0},{128,192},{192,128},{256,320},{320,256},{384,448},{4... | collective-permute-start | bytes 1032200 | tf_op jit(solution)/shard_map/ppermute | solution.py:239
  76.6 1.6 %collective-permute-done.5 = bf16[21,64,128]{2,1,0:T(8,128)(2,1)S(1)} collective-permute-done((bf16[21,64,128]{2,1,0:T(8,128)(2,1)S(1)}, bf16[21,64,128]{2,1,0:T(8,128)(2,1)S(1)}, u32[]{:S(2)}, u32[]{:S(2)}) %collective-permute-start.5) | collective-permute-done | bytes 344096 | tf_op jit(solution)/shard_map/ppermute | solution.py:239
  78.2 0.1 fusion.1
  78.3 2.5 %collective-permute-start.6 = (bf16[21,64,128]{2,1,0:T(8,128)(2,1)S(1)}, bf16[21,64,128]{2,1,0:T(8,128)(2,1)S(1)}, u32[]{:S(2)}, u32[]{:S(2)}) collective-permute-start(bf16[21,64,128]{2,1,0:T(8,128)(2,1)S(1)} %fusion.1), channel_id=1, source_target_pairs={{0,128},{64,448},{128,0},{192,320},{256,384},{320,192},{384,256},{... | collective-permute-start | bytes 1032200 | tf_op jit(solution)/shard_map/ppermute | solution.py:248
  80.8 6.6 %collective-permute-done.6 = bf16[21,64,128]{2,1,0:T(8,128)(2,1)S(1)} collective-permute-done((bf16[21,64,128]{2,1,0:T(8,128)(2,1)S(1)}, bf16[21,64,128]{2,1,0:T(8,128)(2,1)S(1)}, u32[]{:S(2)}, u32[]{:S(2)}) %collective-permute-start.6) | collective-permute-done | bytes 344096 | tf_op jit(solution)/shard_map/ppermute | solution.py:248
  87.4 0.1 fusion.3
  87.6 4.8 %collective-permute-start.7 = (bf16[21,64,128]{2,1,0:T(8,128)(2,1)S(1)}, bf16[21,64,128]{2,1,0:T(8,128)(2,1)S(1)}, u32[]{:S(2)}, u32[]{:S(2)}) collective-permute-start(bf16[21,64,128]{2,1,0:T(8,128)(2,1)S(1)} %fusion.3), channel_id=1, source_target_pairs={{0,384},{64,192},{128,256},{192,64},{256,128},{320,448},{384,0},{4... | collective-permute-start | bytes 1032200 | tf_op jit(solution)/shard_map/ppermute | solution.py:248
  92.4 5.5 %collective-permute-done.7 = bf16[21,64,128]{2,1,0:T(8,128)(2,1)S(1)} collective-permute-done((bf16[21,64,128]{2,1,0:T(8,128)(2,1)S(1)}, bf16[21,64,128]{2,1,0:T(8,128)(2,1)S(1)}, u32[]{:S(2)}, u32[]{:S(2)}) %collective-permute-start.7) | collective-permute-done | bytes 344096 | tf_op jit(solution)/shard_map/ppermute | solution.py:248
  97.9 0.2 add_convert_fusion.2.own
  98.1 1.9 %collective-permute-start.8 = (bf16[21,64,128]{2,1,0:T(8,128)(2,1)S(1)}, bf16[21,64,128]{2,1,0:T(8,128)(2,1)S(1)}, u32[]{:S(2)}, u32[]{:S(2)}) collective-permute-start(bf16[21,64,128]{2,1,0:T(8,128)(2,1)S(1)} %add_convert_fusion.2.own), channel_id=1, source_target_pairs={{0,64},{64,0},{128,192},{192,128},{256,320},{320,256},{384,448},{4... | collective-permute-start | bytes 1032200 | tf_op jit(solution)/shard_map/ppermute | solution.py:239
  100.0 1.6 %collective-permute-done.8.other = bf16[21,64,128]{2,1,0:T(8,128)(2,1)S(1)} collective-permute-done((bf16[21,64,128]{2,1,0:T(8,128)(2,1)S(1)}, bf16[21,64,128]{2,1,0:T(8,128)(2,1)S(1)}, u32[]{:S(2)}, u32[]{:S(2)}) %collective-permute-start.8) | collective-permute-done | bytes 344096 | tf_op jit(solution)/shard_map/ppermute | solution.py:239
  101.7 4.5 %polish.1 = bf16[64,4,768]{2,1,0:T(4,128)(2,1)S(1)} custom-call(bf16[21,64,128]{2,1,0:T(8,128)(2,1)S(1)} %add_convert_fusion.2.own, bf16[21,64,128]{2,1,0:T(8,128)(2,1)S(1)} %collective-permute-done.8.other, bf16[256,768]{1,0:T(8,128)(2,1)S(1)} %get-tuple-element.18.rows_ref), custom_call_target="tpu_custom_call" | custom-call | tf_op jit(solution)/shard_map/polish/pallas_call | solution.py:221
  106.2 33.1 %all_to_all.11 = bf16[64,4,768]{2,1,0:T(4,128)(2,1)S(1)} all-to-all(bf16[64,4,768]{2,1,0:T(4,128)(2,1)S(1)} %polish.1), channel_id=1, replica_groups={{18,2,40,48,17,41,29,21,32,45,15,20,31,51,13,22,27,30,10,43,12,37,36,1,..., dimensions={0} | all-to-all | bytes 786432 | tf_op jit(solution)/shard_map/all_to_all | solution.py:254
  139.3 0.7 copy.6
Async XLA Ops:
  2.7 9.4 %collective-permute-start = (bf16[3,64,4,768]{3,2,1,0:T(4,128)(2,1)S(1)}, bf16[3,64,4,768]{3,2,1,0:T(4,128)(2,1)S(1)}, u32[]{:S(2)}, u32[]{:S(2)}) collective-permute-start(bf16[3,64,4,768]{3,2,1,0:T(4,128)(2,1)S(1)} %get-tuple-element.12), channel_id=1, source_target_pairs={{0,64},{64,0},{128,192},{192,128},{256,320},{320,256},{384,448},{4... | collective-permute-start | bytes 3538952 | tf_op jit(solution)/shard_map/ppermute | solution.py:239
  4.6 3.7 %collective-permute-start.2 = (bf16[64,4,768]{2,1,0:T(4,128)(2,1)S(1)}, bf16[64,4,768]{2,1,0:T(4,128)(2,1)S(1)}, u32[]{:S(2)}, u32[]{:S(2)}) collective-permute-start(bf16[64,4,768]{2,1,0:T(4,128)(2,1)S(1)} %get-tuple-element.14), channel_id=1, source_target_pairs={{0,64},{64,0},{128,192},{192,128},{256,320},{320,256},{384,448},{4... | collective-permute-start | bytes 1179656 | tf_op jit(solution)/shard_map/ppermute | solution.py:239
  8.5 9.7 %collective-permute-start.3 = (bf16[64,4,768]{2,1,0:T(4,128)(2,1)S(1)}, bf16[64,4,768]{2,1,0:T(4,128)(2,1)S(1)}, u32[]{:S(2)}, u32[]{:S(2)}) collective-permute-start(bf16[64,4,768]{2,1,0:T(4,128)(2,1)S(1)} %add_convert_fusion), channel_id=1, source_target_pairs={{0,128},{64,448},{128,0},{192,320},{256,384},{320,192},{384,256},{... | collective-permute-start | bytes 1179656 | tf_op jit(solution)/shard_map/ppermute | solution.py:248
  12.0 17.4 %copy-start = (f32[64,4,768]{2,1,0:T(4,128)S(1)}, f32[64,4,768]{2,1,0:T(4,128)}, u32[]{:S(2)}) copy-start(f32[64,4,768]{2,1,0:T(4,128)} %mom.1) | copy-start | bytes 2359300
  12.1 17.4 %copy-start.1 = (s32[64]{0:T(128)S(1)}, s32[64]{0:T(128)}, u32[]{:S(2)}) copy-start(s32[64]{0:T(128)} %slots.1) | copy-start | bytes 772
  12.3 11.2 %collective-permute-start.1 = (bf16[64,4,768]{2,1,0:T(4,128)(2,1)S(1)}, bf16[64,4,768]{2,1,0:T(4,128)(2,1)S(1)}, u32[]{:S(2)}, u32[]{:S(2)}) collective-permute-start(bf16[64,4,768]{2,1,0:T(4,128)(2,1)S(1)} %fusion.2), channel_id=1, source_target_pairs={{0,128},{64,448},{128,0},{192,320},{256,384},{320,192},{384,256},{... | collective-permute-start | bytes 1179656 | tf_op jit(solution)/shard_map/ppermute | solution.py:248
  18.5 10.9 %collective-permute-start.4 = (bf16[64,4,768]{2,1,0:T(4,128)(2,1)S(1)}, bf16[64,4,768]{2,1,0:T(4,128)(2,1)S(1)}, u32[]{:S(2)}, u32[]{:S(2)}) collective-permute-start(bf16[64,4,768]{2,1,0:T(4,128)(2,1)S(1)} %fusion), channel_id=1, source_target_pairs={{0,384},{64,192},{128,256},{192,64},{256,128},{320,448},{384,0},{4... | collective-permute-start | bytes 1179656 | tf_op jit(solution)/shard_map/ppermute | solution.py:248
  74.6 3.5 %collective-permute-start.5 = (bf16[21,64,128]{2,1,0:T(8,128)(2,1)S(1)}, bf16[21,64,128]{2,1,0:T(8,128)(2,1)S(1)}, u32[]{:S(2)}, u32[]{:S(2)}) collective-permute-start(bf16[21,64,128]{2,1,0:T(8,128)(2,1)S(1)} %get-tuple-element.17), channel_id=1, source_target_pairs={{0,64},{64,0},{128,192},{192,128},{256,320},{320,256},{384,448},{4... | collective-permute-start | bytes 1032200 | tf_op jit(solution)/shard_map/ppermute | solution.py:239
  78.3 9.1 %collective-permute-start.6 = (bf16[21,64,128]{2,1,0:T(8,128)(2,1)S(1)}, bf16[21,64,128]{2,1,0:T(8,128)(2,1)S(1)}, u32[]{:S(2)}, u32[]{:S(2)}) collective-permute-start(bf16[21,64,128]{2,1,0:T(8,128)(2,1)S(1)} %fusion.1), channel_id=1, source_target_pairs={{0,128},{64,448},{128,0},{192,320},{256,384},{320,192},{384,256},{... | collective-permute-start | bytes 1032200 | tf_op jit(solution)/shard_map/ppermute | solution.py:248
  87.6 10.4 %collective-permute-start.7 = (bf16[21,64,128]{2,1,0:T(8,128)(2,1)S(1)}, bf16[21,64,128]{2,1,0:T(8,128)(2,1)S(1)}, u32[]{:S(2)}, u32[]{:S(2)}) collective-permute-start(bf16[21,64,128]{2,1,0:T(8,128)(2,1)S(1)} %fusion.3), channel_id=1, source_target_pairs={{0,384},{64,192},{128,256},{192,64},{256,128},{320,448},{384,0},{4... | collective-permute-start | bytes 1032200 | tf_op jit(solution)/shard_map/ppermute | solution.py:248
  98.1 3.5 %collective-permute-start.8 = (bf16[21,64,128]{2,1,0:T(8,128)(2,1)S(1)}, bf16[21,64,128]{2,1,0:T(8,128)(2,1)S(1)}, u32[]{:S(2)}, u32[]{:S(2)}) collective-permute-start(bf16[21,64,128]{2,1,0:T(8,128)(2,1)S(1)} %add_convert_fusion.2.own), channel_id=1, source_target_pairs={{0,64},{64,0},{128,192},{192,128},{256,320},{320,256},{384,448},{4... | collective-permute-start | bytes 1032200 | tf_op jit(solution)/shard_map/ppermute | solution.py:239

commit v5 on v4

--- a/solution.py
+++ b/solution.py
@@ -3,7 +3,6 @@
 
 import jax
 import jax.numpy as jnp
-import numpy as np
 from jax import lax
 from jax.experimental import pallas as pl
 from jax.experimental.pallas import tpu as pltpu
@@ -95,7 +94,8 @@
 
 
 def momentum_kernel(slots, keep, swapped, first, second, mom, nesterov, new_mom):
-    m = mom.shape[0]
+    m, _, cols = mom.shape
+    half = cols // 2
 
     def step(j, carry):
         mat = slots[j]
@@ -104,7 +104,8 @@
         )
         new = DECAY * mom[mat] + gradient
         new_mom[mat] = new
-        nesterov[mat] = (gradient + DECAY * new).astype(BF)
+        value = gradient + DECAY * new
+        nesterov[mat] = jnp.concatenate([value[:, :half], value[:, half:]], axis=0).astype(BF)
         return carry
 
     lax.fori_loop(0, m, step, 0, unroll=min(8, m))
@@ -116,7 +117,7 @@
         momentum_kernel,
         in_specs=[pl.BlockSpec(memory_space=SMEM)] + whole(5),
         out_specs=whole(2),
-        out_shape=[sds((m, 4, cols), BF), sds((m, 4, cols), F32)],
+        out_shape=[sds((m, 8, cols // 2), BF), sds((m, 4, cols), F32)],
         compiler_params=params(),
         name="momentum_step",
     )(slots, keep, swapped, first, second, mom)
@@ -127,13 +128,14 @@
     return [(i, j) for i in range(n) for j in range(i, n)]
 
 
-def gram_kernel(a_ref, rows_ref, send, keep, slabs):
-    c = lax.rem(lax.axis_index("dp"), 2)
-    count, _, cols = a_ref.shape
+def gram_kernel(a_ref, rows_ref, gram):
+    count, _, half = a_ref.shape
     for g in range(count // 4):
         four = [a_ref[4 * g + i].astype(F32) for i in range(4)]
-        rows_ref[16 * g : 16 * g + 16, :] = jnp.concatenate(four, axis=0).astype(BF)
-    n = cols // 128
+        here = slice(16 * g, 16 * g + 16)
+        rows_ref[here, :half] = jnp.concatenate([v[:4] for v in four], axis=0).astype(BF)
+        rows_ref[here, half:] = jnp.concatenate([v[4:] for v in four], axis=0).astype(BF)
+    n = 2 * half // 128
     b = 0
     for i in range(n):
         strip = lax.dot_general(
@@ -143,38 +145,31 @@
             preferred_element_type=F32,
         )
         for j in range(i, n):
-            block = strip[:, 128 * (j - i) : 128 * (j - i) + 128]
-            slabs[0, b] = block[:64, :]
-            slabs[1, b] = block[64:, :]
+            block = strip[:, 128 * (j - i) : 128 * (j - i) + 128].astype(BF)
+            for k in range(8):
+                gram[k, 16 * b : 16 * b + 16, :] = block[16 * k : 16 * k + 16, :]
             b += 1
-    send[...] = slabs[1 - c].astype(BF)
-    keep[...] = slabs[c]
 
 
 def partial_gram(a):
-    count, _, cols = a.shape
-    nb = len(blocks_of(cols))
+    count, _, half = a.shape
+    nb = len(blocks_of(2 * half))
     return pl.pallas_call(
         gram_kernel,
         in_specs=whole(1),
-        out_specs=whole(3),
-        out_shape=[
-            sds((4 * count, cols), BF),
-            sds((nb, 64, 128), BF),
-            sds((nb, 64, 128), F32),
-        ],
-        scratch_shapes=[pltpu.VMEM((2, nb, 64, 128), F32)],
+        out_specs=whole(2),
+        out_shape=[sds((4 * count, 2 * half), BF), sds((8, 16 * nb, 128), BF)],
         compiler_params=params(),
         name="partial_gram",
     )(a)
 
 
-def polish_kernel(scale, own, other, rows_ref, out, slabs, level, low, poly, high):
-    c = lax.rem(lax.axis_index("dp"), 2)
+def polish_kernel(scale, gram, rows_ref, out, level, low, poly, high):
     count, cols = rows_ref.shape
     n = cols // 128
-    slabs[c] = own[...].astype(F32)
-    slabs[1 - c] = other[...].astype(F32)
+
+    def block_of(b):
+        return gram[:, 16 * b : 16 * b + 16, :].reshape(128, 128).astype(F32)
 
     eye = (
         lax.broadcasted_iota(jnp.int32, (128, 128), 0) == lax.broadcasted_iota(jnp.int32, (128, 128), 1)
@@ -182,12 +177,12 @@
     diag = jnp.zeros((128, 128), F32)
     for b, (i, j) in enumerate(blocks_of(cols)):
         if i == j:
-            diag += slabs[:, b].reshape(128, 128)
+            diag += block_of(b)
     trace = jnp.sum(jnp.where(eye, diag, 0.0))
     inv_norm = 1.0 / (jnp.sqrt(jnp.full((1, 1), trace)) + 1e-7)
     square = inv_norm * inv_norm
     for b, (i, j) in enumerate(blocks_of(cols)):
-        block = slabs[:, b].reshape(128, 128) * square
+        block = block_of(b) * square
         level[128 * i : 128 * i + 128, 128 * j : 128 * j + 128] = block
         low[128 * i : 128 * i + 128, 128 * j : 128 * j + 128] = block.astype(BF)
         if i != j:
@@ -215,16 +210,14 @@
         out[i] = result[4 * i : 4 * i + 4, :].astype(BF)
 
 
-def polish(scale, own, other, rows):
+def polish(scale, gram, rows):
     count, cols = rows.shape
-    nb = own.shape[0]
     return pl.pallas_call(
         functools.partial(polish_kernel, scale),
-        in_specs=whole(3),
+        in_specs=whole(2),
         out_specs=whole(1)[0],
         out_shape=sds((count // 4, 4, cols), BF),
         scratch_shapes=[
-            pltpu.VMEM((2, nb, 64, 128), F32),
             pltpu.VMEM((cols, cols), F32),
             pltpu.VMEM((cols, cols), BF),
             pltpu.VMEM((cols, cols), BF),
@@ -232,7 +225,7 @@
         ],
         compiler_params=params(32),
         name="polish",
-    )(own, other, rows)
+    )(gram, rows)
 
 
 def core_swap(v):
@@ -248,10 +241,8 @@
     return lax.ppermute(v, "dp", perm)
 
 
-def exchange(v):
-    order = np.random.RandomState(7).permutation(v.shape[0])
-    groups = [[int(i) for i in order]]
-    return lax.all_to_all(v, "fsdp", split_axis=0, concat_axis=0, axis_index_groups=groups, tiled=True)
+def exchange(v, axis):
+    return lax.all_to_all(v, axis, split_axis=0, concat_axis=0, tiled=True)
 
 
 def shards(n_rows, grads, momentum, slot_matrix):
@@ -259,25 +250,23 @@
     cols = grads.shape[3]
 
     send_across, send_rest, keep_across, keep_rest = split_rows(grads, 8)
-    across = keep_across.astype(F32) + core_swap(send_across).astype(F32)
-    first_far = y_swap(across.astype(BF), 0)
+    across = (keep_across.astype(F32) + core_swap(send_across).astype(F32)).astype(BF)
+    across, send_rest = lax.optimization_barrier((across, send_rest))
+    first_far = y_swap(across, 0)
     swapped = core_swap(send_rest)
     first_own = y_swap((keep_rest[2].astype(F32) + swapped[2].astype(F32)).astype(BF), 0)
     far = (keep_rest[1].astype(F32) + swapped[1].astype(F32)) + first_far.astype(F32)
     second = y_swap(far.astype(BF), 1)
     nesterov, new_momentum = momentum_step(slot_matrix, keep_rest, swapped, first_own, second, momentum)
 
-    mine = exchange(nesterov)
-
-    rows, gram_send, gram_keep = partial_gram(mine)
-    gram = gram_keep + core_swap(gram_send).astype(F32)
-    gram = gram + y_swap(gram.astype(BF), 0).astype(F32)
-    gram = gram + y_swap(gram.astype(BF), 1).astype(F32)
-    own = gram.astype(BF)
-    other = core_swap(own)
-
-    update = polish(math.sqrt(max(n_rows, cols)), own, other, rows)
-    return (exchange(update), new_momentum)
+    mine = exchange(nesterov, "fsdp")
+
+    rows, gram = partial_gram(mine)
+    summed = jnp.sum(exchange(gram, "dp").astype(F32), axis=0).astype(BF)
+    gram = exchange(jnp.broadcast_to(summed[None], gram.shape), "dp")
+
+    update = polish(math.sqrt(max(n_rows, cols)), gram, rows)
+    return (exchange(update, "fsdp"), new_momentum)
 
 
 def solution(mesh):

time: 142 us -> 144 us (1.014); the launches traced: 140 us -> 144 us
  blocking collectives: 75.9 us -> 107 us
  waiting for transfers between devices: 26.1 us -> 10.8 us
  starting transfers between devices: 26.4 us -> 15.2 us
    all_to_all x2 -> x4, blocking collectives: 75.9 us -> 107 us  [exchange(): return lax.all_to_all(v, axis, split_axis=0, concat_axis=0, tiled=True)]
    ppermute x5 -> x3, waiting for transfers between devices: 21.5 us -> 9.09 us  [y_swap(): return lax.ppermute(v, 'dp', perm)]
    ppermute x5 -> x3, starting transfers between devices: 18.2 us -> 11.2 us  [y_swap(): return lax.ppermute(v, 'dp', perm)]
    ppermute x4 -> x2, starting transfers between devices: 8.17 us -> 3.97 us  [core_swap(): return lax.ppermute(v, 'dp', [(i, i ^ 1) for i in range(2 * NY)])]
    ppermute x4 -> x2, waiting for transfers between devices: 4.57 us -> 1.69 us  [core_swap(): return lax.ppermute(v, 'dp', [(i, i ^ 1) for i in range(2 * NY)])]
  transfers between devices with their start and end apart: 9 -> 5, of which waited for: 7 -> 3; matrix products, arithmetic and copies ran while one was open for 1% -> 0% of each run, Pallas kernels for 0% -> 0%
where the time goes in v5:
time: 144 us
  blocking collectives  107 us (74%)
  starting transfers between devices  15.2 us (11%)
  waiting for transfers between devices  10.8 us (8%)
  Pallas kernels  8.74 us (6%)
    all_to_all x4, blocking collectives, exchange(): return lax.all_to_all(v, axis, split_axis=0, concat_axis=0, tiled=True)  107 us
    ppermute x3, starting transfers between devices, y_swap(): return lax.ppermute(v, 'dp', perm)  11.2 us
    ppermute x3, waiting for transfers between devices, y_swap(): return lax.ppermute(v, 'dp', perm)  9.09 us
    pallas_call x1, Pallas kernels, polish(): pl.pallas_call(functools.partial(polish_kernel, scale), in_specs=whole(2)...  4.4 us
    ppermute x2, starting transfers between devices, core_swap(): return lax.ppermute(v, 'dp', [(i, i ^ 1) for i in range(2 * NY)])  3.97 us
  transfers between devices with their start and end apart: 5, of which 3 were waited for; matrix products, arithmetic and copies ran while one was open for 0% of the time, Pallas kernels for 0%

profile of v5, /device:TPU:6, one launch (start us, length us, event | category | flops | bytes accessed | tf_op | source)
XLA Modules:
  0.0 143.7 jit_solution(3633552665100747387)
XLA Ops:
  0.6 2.0 %split_rows.1 = (bf16[64,4,768]{2,1,0:T(4,128)(2,1)S(1)}, bf16[3,64,4,768]{3,2,1,0:T(4,128)(2,1)S(1)}, bf16[64,4,768]{2,1,0:T(4,128)(2,1)S(1)}, bf16[3,64,4,768]{3,2,1,0:T(4,128)(2,1)S(1)}) custom-call(bf16[1,64,32,768]{3,2,1,0:T(8,128)(2,1)} %g_hbm.1), custom_call_target="tpu_custom_call" | custom-call | tf_op jit(solution)/shard_map/split_rows/pallas_call | solution.py:81
  2.7 1.9 %collective-permute-start = (bf16[64,4,768]{2,1,0:T(4,128)(2,1)S(1)}, bf16[64,4,768]{2,1,0:T(4,128)(2,1)S(1)}, u32[]{:S(2)}, u32[]{:S(2)}) collective-permute-start(bf16[64,4,768]{2,1,0:T(4,128)(2,1)S(1)} %get-tuple-element.14), channel_id=1, source_target_pairs={{0,64},{64,0},{128,192},{192,128},{256,320},{320,256},{384,448},{4... | collective-permute-start | bytes 1179656 | tf_op jit(solution)/shard_map/ppermute | solution.py:232
  4.6 1.7 %collective-permute-done = bf16[64,4,768]{2,1,0:T(4,128)(2,1)S(1)} collective-permute-done((bf16[64,4,768]{2,1,0:T(4,128)(2,1)S(1)}, bf16[64,4,768]{2,1,0:T(4,128)(2,1)S(1)}, u32[]{:S(2)}, u32[]{:S(2)}) %collective-permute-start) | collective-permute-done | bytes 393248 | tf_op jit(solution)/shard_map/ppermute | solution.py:232
  6.3 0.2 add_convert_fusion.1
  6.5 2.0 %collective-permute-start.1 = (bf16[3,64,4,768]{3,2,1,0:T(4,128)(2,1)S(1)}, bf16[3,64,4,768]{3,2,1,0:T(4,128)(2,1)S(1)}, u32[]{:S(2)}, u32[]{:S(2)}) collective-permute-start(bf16[3,64,4,768]{3,2,1,0:T(4,128)(2,1)S(1)} %get-tuple-element.16), channel_id=1, source_target_pairs={{0,64},{64,0},{128,192},{192,128},{256,320},{320,256},{384,448},{4... | collective-permute-start | bytes 3538952 | tf_op jit(solution)/shard_map/ppermute | solution.py:232
  8.5 3.5 %collective-permute-start.3 = (bf16[64,4,768]{2,1,0:T(4,128)(2,1)S(1)}, bf16[64,4,768]{2,1,0:T(4,128)(2,1)S(1)}, u32[]{:S(2)}, u32[]{:S(2)}) collective-permute-start(bf16[64,4,768]{2,1,0:T(4,128)(2,1)S(1)} %add_convert_fusion.1), channel_id=1, source_target_pairs={{0,128},{64,448},{128,0},{192,320},{256,384},{320,192},{384,256},{... | collective-permute-start | bytes 1179656 | tf_op jit(solution)/shard_map/ppermute | solution.py:241
  12.0 0.0 collective-permute-done.1.swapped
  12.0 0.0 copy-start
  12.1 0.0 copy-start.1
  12.1 0.2 fusion.1
  12.3 2.8 %collective-permute-start.2 = (bf16[64,4,768]{2,1,0:T(4,128)(2,1)S(1)}, bf16[64,4,768]{2,1,0:T(4,128)(2,1)S(1)}, u32[]{:S(2)}, u32[]{:S(2)}) collective-permute-start(bf16[64,4,768]{2,1,0:T(4,128)(2,1)S(1)} %fusion.1), channel_id=1, source_target_pairs={{0,128},{64,448},{128,0},{192,320},{256,384},{320,192},{384,256},{... | collective-permute-start | bytes 1179656 | tf_op jit(solution)/shard_map/ppermute | solution.py:241
  15.1 3.1 %collective-permute-done.3 = bf16[64,4,768]{2,1,0:T(4,128)(2,1)S(1)} collective-permute-done((bf16[64,4,768]{2,1,0:T(4,128)(2,1)S(1)}, bf16[64,4,768]{2,1,0:T(4,128)(2,1)S(1)}, u32[]{:S(2)}, u32[]{:S(2)}) %collective-permute-start.3) | collective-permute-done | bytes 393248 | tf_op jit(solution)/shard_map/ppermute | solution.py:241
  18.2 0.3 fusion
  18.5 4.9 %collective-permute-start.4 = (bf16[64,4,768]{2,1,0:T(4,128)(2,1)S(1)}, bf16[64,4,768]{2,1,0:T(4,128)(2,1)S(1)}, u32[]{:S(2)}, u32[]{:S(2)}) collective-permute-start(bf16[64,4,768]{2,1,0:T(4,128)(2,1)S(1)} %fusion), channel_id=1, source_target_pairs={{0,384},{64,192},{128,256},{192,64},{256,128},{320,448},{384,0},{4... | collective-permute-start | bytes 1179656 | tf_op jit(solution)/shard_map/ppermute | solution.py:241
  23.5 0.0 collective-permute-done.2.first
  23.5 5.9 %collective-permute-done.4.second = bf16[64,4,768]{2,1,0:T(4,128)(2,1)S(1)} collective-permute-done((bf16[64,4,768]{2,1,0:T(4,128)(2,1)S(1)}, bf16[64,4,768]{2,1,0:T(4,128)(2,1)S(1)}, u32[]{:S(2)}, u32[]{:S(2)}) %collective-permute-start.4) | collective-permute-done | bytes 393248 | tf_op jit(solution)/shard_map/ppermute | solution.py:241
  29.4 0.0 copy-done
  29.4 0.0 copy-done.1
  29.4 1.8 %momentum_step.1 = (bf16[64,8,384]{2,1,0:T(8,128)(2,1)S(1)}, f32[64,4,768]{2,1,0:T(4,128)}) custom-call(s32[64]{0:T(128)S(1)} %copy-done.1, bf16[3,64,4,768]{3,2,1,0:T(4,128)(2,1)S(1)} %get-tuple-element.12.keep, bf16[3,64,4,768]{3,2,1,0:T(4,128)(2,1)S(1)} %collective-permute-done.1.swapped, bf16[64,4,768]{2,1,0:T(4,128)(2,1)S(1)} %collective-permute-done.2.first, ...), custom_call_target="tpu_custom_call" | custom-call | tf_op jit(solution)/shard_map/momentum_step/pallas_call | solution.py:116
  31.2 43.5 %all_to_all.20.a_ref = bf16[64,8,384]{2,1,0:T(8,128)(2,1)S(1)} all-to-all(bf16[64,8,384]{2,1,0:T(8,128)(2,1)S(1)} %get-tuple-element.18), channel_id=1, replica_groups=mesh['dp'=8,'fsdp'=64] {'fsdp'}, dimensions={0} | all-to-all | bytes 786432 | tf_op jit(solution)/shard_map/all_to_all | solution.py:245
  74.7 0.5 partial_gram.1
  75.2 16.2 %all_to_all.21 = bf16[8,336,128]{2,1,0:T(8,128)(2,1)S(1)} all-to-all(bf16[8,336,128]{2,1,0:T(8,128)(2,1)S(1)} %get-tuple-element.19), channel_id=1, replica_groups=mesh['dp'=8,'fsdp'=64] {'dp'}, dimensions={0} | all-to-all | bytes 1376256 | tf_op jit(solution)/shard_map/all_to_all | solution.py:245
  91.4 0.1 reduce_sum.12
  91.5 0.1 broadcast_in_dim.2
  91.6 14.5 %all_to_all.22.gram = bf16[8,336,128]{2,1,0:T(8,128)(2,1)S(1)} all-to-all(bf16[8,336,128]{2,1,0:T(8,128)(2,1)S(1)} %broadcast_in_dim.2), channel_id=1, replica_groups=mesh['dp'=8,'fsdp'=64] {'dp'}, dimensions={0} | all-to-all | bytes 1376256 | tf_op jit(solution)/shard_map/all_to_all | solution.py:245
  106.1 4.4 %polish.1 = bf16[64,4,768]{2,1,0:T(4,128)(2,1)S(1)} custom-call(bf16[8,336,128]{2,1,0:T(8,128)(2,1)S(1)} %all_to_all.22.gram, bf16[256,768]{1,0:T(8,128)(2,1)S(1)} %get-tuple-element.20.rows_ref), custom_call_target="tpu_custom_call" | custom-call | tf_op jit(solution)/shard_map/polish/pallas_call | solution.py:215
  110.5 32.5 %all_to_all.23 = bf16[64,4,768]{2,1,0:T(4,128)(2,1)S(1)} all-to-all(bf16[64,4,768]{2,1,0:T(4,128)(2,1)S(1)} %polish.1), channel_id=1, replica_groups=mesh['dp'=8,'fsdp'=64] {'fsdp'}, dimensions={0} | all-to-all | bytes 786432 | tf_op jit(solution)/shard_map/all_to_all | solution.py:245
  143.0 0.7 copy.6
Async XLA Ops:
  2.7 3.6 %collective-permute-start = (bf16[64,4,768]{2,1,0:T(4,128)(2,1)S(1)}, bf16[64,4,768]{2,1,0:T(4,128)(2,1)S(1)}, u32[]{:S(2)}, u32[]{:S(2)}) collective-permute-start(bf16[64,4,768]{2,1,0:T(4,128)(2,1)S(1)} %get-tuple-element.14), channel_id=1, source_target_pairs={{0,64},{64,0},{128,192},{192,128},{256,320},{320,256},{384,448},{4... | collective-permute-start | bytes 1179656 | tf_op jit(solution)/shard_map/ppermute | solution.py:232
  6.5 5.5 %collective-permute-start.1 = (bf16[3,64,4,768]{3,2,1,0:T(4,128)(2,1)S(1)}, bf16[3,64,4,768]{3,2,1,0:T(4,128)(2,1)S(1)}, u32[]{:S(2)}, u32[]{:S(2)}) collective-permute-start(bf16[3,64,4,768]{3,2,1,0:T(4,128)(2,1)S(1)} %get-tuple-element.16), channel_id=1, source_target_pairs={{0,64},{64,0},{128,192},{192,128},{256,320},{320,256},{384,448},{4... | collective-permute-start | bytes 3538952 | tf_op jit(solution)/shard_map/ppermute | solution.py:232
  8.5 9.7 %collective-permute-start.3 = (bf16[64,4,768]{2,1,0:T(4,128)(2,1)S(1)}, bf16[64,4,768]{2,1,0:T(4,128)(2,1)S(1)}, u32[]{:S(2)}, u32[]{:S(2)}) collective-permute-start(bf16[64,4,768]{2,1,0:T(4,128)(2,1)S(1)} %add_convert_fusion.1), channel_id=1, source_target_pairs={{0,128},{64,448},{128,0},{192,320},{256,384},{320,192},{384,256},{... | collective-permute-start | bytes 1179656 | tf_op jit(solution)/shard_map/ppermute | solution.py:241
  12.0 17.4 %copy-start = (f32[64,4,768]{2,1,0:T(4,128)S(1)}, f32[64,4,768]{2,1,0:T(4,128)}, u32[]{:S(2)}) copy-start(f32[64,4,768]{2,1,0:T(4,128)} %mom.1) | copy-start | bytes 2359300
  12.1 17.4 %copy-start.1 = (s32[64]{0:T(128)S(1)}, s32[64]{0:T(128)}, u32[]{:S(2)}) copy-start(s32[64]{0:T(128)} %slots.1) | copy-start | bytes 772
  12.3 11.2 %collective-permute-start.2 = (bf16[64,4,768]{2,1,0:T(4,128)(2,1)S(1)}, bf16[64,4,768]{2,1,0:T(4,128)(2,1)S(1)}, u32[]{:S(2)}, u32[]{:S(2)}) collective-permute-start(bf16[64,4,768]{2,1,0:T(4,128)(2,1)S(1)} %fusion.1), channel_id=1, source_target_pairs={{0,128},{64,448},{128,0},{192,320},{256,384},{320,192},{384,256},{... | collective-permute-start | bytes 1179656 | tf_op jit(solution)/shard_map/ppermute | solution.py:241
  18.5 10.9 %collective-permute-start.4 = (bf16[64,4,768]{2,1,0:T(4,128)(2,1)S(1)}, bf16[64,4,768]{2,1,0:T(4,128)(2,1)S(1)}, u32[]{:S(2)}, u32[]{:S(2)}) collective-permute-start(bf16[64,4,768]{2,1,0:T(4,128)(2,1)S(1)} %fusion), channel_id=1, source_target_pairs={{0,384},{64,192},{128,256},{192,64},{256,128},{320,448},{384,0},{4... | collective-permute-start | bytes 1179656 | tf_op jit(solution)/shard_map/ppermute | solution.py:241

commit v6 on v4

--- a/solution.py
+++ b/solution.py
@@ -3,7 +3,6 @@
 
 import jax
 import jax.numpy as jnp
-import numpy as np
 from jax import lax
 from jax.experimental import pallas as pl
 from jax.experimental.pallas import tpu as pltpu
@@ -40,7 +39,7 @@
     return y, c, near, far, lax.rem(y + 2, NY)
 
 
-def split_kernel(g_hbm, send_across, send_rest, keep_across, keep_rest, raw, wide, sems):
+def split_kernel(g_hbm, send_a, send_b, keep_a, keep_b, raw, wide, sems):
     y, c, near, far, across = place_of()
     parts = sems.shape[0]
     mb = raw.shape[0] // parts
@@ -60,14 +59,14 @@
             both = wide[:, pl.ds(pl.multiple_of(8 * yy, 8), 8), :]
             return both[:, 4 * core : 4 * core + 4, :].astype(BF)
 
-        send_across[here] = rows(across, 1 - low)
-        send_rest[0, here] = rows(y, 1 - low)
-        send_rest[1, here] = rows(near, 1 - low)
-        send_rest[2, here] = rows(far, 1 - low)
-        keep_across[here] = rows(across, low)
-        keep_rest[0, here] = rows(y, low)
-        keep_rest[1, here] = rows(far, low)
-        keep_rest[2, here] = rows(near, low)
+        send_a[0, here] = rows(across, 1 - low)
+        send_a[1, here] = rows(far, 1 - low)
+        send_b[0, here] = rows(y, 1 - low)
+        send_b[1, here] = rows(near, 1 - low)
+        keep_a[0, here] = rows(across, low)
+        keep_a[1, here] = rows(near, low)
+        keep_b[0, here] = rows(y, low)
+        keep_b[1, here] = rows(far, low)
 
     for i in range(parts):
         fetch(i).wait()
@@ -78,12 +77,12 @@
 
 def split_rows(grads, parts):
     _, m, rows, cols = grads.shape
-    one, three = sds((m, 4, cols), BF), sds((3, m, 4, cols), BF)
+    two = sds((2, m, 4, cols), BF)
     return pl.pallas_call(
         split_kernel,
         in_specs=[pl.BlockSpec(memory_space=pl.ANY)],
         out_specs=whole(4),
-        out_shape=[one, three, one, three],
+        out_shape=[two] * 4,
         scratch_shapes=[
             pltpu.VMEM((m, rows, cols), BF),
             pltpu.VMEM((m // parts, rows, cols), F32),
@@ -94,32 +93,44 @@
     )(grads)
 
 
-def momentum_kernel(slots, keep, swapped, first, second, mom, nesterov, new_mom):
-    m = mom.shape[0]
-
+def gradient_at(j, keep, swapped, first, second):
+    return (keep[0, j].astype(F32) + swapped[0, j].astype(F32)) + (
+        first[j].astype(F32) + second[j].astype(F32)
+    )
+
+
+def nesterov_kernel(slots, keep, swapped, first, second, mom, nesterov):
     def step(j, carry):
         mat = slots[j]
-        gradient = (keep[0, j].astype(F32) + swapped[0, j].astype(F32)) + (
-            first[j].astype(F32) + second[j].astype(F32)
-        )
-        new = DECAY * mom[mat] + gradient
-        new_mom[mat] = new
-        nesterov[mat] = (gradient + DECAY * new).astype(BF)
+        gradient = gradient_at(j, keep, swapped, first, second)
+        nesterov[mat] = (gradient + DECAY * (DECAY * mom[mat] + gradient)).astype(BF)
         return carry
 
+    m = mom.shape[0]
     lax.fori_loop(0, m, step, 0, unroll=min(8, m))
 
 
-def momentum_step(slots, keep, swapped, first, second, mom):
-    m, _, cols = mom.shape
+def momentum_kernel(slots, keep, swapped, first, second, mom, new_mom):
+    def step(j, carry):
+        mat = slots[j]
+        new_mom[mat] = DECAY * mom[mat] + gradient_at(j, keep, swapped, first, second)
+        return carry
+
+    m = mom.shape[0]
+    lax.fori_loop(0, m, step, 0, unroll=min(8, m))
+
+
+def momentum_call(kernel, dtype, name, *args):
+    mom = args[-1]
     return pl.pallas_call(
-        momentum_kernel,
+        kernel,
         in_specs=[pl.BlockSpec(memory_space=SMEM)] + whole(5),
-        out_specs=whole(2),
-        out_shape=[sds((m, 4, cols), BF), sds((m, 4, cols), F32)],
+        out_specs=whole(1)[0],
+        out_shape=sds(mom.shape, dtype),
         compiler_params=params(),
-        name="momentum_step",
-    )(slots, keep, swapped, first, second, mom)
+        cost_estimate=pl.CostEstimate(flops=6 * mom.size, bytes_accessed=16 * mom.size, transcendentals=0),
+        name=name,
+    )(*args)
 
 
 def blocks_of(cols):
@@ -249,27 +260,28 @@
 
 
 def exchange(v):
-    order = np.random.RandomState(7).permutation(v.shape[0])
-    groups = [[int(i) for i in order]]
-    return lax.all_to_all(v, "fsdp", split_axis=0, concat_axis=0, axis_index_groups=groups, tiled=True)
+    return lax.all_to_all(v, "fsdp", split_axis=0, concat_axis=0, tiled=True)
 
 
 def shards(n_rows, grads, momentum, slot_matrix):
     m = grads.shape[1]
     cols = grads.shape[3]
 
-    send_across, send_rest, keep_across, keep_rest = split_rows(grads, 8)
-    across = keep_across.astype(F32) + core_swap(send_across).astype(F32)
-    first_far = y_swap(across.astype(BF), 0)
-    swapped = core_swap(send_rest)
-    first_own = y_swap((keep_rest[2].astype(F32) + swapped[2].astype(F32)).astype(BF), 0)
-    far = (keep_rest[1].astype(F32) + swapped[1].astype(F32)) + first_far.astype(F32)
+    send_a, send_b, keep_a, keep_b = split_rows(grads, 8)
+    swapped_a = core_swap(send_a)
+    swapped_b = core_swap(send_b)
+    first_far = y_swap((keep_a[0].astype(F32) + swapped_a[0].astype(F32)).astype(BF), 0)
+    first_own = y_swap((keep_a[1].astype(F32) + swapped_a[1].astype(F32)).astype(BF), 0)
+    far = (keep_b[1].astype(F32) + swapped_b[1].astype(F32)) + first_far.astype(F32)
     second = y_swap(far.astype(BF), 1)
-    nesterov, new_momentum = momentum_step(slot_matrix, keep_rest, swapped, first_own, second, momentum)
+    parts = (slot_matrix, keep_b, swapped_b, first_own, second, momentum)
+    nesterov = momentum_call(nesterov_kernel, BF, "nesterov", *parts)
 
     mine = exchange(nesterov)
 
     rows, gram_send, gram_keep = partial_gram(mine)
+    gram_keep, parts = lax.optimization_barrier((gram_keep, parts))
+    new_momentum = momentum_call(momentum_kernel, F32, "new_momentum", *parts)
     gram = gram_keep + core_swap(gram_send).astype(F32)
     gram = gram + y_swap(gram.astype(BF), 0).astype(F32)
     gram = gram + y_swap(gram.astype(BF), 1).astype(F32)

time: 142 us -> 140 us (0.986)
  blocking collectives: 75.9 us -> 43.1 us
  waiting for transfers between devices: 26.1 us -> 49.7 us
  starting transfers between devices: 26.4 us -> 33.2 us
  Pallas kernels: 9 us -> 10.6 us
    all_to_all x2 -> x1, blocking collectives: 75.9 us -> 43.1 us  [exchange(): return lax.all_to_all(v, 'fsdp', split_axis=0, concat_axis=0, tiled=True)]
    all_to_all x0 -> x1, waiting for transfers between devices: none -> 24.8 us  [exchange(): return lax.all_to_all(v, 'fsdp', split_axis=0, concat_axis=0, tiled=True)]
    all_to_all x0 -> x1, starting transfers between devices: none -> 6.66 us  [exchange(): return lax.all_to_all(v, 'fsdp', split_axis=0, concat_axis=0, tiled=True)]
  transfers between devices with their start and end apart: 9 -> 10, of which waited for: 7 -> 7; matrix products, arithmetic and copies ran while one was open for 1% -> 1% of each run, Pallas kernels for 0% -> 1%
where the time goes in v6:
time: 140 us; the launch traced here: 139 us
  waiting for transfers between devices  49.7 us (36%)
  blocking collectives  43.1 us (31%)
  starting transfers between devices  33.2 us (24%)
  Pallas kernels  10.6 us (8%)
    all_to_all x1, blocking collectives, exchange(): return lax.all_to_all(v, 'fsdp', split_axis=0, concat_axis=0, tiled=True)  43.1 us
    all_to_all x1, waiting for transfers between devices, exchange(): return lax.all_to_all(v, 'fsdp', split_axis=0, concat_axis=0, tiled=True)  24.8 us
    ppermute x5, waiting for transfers between devices, y_swap(): return lax.ppermute(v, 'dp', perm)  21.6 us
    ppermute x5, starting transfers between devices, y_swap(): return lax.ppermute(v, 'dp', perm)  18.3 us
    ppermute x4, starting transfers between devices, core_swap(): return lax.ppermute(v, 'dp', [(i, i ^ 1) for i in range(2 * NY)])  8.17 us
    all_to_all x1, starting transfers between devices, exchange(): return lax.all_to_all(v, 'fsdp', split_axis=0, concat_axis=0, tiled=True)  6.66 us
    pallas_call x1, Pallas kernels, polish(): pl.pallas_call(functools.partial(polish_kernel, scale), in_specs=whole(3)...  5.23 us
    ppermute x4, waiting for transfers between devices, core_swap(): return lax.ppermute(v, 'dp', [(i, i ^ 1) for i in range(2 * NY)])  3.24 us
  transfers between devices with their start and end apart: 10, of which 7 were waited for; matrix products, arithmetic and copies ran while one was open for 1% of the time, Pallas kernels for 1%

profile of v6, /device:TPU:6, one launch (start us, length us, event | category | flops | bytes accessed | tf_op | source)
XLA Modules:
  0.0 139.3 jit_solution(5748257389003561111)
XLA Ops:
  0.6 0.0 copy-start.1
  0.6 0.0 copy-start
  0.6 2.1 %split_rows.1 = (bf16[2,64,4,768]{3,2,1,0:T(4,128)(2,1)S(1)}, bf16[2,64,4,768]{3,2,1,0:T(4,128)(2,1)S(1)}, bf16[2,64,4,768]{3,2,1,0:T(4,128)(2,1)S(1)}, bf16[2,64,4,768]{3,2,1,0:T(4,128)(2,1)S(1)}) custom-call(bf16[1,64,32,768]{3,2,1,0:T(8,128)(2,1)} %g_hbm.1), custom_call_target="tpu_custom_call" | custom-call | tf_op jit(solution)/shard_map/split_rows/pallas_call | solution.py:81
  2.8 1.9 %collective-permute-start.1 = (bf16[2,64,4,768]{3,2,1,0:T(4,128)(2,1)S(1)}, bf16[2,64,4,768]{3,2,1,0:T(4,128)(2,1)S(1)}, u32[]{:S(2)}, u32[]{:S(2)}) collective-permute-start(bf16[2,64,4,768]{3,2,1,0:T(4,128)(2,1)S(1)} %get-tuple-element.19), channel_id=1, source_target_pairs={{0,64},{64,0},{128,192},{192,128},{256,320},{320,256},{384,448},{4... | collective-permute-start | bytes 2359304 | tf_op jit(solution)/shard_map/ppermute | solution.py:250
  4.7 2.4 %collective-permute-start = (bf16[2,64,4,768]{3,2,1,0:T(4,128)(2,1)S(1)}, bf16[2,64,4,768]{3,2,1,0:T(4,128)(2,1)S(1)}, u32[]{:S(2)}, u32[]{:S(2)}) collective-permute-start(bf16[2,64,4,768]{3,2,1,0:T(4,128)(2,1)S(1)} %get-tuple-element.17), channel_id=1, source_target_pairs={{0,64},{64,0},{128,192},{192,128},{256,320},{320,256},{384,448},{4... | collective-permute-start | bytes 2359304 | tf_op jit(solution)/shard_map/ppermute | solution.py:250
  7.1 0.0 collective-permute-done.1
  7.1 0.4 fusion.3
  7.5 3.5 %collective-permute-start.3 = (bf16[64,4,768]{2,1,0:T(4,128)(2,1)S(1)}, bf16[64,4,768]{2,1,0:T(4,128)(2,1)S(1)}, u32[]{:S(2)}, u32[]{:S(2)}) collective-permute-start(bf16[64,4,768]{2,1,0:T(4,128)(2,1)S(1)} %get-tuple-element.30), channel_id=1, source_target_pairs={{0,128},{64,448},{128,0},{192,320},{256,384},{320,192},{384,256},{... | collective-permute-start | bytes 1179656 | tf_op jit(solution)/shard_map/ppermute | solution.py:259
  11.0 2.4 %collective-permute-start.2 = (bf16[64,4,768]{2,1,0:T(4,128)(2,1)S(1)}, bf16[64,4,768]{2,1,0:T(4,128)(2,1)S(1)}, u32[]{:S(2)}, u32[]{:S(2)}) collective-permute-start(bf16[64,4,768]{2,1,0:T(4,128)(2,1)S(1)} %get-tuple-element.31), channel_id=1, source_target_pairs={{0,128},{64,448},{128,0},{192,320},{256,384},{320,192},{384,256},{... | collective-permute-start | bytes 1179656 | tf_op jit(solution)/shard_map/ppermute | solution.py:259
  13.4 0.0 collective-permute-done.swapped
  13.4 3.8 %collective-permute-done.3 = bf16[64,4,768]{2,1,0:T(4,128)(2,1)S(1)} collective-permute-done((bf16[64,4,768]{2,1,0:T(4,128)(2,1)S(1)}, bf16[64,4,768]{2,1,0:T(4,128)(2,1)S(1)}, u32[]{:S(2)}, u32[]{:S(2)}) %collective-permute-start.3) | collective-permute-done | bytes 393248 | tf_op jit(solution)/shard_map/ppermute | solution.py:259
  17.2 0.3 fusion
  17.5 4.9 %collective-permute-start.4 = (bf16[64,4,768]{2,1,0:T(4,128)(2,1)S(1)}, bf16[64,4,768]{2,1,0:T(4,128)(2,1)S(1)}, u32[]{:S(2)}, u32[]{:S(2)}) collective-permute-start(bf16[64,4,768]{2,1,0:T(4,128)(2,1)S(1)} %fusion), channel_id=1, source_target_pairs={{0,384},{64,192},{128,256},{192,64},{256,128},{320,448},{384,0},{4... | collective-permute-start | bytes 1179656 | tf_op jit(solution)/shard_map/ppermute | solution.py:259
  22.4 0.0 collective-permute-done.2.first
  22.4 5.9 %collective-permute-done.4.second = bf16[64,4,768]{2,1,0:T(4,128)(2,1)S(1)} collective-permute-done((bf16[64,4,768]{2,1,0:T(4,128)(2,1)S(1)}, bf16[64,4,768]{2,1,0:T(4,128)(2,1)S(1)}, u32[]{:S(2)}, u32[]{:S(2)}) %collective-permute-start.4) | collective-permute-done | bytes 393248 | tf_op jit(solution)/shard_map/ppermute | solution.py:259
  28.4 0.0 copy-done.1
  28.4 0.0 copy-done
  28.4 1.0 nesterov.1
  29.4 43.1 %all_to_all.10.a_ref = bf16[64,4,768]{2,1,0:T(4,128)(2,1)S(1)} all-to-all(bf16[64,4,768]{2,1,0:T(4,128)(2,1)S(1)} %nesterov.1), channel_id=1, replica_groups=mesh['dp'=8,'fsdp'=64] {'fsdp'}, dimensions={0} | all-to-all | bytes 786432 | tf_op jit(solution)/shard_map/all_to_all | solution.py:263
  72.5 0.6 partial_gram.1
  73.2 1.9 %collective-permute-start.5 = (bf16[21,64,128]{2,1,0:T(8,128)(2,1)S(1)}, bf16[21,64,128]{2,1,0:T(8,128)(2,1)S(1)}, u32[]{:S(2)}, u32[]{:S(2)}) collective-permute-start(bf16[21,64,128]{2,1,0:T(8,128)(2,1)S(1)} %get-tuple-element.22), channel_id=1, source_target_pairs={{0,64},{64,0},{128,192},{192,128},{256,320},{320,256},{384,448},{4... | collective-permute-start | bytes 1032200 | tf_op jit(solution)/shard_map/ppermute | solution.py:250
  75.1 1.6 %collective-permute-done.5 = bf16[21,64,128]{2,1,0:T(8,128)(2,1)S(1)} collective-permute-done((bf16[21,64,128]{2,1,0:T(8,128)(2,1)S(1)}, bf16[21,64,128]{2,1,0:T(8,128)(2,1)S(1)}, u32[]{:S(2)}, u32[]{:S(2)}) %collective-permute-start.5) | collective-permute-done | bytes 344096 | tf_op jit(solution)/shard_map/ppermute | solution.py:250
  76.7 0.1 fusion.1
  76.8 2.7 %collective-permute-start.6 = (bf16[21,64,128]{2,1,0:T(8,128)(2,1)S(1)}, bf16[21,64,128]{2,1,0:T(8,128)(2,1)S(1)}, u32[]{:S(2)}, u32[]{:S(2)}) collective-permute-start(bf16[21,64,128]{2,1,0:T(8,128)(2,1)S(1)} %fusion.1), channel_id=1, source_target_pairs={{0,128},{64,448},{128,0},{192,320},{256,384},{320,192},{384,256},{... | collective-permute-start | bytes 1032200 | tf_op jit(solution)/shard_map/ppermute | solution.py:259
  79.5 6.4 %collective-permute-done.6 = bf16[21,64,128]{2,1,0:T(8,128)(2,1)S(1)} collective-permute-done((bf16[21,64,128]{2,1,0:T(8,128)(2,1)S(1)}, bf16[21,64,128]{2,1,0:T(8,128)(2,1)S(1)}, u32[]{:S(2)}, u32[]{:S(2)}) %collective-permute-start.6) | collective-permute-done | bytes 344096 | tf_op jit(solution)/shard_map/ppermute | solution.py:259
  86.0 0.1 fusion.4
  86.1 4.8 %collective-permute-start.7 = (bf16[21,64,128]{2,1,0:T(8,128)(2,1)S(1)}, bf16[21,64,128]{2,1,0:T(8,128)(2,1)S(1)}, u32[]{:S(2)}, u32[]{:S(2)}) collective-permute-start(bf16[21,64,128]{2,1,0:T(8,128)(2,1)S(1)} %fusion.4), channel_id=1, source_target_pairs={{0,384},{64,192},{128,256},{192,64},{256,128},{320,448},{384,0},{4... | collective-permute-start | bytes 1032200 | tf_op jit(solution)/shard_map/ppermute | solution.py:259
  90.9 5.5 %collective-permute-done.7 = bf16[21,64,128]{2,1,0:T(8,128)(2,1)S(1)} collective-permute-done((bf16[21,64,128]{2,1,0:T(8,128)(2,1)S(1)}, bf16[21,64,128]{2,1,0:T(8,128)(2,1)S(1)}, u32[]{:S(2)}, u32[]{:S(2)}) %collective-permute-start.7) | collective-permute-done | bytes 344096 | tf_op jit(solution)/shard_map/ppermute | solution.py:259
  96.4 0.2 add_convert_fusion.2.own
  96.6 1.9 %collective-permute-start.8 = (bf16[21,64,128]{2,1,0:T(8,128)(2,1)S(1)}, bf16[21,64,128]{2,1,0:T(8,128)(2,1)S(1)}, u32[]{:S(2)}, u32[]{:S(2)}) collective-permute-start(bf16[21,64,128]{2,1,0:T(8,128)(2,1)S(1)} %add_convert_fusion.2.own), channel_id=1, source_target_pairs={{0,64},{64,0},{128,192},{192,128},{256,320},{320,256},{384,448},{4... | collective-permute-start | bytes 1032200 | tf_op jit(solution)/shard_map/ppermute | solution.py:250
  98.6 1.6 %collective-permute-done.8.other = bf16[21,64,128]{2,1,0:T(8,128)(2,1)S(1)} collective-permute-done((bf16[21,64,128]{2,1,0:T(8,128)(2,1)S(1)}, bf16[21,64,128]{2,1,0:T(8,128)(2,1)S(1)}, u32[]{:S(2)}, u32[]{:S(2)}) %collective-permute-start.8) | collective-permute-done | bytes 344096 | tf_op jit(solution)/shard_map/ppermute | solution.py:250
  100.2 5.2 %polish.1 = bf16[64,4,768]{2,1,0:T(4,128)(2,1)} custom-call(bf16[21,64,128]{2,1,0:T(8,128)(2,1)S(1)} %add_convert_fusion.2.own, bf16[21,64,128]{2,1,0:T(8,128)(2,1)S(1)} %collective-permute-done.8.other, bf16[256,768]{1,0:T(8,128)(2,1)S(1)} %get-tuple-element.23.rows_ref), custom_call_target="tpu_custom_call" | custom-call | tf_op jit(solution)/shard_map/polish/pallas_call | solution.py:232
  105.4 6.7 %all-to-all-start.1 = ((bf16[64,4,768]{2,1,0:T(4,128)(2,1)}), bf16[64,4,768]{2,1,0:T(4,128)(2,1)S(1)}, u32[]{:S(2)}, u32[]{:S(2)}) async-start(bf16[64,4,768]{2,1,0:T(4,128)(2,1)} %polish.1), calls=%async_computation.1 | async-start | bytes 786432 | tf_op jit(solution)/shard_map/all_to_all | solution.py:263
  112.1 1.7 %new_momentum.1 = f32[64,4,768]{2,1,0:T(4,128)} custom-call(s32[64]{0:T(128)S(1)} %copy-done.1, bf16[2,64,4,768]{3,2,1,0:T(4,128)(2,1)S(1)} %get-tuple-element.25.keep, bf16[2,64,4,768]{3,2,1,0:T(4,128)(2,1)S(1)} %collective-permute-done.swapped, bf16[64,4,768]{2,1,0:T(4,128)(2,1)S(1)} %collective-permute-done.2.first, ...), custom_call_target="tpu_custom_call" | custom-call | flops 1179648 | bytes 3145728 | tf_op jit(solution)/shard_map/new_momentum/pallas_call | solution.py:125
  113.8 24.8 %all-to-all-done.1 = bf16[64,4,768]{2,1,0:T(4,128)(2,1)S(1)} async-done(((bf16[64,4,768]{2,1,0:T(4,128)(2,1)}), bf16[64,4,768]{2,1,0:T(4,128)(2,1)S(1)}, u32[]{:S(2)}, u32[]{:S(2)}) %all-to-all-start.1) | async-done | bytes 393248 | tf_op jit(solution)/shard_map/all_to_all | solution.py:263
  138.6 0.7 copy.6
Async XLA Ops:
  0.6 27.8 %copy-start.1 = (s32[64]{0:T(128)S(1)}, s32[64]{0:T(128)}, u32[]{:S(2)}) copy-start(s32[64]{0:T(128)} %slots.2) | copy-start | bytes 772
  0.6 27.8 %copy-start = (f32[64,4,768]{2,1,0:T(4,128)S(1)}, f32[64,4,768]{2,1,0:T(4,128)}, u32[]{:S(2)}) copy-start(f32[64,4,768]{2,1,0:T(4,128)} %mom.2) | copy-start | bytes 2359300
  2.8 4.3 %collective-permute-start.1 = (bf16[2,64,4,768]{3,2,1,0:T(4,128)(2,1)S(1)}, bf16[2,64,4,768]{3,2,1,0:T(4,128)(2,1)S(1)}, u32[]{:S(2)}, u32[]{:S(2)}) collective-permute-start(bf16[2,64,4,768]{3,2,1,0:T(4,128)(2,1)S(1)} %get-tuple-element.19), channel_id=1, source_target_pairs={{0,64},{64,0},{128,192},{192,128},{256,320},{320,256},{384,448},{4... | collective-permute-start | bytes 2359304 | tf_op jit(solution)/shard_map/ppermute | solution.py:250
  4.7 8.7 %collective-permute-start = (bf16[2,64,4,768]{3,2,1,0:T(4,128)(2,1)S(1)}, bf16[2,64,4,768]{3,2,1,0:T(4,128)(2,1)S(1)}, u32[]{:S(2)}, u32[]{:S(2)}) collective-permute-start(bf16[2,64,4,768]{3,2,1,0:T(4,128)(2,1)S(1)} %get-tuple-element.17), channel_id=1, source_target_pairs={{0,64},{64,0},{128,192},{192,128},{256,320},{320,256},{384,448},{4... | collective-permute-start | bytes 2359304 | tf_op jit(solution)/shard_map/ppermute | solution.py:250
  7.5 9.7 %collective-permute-start.3 = (bf16[64,4,768]{2,1,0:T(4,128)(2,1)S(1)}, bf16[64,4,768]{2,1,0:T(4,128)(2,1)S(1)}, u32[]{:S(2)}, u32[]{:S(2)}) collective-permute-start(bf16[64,4,768]{2,1,0:T(4,128)(2,1)S(1)} %get-tuple-element.30), channel_id=1, source_target_pairs={{0,128},{64,448},{128,0},{192,320},{256,384},{320,192},{384,256},{... | collective-permute-start | bytes 1179656 | tf_op jit(solution)/shard_map/ppermute | solution.py:259
  11.0 11.4 %collective-permute-start.2 = (bf16[64,4,768]{2,1,0:T(4,128)(2,1)S(1)}, bf16[64,4,768]{2,1,0:T(4,128)(2,1)S(1)}, u32[]{:S(2)}, u32[]{:S(2)}) collective-permute-start(bf16[64,4,768]{2,1,0:T(4,128)(2,1)S(1)} %get-tuple-element.31), channel_id=1, source_target_pairs={{0,128},{64,448},{128,0},{192,320},{256,384},{320,192},{384,256},{... | collective-permute-start | bytes 1179656 | tf_op jit(solution)/shard_map/ppermute | solution.py:259
  17.5 10.9 %collective-permute-start.4 = (bf16[64,4,768]{2,1,0:T(4,128)(2,1)S(1)}, bf16[64,4,768]{2,1,0:T(4,128)(2,1)S(1)}, u32[]{:S(2)}, u32[]{:S(2)}) collective-permute-start(bf16[64,4,768]{2,1,0:T(4,128)(2,1)S(1)} %fusion), channel_id=1, source_target_pairs={{0,384},{64,192},{128,256},{192,64},{256,128},{320,448},{384,0},{4... | collective-permute-start | bytes 1179656 | tf_op jit(solution)/shard_map/ppermute | solution.py:259
  73.2 3.5 %collective-permute-start.5 = (bf16[21,64,128]{2,1,0:T(8,128)(2,1)S(1)}, bf16[21,64,128]{2,1,0:T(8,128)(2,1)S(1)}, u32[]{:S(2)}, u32[]{:S(2)}) collective-permute-start(bf16[21,64,128]{2,1,0:T(8,128)(2,1)S(1)} %get-tuple-element.22), channel_id=1, source_target_pairs={{0,64},{64,0},{128,192},{192,128},{256,320},{320,256},{384,448},{4... | collective-permute-start | bytes 1032200 | tf_op jit(solution)/shard_map/ppermute | solution.py:250
  76.8 9.1 %collective-permute-start.6 = (bf16[21,64,128]{2,1,0:T(8,128)(2,1)S(1)}, bf16[21,64,128]{2,1,0:T(8,128)(2,1)S(1)}, u32[]{:S(2)}, u32[]{:S(2)}) collective-permute-start(bf16[21,64,128]{2,1,0:T(8,128)(2,1)S(1)} %fusion.1), channel_id=1, source_target_pairs={{0,128},{64,448},{128,0},{192,320},{256,384},{320,192},{384,256},{... | collective-permute-start | bytes 1032200 | tf_op jit(solution)/shard_map/ppermute | solution.py:259
  86.1 10.4 %collective-permute-start.7 = (bf16[21,64,128]{2,1,0:T(8,128)(2,1)S(1)}, bf16[21,64,128]{2,1,0:T(8,128)(2,1)S(1)}, u32[]{:S(2)}, u32[]{:S(2)}) collective-permute-start(bf16[21,64,128]{2,1,0:T(8,128)(2,1)S(1)} %fusion.4), channel_id=1, source_target_pairs={{0,384},{64,192},{128,256},{192,64},{256,128},{320,448},{384,0},{4... | collective-permute-start | bytes 1032200 | tf_op jit(solution)/shard_map/ppermute | solution.py:259
  96.6 3.5 %collective-permute-start.8 = (bf16[21,64,128]{2,1,0:T(8,128)(2,1)S(1)}, bf16[21,64,128]{2,1,0:T(8,128)(2,1)S(1)}, u32[]{:S(2)}, u32[]{:S(2)}) collective-permute-start(bf16[21,64,128]{2,1,0:T(8,128)(2,1)S(1)} %add_convert_fusion.2.own), channel_id=1, source_target_pairs={{0,64},{64,0},{128,192},{192,128},{256,320},{320,256},{384,448},{4... | collective-permute-start | bytes 1032200 | tf_op jit(solution)/shard_map/ppermute | solution.py:250
  105.4 33.2 %all-to-all-start.1 = ((bf16[64,4,768]{2,1,0:T(4,128)(2,1)}), bf16[64,4,768]{2,1,0:T(4,128)(2,1)S(1)}, u32[]{:S(2)}, u32[]{:S(2)}) async-start(bf16[64,4,768]{2,1,0:T(4,128)(2,1)} %polish.1), calls=%async_computation.1 | async-start | bytes 786432 | tf_op jit(solution)/shard_map/all_to_all | solution.py:263

commit v7 on v6

--- a/solution.py
+++ b/solution.py
@@ -9,6 +9,7 @@
 from jax.sharding import PartitionSpec as P
 
 NY = 4
+PARTS = 2
 COEF_A = 3.4445
 COEF_B = -4.775
 COEF_C = 2.0315
@@ -39,7 +40,9 @@
     return y, c, near, far, lax.rem(y + 2, NY)
 
 
-def split_kernel(g_hbm, send_a, send_b, keep_a, keep_b, raw, wide, sems):
+def split_kernel(g_hbm, *refs):
+    sends, keeps = refs[:PARTS], refs[PARTS : 2 * PARTS]
+    raw, wide, sems = refs[2 * PARTS :]
     y, c, near, far, across = place_of()
     parts = sems.shape[0]
     mb = raw.shape[0] // parts
@@ -55,18 +58,16 @@
     def emit(i, low):
         here = pl.ds(i * mb, mb)
 
-        def rows(yy, core):
+        def fill(out, role, yy, core):
             both = wide[:, pl.ds(pl.multiple_of(8 * yy, 8), 8), :]
-            return both[:, 4 * core : 4 * core + 4, :].astype(BF)
-
-        send_a[0, here] = rows(across, 1 - low)
-        send_a[1, here] = rows(far, 1 - low)
-        send_b[0, here] = rows(y, 1 - low)
-        send_b[1, here] = rows(near, 1 - low)
-        keep_a[0, here] = rows(across, low)
-        keep_a[1, here] = rows(near, low)
-        keep_b[0, here] = rows(y, low)
-        keep_b[1, here] = rows(far, low)
+            chosen = both[:, 4 * core : 4 * core + 4, :].astype(BF)
+            width = chosen.shape[2] // PARTS
+            for p in range(PARTS):
+                out[p][role, here] = chosen[:, :, width * p : width * p + width]
+
+        for role, (mine, theirs) in enumerate(((y, y), (far, near), (across, across), (near, far))):
+            fill(keeps, role, mine, low)
+            fill(sends, role, theirs, 1 - low)
 
     for i in range(parts):
         fetch(i).wait()
@@ -77,12 +78,12 @@
 
 def split_rows(grads, parts):
     _, m, rows, cols = grads.shape
-    two = sds((2, m, 4, cols), BF)
+    four = sds((4, m, 4, cols // PARTS), BF)
     return pl.pallas_call(
         split_kernel,
         in_specs=[pl.BlockSpec(memory_space=pl.ANY)],
-        out_specs=whole(4),
-        out_shape=[two] * 4,
+        out_specs=whole(2 * PARTS),
+        out_shape=[four] * (2 * PARTS),
         scratch_shapes=[
             pltpu.VMEM((m, rows, cols), BF),
             pltpu.VMEM((m // parts, rows, cols), F32),
@@ -95,42 +96,48 @@
 
 def gradient_at(j, keep, swapped, first, second):
     return (keep[0, j].astype(F32) + swapped[0, j].astype(F32)) + (
-        first[j].astype(F32) + second[j].astype(F32)
+        first[1, j].astype(F32) + second[j].astype(F32)
     )
 
 
-def nesterov_kernel(slots, keep, swapped, first, second, mom, nesterov):
+def nesterov_kernel(part, slots, mom, keep, swapped, first, second, nesterov):
+    m, _, width = nesterov.shape
+
     def step(j, carry):
         mat = slots[j]
         gradient = gradient_at(j, keep, swapped, first, second)
-        nesterov[mat] = (gradient + DECAY * (DECAY * mom[mat] + gradient)).astype(BF)
+        old = mom[mat, :, part * width : part * width + width]
+        nesterov[mat] = (gradient + DECAY * (DECAY * old + gradient)).astype(BF)
         return carry
 
-    m = mom.shape[0]
     lax.fori_loop(0, m, step, 0, unroll=min(8, m))
 
 
-def momentum_kernel(slots, keep, swapped, first, second, mom, new_mom):
+def momentum_kernel(slots, mom, *refs):
+    ins, new_mom = refs[:-1], refs[-1]
+    m, _, cols = new_mom.shape
+    width = cols // PARTS
+
     def step(j, carry):
         mat = slots[j]
-        new_mom[mat] = DECAY * mom[mat] + gradient_at(j, keep, swapped, first, second)
+        for p in range(PARTS):
+            here = slice(p * width, p * width + width)
+            new_mom[mat, :, here] = DECAY * mom[mat, :, here] + gradient_at(j, *ins[4 * p : 4 * p + 4])
         return carry
 
-    m = mom.shape[0]
     lax.fori_loop(0, m, step, 0, unroll=min(8, m))
 
 
-def momentum_call(kernel, dtype, name, *args):
-    mom = args[-1]
+def momentum_call(kernel, out, name, slots, mom, *args):
     return pl.pallas_call(
         kernel,
-        in_specs=[pl.BlockSpec(memory_space=SMEM)] + whole(5),
+        in_specs=[pl.BlockSpec(memory_space=SMEM)] + whole(1 + len(args)),
         out_specs=whole(1)[0],
-        out_shape=sds(mom.shape, dtype),
+        out_shape=out,
         compiler_params=params(),
         cost_estimate=pl.CostEstimate(flops=6 * mom.size, bytes_accessed=16 * mom.size, transcendentals=0),
         name=name,
-    )(*args)
+    )(slots, mom, *args)
 
 
 def blocks_of(cols):
@@ -138,12 +145,15 @@
     return [(i, j) for i in range(n) for j in range(i, n)]
 
 
-def gram_kernel(a_ref, rows_ref, send, keep, slabs):
+def gram_kernel(*refs):
+    ins, (rows_ref, send, keep, slabs) = refs[:PARTS], refs[PARTS:]
     c = lax.rem(lax.axis_index("dp"), 2)
-    count, _, cols = a_ref.shape
-    for g in range(count // 4):
-        four = [a_ref[4 * g + i].astype(F32) for i in range(4)]
-        rows_ref[16 * g : 16 * g + 16, :] = jnp.concatenate(four, axis=0).astype(BF)
+    cols = rows_ref.shape[1]
+    count, _, width = ins[0].shape
+    for p, a_ref in enumerate(ins):
+        for g in range(count // 4):
+            four = [a_ref[4 * g + i].astype(F32) for i in range(4)]
+            rows_ref[16 * g : 16 * g + 16, p * width : p * width + width] = jnp.concatenate(four, axis=0).astype(BF)
     n = cols // 128
     b = 0
     for i in range(n):
@@ -162,12 +172,13 @@
     keep[...] = slabs[c]
 
 
-def partial_gram(a):
-    count, _, cols = a.shape
+def partial_gram(parts):
+    count, _, width = parts[0].shape
+    cols = PARTS * width
     nb = len(blocks_of(cols))
     return pl.pallas_call(
         gram_kernel,
-        in_specs=whole(1),
+        in_specs=whole(PARTS),
         out_specs=whole(3),
         out_shape=[
             sds((4 * count, cols), BF),
@@ -177,7 +188,7 @@
         scratch_shapes=[pltpu.VMEM((2, nb, 64, 128), F32)],
         compiler_params=params(),
         name="partial_gram",
-    )(a)
+    )(*parts)
 
 
 def polish_kernel(scale, own, other, rows_ref, out, slabs, level, low, poly, high):
@@ -267,21 +278,29 @@
     m = grads.shape[1]
     cols = grads.shape[3]
 
-    send_a, send_b, keep_a, keep_b = split_rows(grads, 8)
-    swapped_a = core_swap(send_a)
-    swapped_b = core_swap(send_b)
-    first_far = y_swap((keep_a[0].astype(F32) + swapped_a[0].astype(F32)).astype(BF), 0)
-    first_own = y_swap((keep_a[1].astype(F32) + swapped_a[1].astype(F32)).astype(BF), 0)
-    far = (keep_b[1].astype(F32) + swapped_b[1].astype(F32)) + first_far.astype(F32)
-    second = y_swap(far.astype(BF), 1)
-    parts = (slot_matrix, keep_b, swapped_b, first_own, second, momentum)
-    nesterov = momentum_call(nesterov_kernel, BF, "nesterov", *parts)
-
-    mine = exchange(nesterov)
-
-    rows, gram_send, gram_keep = partial_gram(mine)
-    gram_keep, parts = lax.optimization_barrier((gram_keep, parts))
-    new_momentum = momentum_call(momentum_kernel, F32, "new_momentum", *parts)
+    pieces = split_rows(grads, 8)
+    terms, arrived = [], []
+    swaps = [core_swap(v) for v in pieces[:PARTS]]
+    for p, (keep, swapped) in enumerate(zip(pieces[PARTS:], swaps)):
+        first = y_swap((keep[2:].astype(F32) + swapped[2:].astype(F32)).astype(BF), 0)
+        far = (keep[1].astype(F32) + swapped[1].astype(F32)) + first[0].astype(F32)
+        second = y_swap(far.astype(BF), 1)
+        terms += [keep, swapped, first, second]
+        nesterov = momentum_call(
+            functools.partial(nesterov_kernel, p),
+            sds((m, 4, cols // PARTS), BF),
+            "nesterov",
+            slot_matrix,
+            momentum,
+            *terms[-4:],
+        )
+        arrived.append(exchange(nesterov))
+
+    rows, gram_send, gram_keep = partial_gram(arrived)
+    gram_keep, terms = lax.optimization_barrier((gram_keep, terms))
+    new_momentum = momentum_call(
+        momentum_kernel, sds((m, 4, cols), F32), "new_momentum", slot_matrix, momentum, *terms
+    )
     gram = gram_keep + core_swap(gram_send).astype(F32)
     gram = gram + y_swap(gram.astype(BF), 0).astype(F32)
     gram = gram + y_swap(gram.astype(BF), 1).astype(F32)

time: 140 us -> 161 us (1.15)
  starting transfers between devices: 33.2 us -> 56.7 us
  blocking collectives: 43.1 us -> 26.6 us
  local copies, waits for them, and re-layouts: 0.75 us -> 10.3 us
  Pallas kernels: 10.6 us -> 12.6 us
  other arithmetic: 1.14 us -> 2.91 us
    all_to_all x1 -> x2, starting transfers between devices: 6.66 us -> 25.7 us  [exchange(): return lax.all_to_all(v, 'fsdp', split_axis=0, concat_axis=0, tiled=True)]
    all_to_all x1, blocking collectives: 43.1 us -> 26.6 us  [exchange(): return lax.all_to_all(v, 'fsdp', split_axis=0, concat_axis=0, tiled=True)]
    unnamed x5 -> x25, local copies, waits for them, and re-layouts: 0.75 us -> 10.3 us
    ppermute x5 -> x6, starting transfers between devices: 18.3 us -> 22.8 us  [y_swap(): return lax.ppermute(v, 'dp', perm)]
    pallas_call x2 -> x3, Pallas kernels: 2.68 us -> 4.45 us  [momentum_call(): pl.pallas_call(kernel, in_specs=[pl.BlockSpec(memory_space=SMEM)] + whole...]
    all_to_all x1 -> x2, waiting for transfers between devices: 24.8 us -> 25.2 us  [exchange(): return lax.all_to_all(v, 'fsdp', split_axis=0, concat_axis=0, tiled=True)]
    ppermute x5 -> x6, waiting for transfers between devices: 21.6 us -> 22 us  [y_swap(): return lax.ppermute(v, 'dp', perm)]
  transfers between devices with their start and end apart: 10 -> 12, of which waited for: 7 -> 8; matrix products, arithmetic and copies ran while one was open for 1% -> 2% of each run, Pallas kernels for 1% -> 3%
where the time goes in v7:
time: 161 us
  starting transfers between devices  56.7 us (35%)
  waiting for transfers between devices  50.5 us (31%)
  blocking collectives  26.6 us (17%)
  Pallas kernels  12.6 us (8%)
  local copies, waits for them, and re-layouts  10.3 us (6%)
  other arithmetic  2.91 us (2%)
    all_to_all x1, blocking collectives, exchange(): return lax.all_to_all(v, 'fsdp', split_axis=0, concat_axis=0, tiled=True)  26.6 us
    all_to_all x2, starting transfers between devices, exchange(): return lax.all_to_all(v, 'fsdp', split_axis=0, concat_axis=0, tiled=True)  25.7 us
    all_to_all x2, waiting for transfers between devices, exchange(): return lax.all_to_all(v, 'fsdp', split_axis=0, concat_axis=0, tiled=True)  25.2 us
    ppermute x6, starting transfers between devices, y_swap(): return lax.ppermute(v, 'dp', perm)  22.8 us
    ppermute x6, waiting for transfers between devices, y_swap(): return lax.ppermute(v, 'dp', perm)  22 us
    unnamed x25, local copies, waits for them, and re-layouts  10.3 us
    ppermute x4, starting transfers between devices, core_swap(): return lax.ppermute(v, 'dp', [(i, i ^ 1) for i in range(2 * NY)])  8.17 us
    pallas_call x1, Pallas kernels, polish(): pl.pallas_call(functools.partial(polish_kernel, scale), in_specs=whole(3)...  4.48 us
  transfers between devices with their start and end apart: 12, of which 8 were waited for; matrix products, arithmetic and copies ran while one was open for 2% of the time, Pallas kernels for 3%

profile of v7, /device:TPU:6, one launch (start us, length us, event | category | flops | bytes accessed | tf_op | source)
XLA Modules:
  0.0 160.6 jit_solution(6590917458521618116)
XLA Ops:
  0.6 2.2 %split_rows.1 = (bf16[4,64,4,384]{3,2,1,0:T(4,128)(2,1)S(1)}, bf16[4,64,4,384]{3,2,1,0:T(4,128)(2,1)S(1)}, bf16[4,64,4,384]{3,2,1,0:T(4,128)(2,1)S(1)}, bf16[4,64,4,384]{3,2,1,0:T(4,128)(2,1)S(1)}) custom-call(bf16[1,64,32,768]{3,2,1,0:T(8,128)(2,1)} %g_hbm.1), custom_call_target="tpu_custom_call" | custom-call | tf_op jit(solution)/shard_map/split_rows/pallas_call | solution.py:82
  2.8 1.9 %collective-permute-start = (bf16[4,64,4,384]{3,2,1,0:T(4,128)(2,1)S(1)}, bf16[4,64,4,384]{3,2,1,0:T(4,128)(2,1)S(1)}, u32[]{:S(2)}, u32[]{:S(2)}) collective-permute-start(bf16[4,64,4,384]{3,2,1,0:T(4,128)(2,1)S(1)} %get-tuple-element.19), channel_id=1, source_target_pairs={{0,64},{64,0},{128,192},{192,128},{256,320},{320,256},{384,448},{4... | collective-permute-start | bytes 2359304 | tf_op jit(solution)/shard_map/ppermute | solution.py:261
  4.7 2.4 %collective-permute-start.3 = (bf16[4,64,4,384]{3,2,1,0:T(4,128)(2,1)S(1)}, bf16[4,64,4,384]{3,2,1,0:T(4,128)(2,1)S(1)}, u32[]{:S(2)}, u32[]{:S(2)}) collective-permute-start(bf16[4,64,4,384]{3,2,1,0:T(4,128)(2,1)S(1)} %get-tuple-element.21), channel_id=1, source_target_pairs={{0,64},{64,0},{128,192},{192,128},{256,320},{320,256},{384,448},{4... | collective-permute-start | bytes 2359304 | tf_op jit(solution)/shard_map/ppermute | solution.py:261
  7.2 0.2 add_convert_fusion.1
  7.4 3.5 %collective-permute-start.1 = (bf16[2,64,4,384]{3,2,1,0:T(4,128)(2,1)S(1)}, bf16[2,64,4,384]{3,2,1,0:T(4,128)(2,1)S(1)}, u32[]{:S(2)}, u32[]{:S(2)}) collective-permute-start(bf16[2,64,4,384]{3,2,1,0:T(4,128)(2,1)S(1)} %add_convert_fusion.1), channel_id=1, source_target_pairs={{0,128},{64,448},{128,0},{192,320},{256,384},{320,192},{384,256},{... | collective-permute-start | bytes 1179656 | tf_op jit(solution)/shard_map/ppermute | solution.py:270
  10.9 6.2 %collective-permute-done.1.first.refs_2_ = bf16[2,64,4,384]{3,2,1,0:T(4,128)(2,1)S(1)} collective-permute-done((bf16[2,64,4,384]{3,2,1,0:T(4,128)(2,1)S(1)}, bf16[2,64,4,384]{3,2,1,0:T(4,128)(2,1)S(1)}, u32[]{:S(2)}, u32[]{:S(2)}) %collective-permute-start.1) | collective-permute-done | bytes 393248 | tf_op jit(solution)/shard_map/ppermute | solution.py:270
  17.1 0.2 fusion.2
  17.2 4.9 %collective-permute-start.2 = (bf16[64,4,384]{2,1,0:T(4,128)(2,1)S(1)}, bf16[64,4,384]{2,1,0:T(4,128)(2,1)S(1)}, u32[]{:S(2)}, u32[]{:S(2)}) collective-permute-start(bf16[64,4,384]{2,1,0:T(4,128)(2,1)S(1)} %fusion.2), channel_id=1, source_target_pairs={{0,384},{64,192},{128,256},{192,64},{256,128},{320,448},{384,0},{4... | collective-permute-start | bytes 589832 | tf_op jit(solution)/shard_map/ppermute | solution.py:270
  22.2 0.0 copy-start.1
  22.2 0.9 copy-done.1
  23.0 1.0 add_convert_fusion
  24.0 2.0 %collective-permute-start.4 = (bf16[2,64,4,384]{3,2,1,0:T(4,128)(2,1)}, bf16[2,64,4,384]{3,2,1,0:T(4,128)(2,1)}, u32[]{:S(2)}, u32[]{:S(2)}) collective-permute-start(bf16[2,64,4,384]{3,2,1,0:T(4,128)(2,1)} %add_convert_fusion), channel_id=1, source_target_pairs={{0,128},{64,448},{128,0},{192,320},{256,384},{320,192},{384,256},{... | collective-permute-start | bytes 1179656 | tf_op jit(solution)/shard_map/ppermute | solution.py:270
  26.1 0.9 nesterov.2
  26.9 0.7 copy-done.5
  27.6 0.7 copy-done.9
  28.3 19.0 %all-to-all-start = ((bf16[64,4,384]{2,1,0:T(4,128)(2,1)}), bf16[64,4,384]{2,1,0:T(4,128)(2,1)}, u32[]{:S(2)}, u32[]{:S(2)}) async-start(bf16[64,4,384]{2,1,0:T(4,128)(2,1)} %copy-done.9), calls=%async_computation | async-start | bytes 393216 | tf_op jit(solution)/shard_map/all_to_all | solution.py:274
  47.2 1.2 fusion.3
  48.4 4.9 %collective-permute-start.5 = (bf16[64,4,384]{2,1,0:T(4,128)(2,1)S(1)}, bf16[64,4,384]{2,1,0:T(4,128)(2,1)S(1)}, u32[]{:S(2)}, u32[]{:S(2)}) collective-permute-start(bf16[64,4,384]{2,1,0:T(4,128)(2,1)S(1)} %fusion.3), channel_id=1, source_target_pairs={{0,384},{64,192},{128,256},{192,64},{256,128},{320,448},{384,0},{4... | collective-permute-start | bytes 589832 | tf_op jit(solution)/shard_map/ppermute | solution.py:270
  53.3 3.9 %collective-permute-done.5.second.refs_7_ = bf16[64,4,384]{2,1,0:T(4,128)(2,1)S(1)} collective-permute-done((bf16[64,4,384]{2,1,0:T(4,128)(2,1)S(1)}, bf16[64,4,384]{2,1,0:T(4,128)(2,1)S(1)}, u32[]{:S(2)}, u32[]{:S(2)}) %collective-permute-start.5) | collective-permute-done | bytes 196640 | tf_op jit(solution)/shard_map/ppermute | solution.py:270
  57.2 1.1 copy-done.2
  58.3 1.3 nesterov.3
  59.7 0.7 copy-done.7
  60.3 0.7 copy-done.10
  61.0 4.1 %all-to-all-done.refs_0_ = bf16[64,4,384]{2,1,0:T(4,128)(2,1)} async-done(((bf16[64,4,384]{2,1,0:T(4,128)(2,1)}), bf16[64,4,384]{2,1,0:T(4,128)(2,1)}, u32[]{:S(2)}, u32[]{:S(2)}) %all-to-all-start) | async-done | bytes 196640 | tf_op jit(solution)/shard_map/all_to_all | solution.py:274
  65.1 26.6 %all_to_all.15.refs_1_ = bf16[64,4,384]{2,1,0:T(4,128)(2,1)S(1)} all-to-all(bf16[64,4,384]{2,1,0:T(4,128)(2,1)} %copy-done.10), channel_id=1, replica_groups=mesh['dp'=8,'fsdp'=64] {'fsdp'}, dimensions={0} | all-to-all | bytes 393216 | tf_op jit(solution)/shard_map/all_to_all | solution.py:274
  91.7 1.6 partial_gram.1
  93.3 1.9 %collective-permute-start.6 = (bf16[21,64,128]{2,1,0:T(8,128)(2,1)S(1)}, bf16[21,64,128]{2,1,0:T(8,128)(2,1)S(1)}, u32[]{:S(2)}, u32[]{:S(2)}) collective-permute-start(bf16[21,64,128]{2,1,0:T(8,128)(2,1)S(1)} %get-tuple-element.24), channel_id=1, source_target_pairs={{0,64},{64,0},{128,192},{192,128},{256,320},{320,256},{384,448},{4... | collective-permute-start | bytes 1032200 | tf_op jit(solution)/shard_map/ppermute | solution.py:261
  95.2 1.6 %collective-permute-done.6 = bf16[21,64,128]{2,1,0:T(8,128)(2,1)S(1)} collective-permute-done((bf16[21,64,128]{2,1,0:T(8,128)(2,1)S(1)}, bf16[21,64,128]{2,1,0:T(8,128)(2,1)S(1)}, u32[]{:S(2)}, u32[]{:S(2)}) %collective-permute-start.6) | collective-permute-done | bytes 344096 | tf_op jit(solution)/shard_map/ppermute | solution.py:261
  96.8 0.1 fusion
  96.9 3.0 %collective-permute-start.7 = (bf16[21,64,128]{2,1,0:T(8,128)(2,1)S(1)}, bf16[21,64,128]{2,1,0:T(8,128)(2,1)S(1)}, u32[]{:S(2)}, u32[]{:S(2)}) collective-permute-start(bf16[21,64,128]{2,1,0:T(8,128)(2,1)S(1)} %fusion), channel_id=1, source_target_pairs={{0,128},{64,448},{128,0},{192,320},{256,384},{320,192},{384,256},{... | collective-permute-start | bytes 1032200 | tf_op jit(solution)/shard_map/ppermute | solution.py:270
  99.9 6.2 %collective-permute-done.7 = bf16[21,64,128]{2,1,0:T(8,128)(2,1)S(1)} collective-permute-done((bf16[21,64,128]{2,1,0:T(8,128)(2,1)S(1)}, bf16[21,64,128]{2,1,0:T(8,128)(2,1)S(1)}, u32[]{:S(2)}, u32[]{:S(2)}) %collective-permute-start.7) | collective-permute-done | bytes 344096 | tf_op jit(solution)/shard_map/ppermute | solution.py:270
  106.1 0.1 fusion.1
  106.2 4.6 %collective-permute-start.8 = (bf16[21,64,128]{2,1,0:T(8,128)(2,1)S(1)}, bf16[21,64,128]{2,1,0:T(8,128)(2,1)S(1)}, u32[]{:S(2)}, u32[]{:S(2)}) collective-permute-start(bf16[21,64,128]{2,1,0:T(8,128)(2,1)S(1)} %fusion.1), channel_id=1, source_target_pairs={{0,384},{64,192},{128,256},{192,64},{256,128},{320,448},{384,0},{4... | collective-permute-start | bytes 1032200 | tf_op jit(solution)/shard_map/ppermute | solution.py:270
  110.8 5.8 %collective-permute-done.8 = bf16[21,64,128]{2,1,0:T(8,128)(2,1)S(1)} collective-permute-done((bf16[21,64,128]{2,1,0:T(8,128)(2,1)S(1)}, bf16[21,64,128]{2,1,0:T(8,128)(2,1)S(1)}, u32[]{:S(2)}, u32[]{:S(2)}) %collective-permute-start.8) | collective-permute-done | bytes 344096 | tf_op jit(solution)/shard_map/ppermute | solution.py:270
  116.6 0.2 add_convert_fusion.2.own
  116.8 1.9 %collective-permute-start.9 = (bf16[21,64,128]{2,1,0:T(8,128)(2,1)S(1)}, bf16[21,64,128]{2,1,0:T(8,128)(2,1)S(1)}, u32[]{:S(2)}, u32[]{:S(2)}) collective-permute-start(bf16[21,64,128]{2,1,0:T(8,128)(2,1)S(1)} %add_convert_fusion.2.own), channel_id=1, source_target_pairs={{0,64},{64,0},{128,192},{192,128},{256,320},{320,256},{384,448},{4... | collective-permute-start | bytes 1032200 | tf_op jit(solution)/shard_map/ppermute | solution.py:261
  118.7 1.6 %collective-permute-done.9.other = bf16[21,64,128]{2,1,0:T(8,128)(2,1)S(1)} collective-permute-done((bf16[21,64,128]{2,1,0:T(8,128)(2,1)S(1)}, bf16[21,64,128]{2,1,0:T(8,128)(2,1)S(1)}, u32[]{:S(2)}, u32[]{:S(2)}) %collective-permute-start.9) | collective-permute-done | bytes 344096 | tf_op jit(solution)/shard_map/ppermute | solution.py:261
  120.3 4.5 %polish.1 = bf16[64,4,768]{2,1,0:T(4,128)(2,1)S(1)} custom-call(bf16[21,64,128]{2,1,0:T(8,128)(2,1)S(1)} %add_convert_fusion.2.own, bf16[21,64,128]{2,1,0:T(8,128)(2,1)S(1)} %collective-permute-done.9.other, bf16[256,768]{1,0:T(8,128)(2,1)S(1)} %get-tuple-element.25.rows_ref), custom_call_target="tpu_custom_call" | custom-call | tf_op jit(solution)/shard_map/polish/pallas_call | solution.py:243
  124.8 0.0 copy-start.4
  124.8 0.7 copy-done.4
  125.5 6.7 %all-to-all-start.2 = ((bf16[64,4,768]{2,1,0:T(4,128)(2,1)}), bf16[64,4,768]{2,1,0:T(4,128)(2,1)}, u32[]{:S(2)}, u32[]{:S(2)}) async-start(bf16[64,4,768]{2,1,0:T(4,128)(2,1)} %copy-done.4), calls=%async_computation.2 | async-start | bytes 786432 | tf_op jit(solution)/shard_map/all_to_all | solution.py:274
  132.3 0.0 copy-start.3
  132.3 1.1 copy-done.3
  133.4 0.9 copy-done.6
  134.3 0.9 copy-done.8
  135.2 2.3 %new_momentum.1 = f32[64,4,768]{2,1,0:T(4,128)} custom-call(s32[64]{0:T(128)S(1)} %copy-done.11, f32[64,4,768]{2,1,0:T(4,128)S(1)} %copy-done, bf16[4,64,4,384]{3,2,1,0:T(4,128)(2,1)S(1)} %get-tuple-element.26.keep.refs_0_, bf16[4,64,4,384]{3,2,1,0:T(4,128)(2,1)S(1)} %collective-permute-done.swapped.refs_1_, ...), custom_call_target="tpu_custom_call" | custom-call | flops 1179648 | bytes 3145728 | tf_op jit(solution)/shard_map/new_momentum/pallas_call | solution.py:132
  137.5 21.2 %all-to-all-done.2 = bf16[64,4,768]{2,1,0:T(4,128)(2,1)} async-done(((bf16[64,4,768]{2,1,0:T(4,128)(2,1)}), bf16[64,4,768]{2,1,0:T(4,128)(2,1)}, u32[]{:S(2)}, u32[]{:S(2)}) %all-to-all-start.2) | async-done | bytes 393248 | tf_op jit(solution)/shard_map/all_to_all | solution.py:274
  158.7 1.9 %copy.6 = bf16[64,4,768]{2,1,0:T(4,128)(2,1)} copy(bf16[64,4,768]{2,1,0:T(4,128)(2,1)} %all-to-all-done.2) | data formatting | bytes 786432
  (15 shorter events, 0.0 us)
Async XLA Ops:
  0.6 25.4 %copy-start.11 = (s32[64]{0:T(128)S(1)}, s32[64]{0:T(128)}, u32[]{:S(2)}) copy-start(s32[64]{0:T(128)} %slots.5) | copy-start | bytes 772
  0.6 25.4 %copy-start = (f32[64,4,768]{2,1,0:T(4,128)S(1)}, f32[64,4,768]{2,1,0:T(4,128)}, u32[]{:S(2)}) copy-start(f32[64,4,768]{2,1,0:T(4,128)} %mom.5) | copy-start | bytes 2359300
  2.8 4.3 %collective-permute-start = (bf16[4,64,4,384]{3,2,1,0:T(4,128)(2,1)S(1)}, bf16[4,64,4,384]{3,2,1,0:T(4,128)(2,1)S(1)}, u32[]{:S(2)}, u32[]{:S(2)}) collective-permute-start(bf16[4,64,4,384]{3,2,1,0:T(4,128)(2,1)S(1)} %get-tuple-element.19), channel_id=1, source_target_pairs={{0,64},{64,0},{128,192},{192,128},{256,320},{320,256},{384,448},{4... | collective-permute-start | bytes 2359304 | tf_op jit(solution)/shard_map/ppermute | solution.py:261
  4.7 17.4 %collective-permute-start.3 = (bf16[4,64,4,384]{3,2,1,0:T(4,128)(2,1)S(1)}, bf16[4,64,4,384]{3,2,1,0:T(4,128)(2,1)S(1)}, u32[]{:S(2)}, u32[]{:S(2)}) collective-permute-start(bf16[4,64,4,384]{3,2,1,0:T(4,128)(2,1)S(1)} %get-tuple-element.21), channel_id=1, source_target_pairs={{0,64},{64,0},{128,192},{192,128},{256,320},{320,256},{384,448},{4... | collective-permute-start | bytes 2359304 | tf_op jit(solution)/shard_map/ppermute | solution.py:261
  7.4 9.7 %collective-permute-start.1 = (bf16[2,64,4,384]{3,2,1,0:T(4,128)(2,1)S(1)}, bf16[2,64,4,384]{3,2,1,0:T(4,128)(2,1)S(1)}, u32[]{:S(2)}, u32[]{:S(2)}) collective-permute-start(bf16[2,64,4,384]{3,2,1,0:T(4,128)(2,1)S(1)} %add_convert_fusion.1), channel_id=1, source_target_pairs={{0,128},{64,448},{128,0},{192,320},{256,384},{320,192},{384,256},{... | collective-permute-start | bytes 1179656 | tf_op jit(solution)/shard_map/ppermute | solution.py:270
  17.2 8.8 %collective-permute-start.2 = (bf16[64,4,384]{2,1,0:T(4,128)(2,1)S(1)}, bf16[64,4,384]{2,1,0:T(4,128)(2,1)S(1)}, u32[]{:S(2)}, u32[]{:S(2)}) collective-permute-start(bf16[64,4,384]{2,1,0:T(4,128)(2,1)S(1)} %fusion.2), channel_id=1, source_target_pairs={{0,384},{64,192},{128,256},{192,64},{256,128},{320,448},{384,0},{4... | collective-permute-start | bytes 589832 | tf_op jit(solution)/shard_map/ppermute | solution.py:270
  22.2 0.9 copy-start.1
  24.0 23.3 %collective-permute-start.4 = (bf16[2,64,4,384]{3,2,1,0:T(4,128)(2,1)}, bf16[2,64,4,384]{3,2,1,0:T(4,128)(2,1)}, u32[]{:S(2)}, u32[]{:S(2)}) collective-permute-start(bf16[2,64,4,384]{3,2,1,0:T(4,128)(2,1)} %add_convert_fusion), channel_id=1, source_target_pairs={{0,128},{64,448},{128,0},{192,320},{256,384},{320,192},{384,256},{... | collective-permute-start | bytes 1179656 | tf_op jit(solution)/shard_map/ppermute | solution.py:270
  26.9 0.7 copy-start.5
  27.6 0.7 copy-start.9
  28.3 36.8 %all-to-all-start = ((bf16[64,4,384]{2,1,0:T(4,128)(2,1)}), bf16[64,4,384]{2,1,0:T(4,128)(2,1)}, u32[]{:S(2)}, u32[]{:S(2)}) async-start(bf16[64,4,384]{2,1,0:T(4,128)(2,1)} %copy-done.9), calls=%async_computation | async-start | bytes 393216 | tf_op jit(solution)/shard_map/all_to_all | solution.py:274
  48.4 8.8 %collective-permute-start.5 = (bf16[64,4,384]{2,1,0:T(4,128)(2,1)S(1)}, bf16[64,4,384]{2,1,0:T(4,128)(2,1)S(1)}, u32[]{:S(2)}, u32[]{:S(2)}) collective-permute-start(bf16[64,4,384]{2,1,0:T(4,128)(2,1)S(1)} %fusion.3), channel_id=1, source_target_pairs={{0,384},{64,192},{128,256},{192,64},{256,128},{320,448},{384,0},{4... | collective-permute-start | bytes 589832 | tf_op jit(solution)/shard_map/ppermute | solution.py:270
  57.2 1.1 copy-start.2
  59.7 0.7 copy-start.7
  60.3 0.7 copy-start.10
  93.3 3.5 %collective-permute-start.6 = (bf16[21,64,128]{2,1,0:T(8,128)(2,1)S(1)}, bf16[21,64,128]{2,1,0:T(8,128)(2,1)S(1)}, u32[]{:S(2)}, u32[]{:S(2)}) collective-permute-start(bf16[21,64,128]{2,1,0:T(8,128)(2,1)S(1)} %get-tuple-element.24), channel_id=1, source_target_pairs={{0,64},{64,0},{128,192},{192,128},{256,320},{320,256},{384,448},{4... | collective-permute-start | bytes 1032200 | tf_op jit(solution)/shard_map/ppermute | solution.py:261
  96.9 9.1 %collective-permute-start.7 = (bf16[21,64,128]{2,1,0:T(8,128)(2,1)S(1)}, bf16[21,64,128]{2,1,0:T(8,128)(2,1)S(1)}, u32[]{:S(2)}, u32[]{:S(2)}) collective-permute-start(bf16[21,64,128]{2,1,0:T(8,128)(2,1)S(1)} %fusion), channel_id=1, source_target_pairs={{0,128},{64,448},{128,0},{192,320},{256,384},{320,192},{384,256},{... | collective-permute-start | bytes 1032200 | tf_op jit(solution)/shard_map/ppermute | solution.py:270
  106.2 10.4 %collective-permute-start.8 = (bf16[21,64,128]{2,1,0:T(8,128)(2,1)S(1)}, bf16[21,64,128]{2,1,0:T(8,128)(2,1)S(1)}, u32[]{:S(2)}, u32[]{:S(2)}) collective-permute-start(bf16[21,64,128]{2,1,0:T(8,128)(2,1)S(1)} %fusion.1), channel_id=1, source_target_pairs={{0,384},{64,192},{128,256},{192,64},{256,128},{320,448},{384,0},{4... | collective-permute-start | bytes 1032200 | tf_op jit(solution)/shard_map/ppermute | solution.py:270
  116.8 3.5 %collective-permute-start.9 = (bf16[21,64,128]{2,1,0:T(8,128)(2,1)S(1)}, bf16[21,64,128]{2,1,0:T(8,128)(2,1)S(1)}, u32[]{:S(2)}, u32[]{:S(2)}) collective-permute-start(bf16[21,64,128]{2,1,0:T(8,128)(2,1)S(1)} %add_convert_fusion.2.own), channel_id=1, source_target_pairs={{0,64},{64,0},{128,192},{192,128},{256,320},{320,256},{384,448},{4... | collective-permute-start | bytes 1032200 | tf_op jit(solution)/shard_map/ppermute | solution.py:261
  124.8 0.7 copy-start.4
  125.5 33.2 %all-to-all-start.2 = ((bf16[64,4,768]{2,1,0:T(4,128)(2,1)}), bf16[64,4,768]{2,1,0:T(4,128)(2,1)}, u32[]{:S(2)}, u32[]{:S(2)}) async-start(bf16[64,4,768]{2,1,0:T(4,128)(2,1)} %copy-done.4), calls=%async_computation.2 | async-start | bytes 786432 | tf_op jit(solution)/shard_map/all_to_all | solution.py:274
  132.3 1.1 copy-start.3
  133.4 0.9 copy-start.6
  134.3 0.9 copy-start.8

commit v8 on v6

--- a/solution.py
+++ b/solution.py
@@ -138,7 +138,7 @@
     return [(i, j) for i in range(n) for j in range(i, n)]
 
 
-def gram_kernel(a_ref, rows_ref, send, keep, slabs):
+def gram_kernel(a_ref, rows_ref, send_a, send_b, keep_a, keep_b, slabs):
     c = lax.rem(lax.axis_index("dp"), 2)
     count, _, cols = a_ref.shape
     for g in range(count // 4):
@@ -158,34 +158,37 @@
             slabs[0, b] = block[:64, :]
             slabs[1, b] = block[64:, :]
             b += 1
-    send[...] = slabs[1 - c].astype(BF)
-    keep[...] = slabs[c]
+    cut = send_a.shape[0]
+    send_a[...] = slabs[1 - c, :cut].astype(BF)
+    send_b[...] = slabs[1 - c, cut:].astype(BF)
+    keep_a[...] = slabs[c, :cut]
+    keep_b[...] = slabs[c, cut:]
 
 
 def partial_gram(a):
     count, _, cols = a.shape
     nb = len(blocks_of(cols))
+    halves = ((nb + 1) // 2, nb // 2)
     return pl.pallas_call(
         gram_kernel,
         in_specs=whole(1),
-        out_specs=whole(3),
-        out_shape=[
-            sds((4 * count, cols), BF),
-            sds((nb, 64, 128), BF),
-            sds((nb, 64, 128), F32),
-        ],
+        out_specs=whole(5),
+        out_shape=[sds((4 * count, cols), BF)] + [sds((k, 64, 128), t) for t in (BF, F32) for k in halves],
         scratch_shapes=[pltpu.VMEM((2, nb, 64, 128), F32)],
         compiler_params=params(),
         name="partial_gram",
     )(a)
 
 
-def polish_kernel(scale, own, other, rows_ref, out, slabs, level, low, poly, high):
+def polish_kernel(scale, own_a, own_b, other_a, other_b, rows_ref, out, slabs, level, low, poly, high):
     c = lax.rem(lax.axis_index("dp"), 2)
     count, cols = rows_ref.shape
     n = cols // 128
-    slabs[c] = own[...].astype(F32)
-    slabs[1 - c] = other[...].astype(F32)
+    cut = own_a.shape[0]
+    slabs[c, :cut] = own_a[...].astype(F32)
+    slabs[c, cut:] = own_b[...].astype(F32)
+    slabs[1 - c, :cut] = other_a[...].astype(F32)
+    slabs[1 - c, cut:] = other_b[...].astype(F32)
 
     eye = (
         lax.broadcasted_iota(jnp.int32, (128, 128), 0) == lax.broadcasted_iota(jnp.int32, (128, 128), 1)
@@ -228,10 +231,10 @@
 
 def polish(scale, own, other, rows):
     count, cols = rows.shape
-    nb = own.shape[0]
+    nb = sum(v.shape[0] for v in own)
     return pl.pallas_call(
         functools.partial(polish_kernel, scale),
-        in_specs=whole(3),
+        in_specs=whole(5),
         out_specs=whole(1)[0],
         out_shape=sds((count // 4, 4, cols), BF),
         scratch_shapes=[
@@ -243,7 +246,7 @@
         ],
         compiler_params=params(32),
         name="polish",
-    )(own, other, rows)
+    )(*own, *other, rows)
 
 
 def core_swap(v):
@@ -279,14 +282,15 @@
 
     mine = exchange(nesterov)
 
-    rows, gram_send, gram_keep = partial_gram(mine)
-    gram_keep, parts = lax.optimization_barrier((gram_keep, parts))
+    rows, *pieces = partial_gram(mine)
+    sends, keeps = pieces[:2], pieces[2:]
+    keeps, parts = lax.optimization_barrier((keeps, parts))
     new_momentum = momentum_call(momentum_kernel, F32, "new_momentum", *parts)
-    gram = gram_keep + core_swap(gram_send).astype(F32)
-    gram = gram + y_swap(gram.astype(BF), 0).astype(F32)
-    gram = gram + y_swap(gram.astype(BF), 1).astype(F32)
-    own = gram.astype(BF)
-    other = core_swap(own)
+    grams = [keep + core_swap(send).astype(F32) for keep, send in zip(keeps, sends)]
+    grams = [gram + y_swap(gram.astype(BF), 0).astype(F32) for gram in grams]
+    grams = [gram + y_swap(gram.astype(BF), 1).astype(F32) for gram in grams]
+    own = [gram.astype(BF) for gram in grams]
+    other = [core_swap(gram) for gram in own]
 
     update = polish(math.sqrt(max(n_rows, cols)), own, other, rows)
     return (exchange(update), new_momentum)

time: 140 us -> 141 us (level)
  starting transfers between devices: 33.2 us -> 42.8 us
  waiting for transfers between devices: 49.7 us -> 41.6 us
    ppermute x5 -> x7, waiting for transfers between devices: 21.6 us -> 15.4 us  [y_swap(): return lax.ppermute(v, 'dp', perm)]
    ppermute x5 -> x7, starting transfers between devices: 18.3 us -> 23.7 us  [y_swap(): return lax.ppermute(v, 'dp', perm)]
    ppermute x4 -> x6, starting transfers between devices: 8.17 us -> 12.5 us  [core_swap(): return lax.ppermute(v, 'dp', [(i, i ^ 1) for i in range(2 * NY)])]
    ppermute x4 -> x6, waiting for transfers between devices: 3.24 us -> 1.37 us  [core_swap(): return lax.ppermute(v, 'dp', [(i, i ^ 1) for i in range(2 * NY)])]
  transfers between devices with their start and end apart: 10 -> 14, of which waited for: 7 -> 7; matrix products, arithmetic and copies ran while one was open for 1% -> 1% of each run, Pallas kernels for 1% -> 1%
where the time goes in v8:
time: 141 us
  blocking collectives  43.1 us (31%)
  starting transfers between devices  42.8 us (30%)
  waiting for transfers between devices  41.6 us (30%)
  Pallas kernels  10.6 us (8%)
    all_to_all x1, blocking collectives, exchange(): return lax.all_to_all(v, 'fsdp', split_axis=0, concat_axis=0, tiled=True)  43.1 us
    all_to_all x1, waiting for transfers between devices, exchange(): return lax.all_to_all(v, 'fsdp', split_axis=0, concat_axis=0, tiled=True)  24.8 us
    ppermute x7, starting transfers between devices, y_swap(): return lax.ppermute(v, 'dp', perm)  23.7 us
    ppermute x7, waiting for transfers between devices, y_swap(): return lax.ppermute(v, 'dp', perm)  15.4 us
    ppermute x6, starting transfers between devices, core_swap(): return lax.ppermute(v, 'dp', [(i, i ^ 1) for i in range(2 * NY)])  12.5 us
    all_to_all x1, starting transfers between devices, exchange(): return lax.all_to_all(v, 'fsdp', split_axis=0, concat_axis=0, tiled=True)  6.67 us
    pallas_call x1, Pallas kernels, polish(): pl.pallas_call(functools.partial(polish_kernel, scale), in_specs=whole(5)...  5.23 us
  transfers between devices with their start and end apart: 14, of which 7 were waited for; matrix products, arithmetic and copies ran while one was open for 1% of the time, Pallas kernels for 1%

profile of v8, /device:TPU:6, one launch (start us, length us, event | category | flops | bytes accessed | tf_op | source)
XLA Modules:
  0.0 140.9 jit_solution(10670746841138320637)
XLA Ops:
  0.6 0.0 copy-start.1
  0.6 0.0 copy-start
  0.6 2.1 %split_rows.1 = (bf16[2,64,4,768]{3,2,1,0:T(4,128)(2,1)S(1)}, bf16[2,64,4,768]{3,2,1,0:T(4,128)(2,1)S(1)}, bf16[2,64,4,768]{3,2,1,0:T(4,128)(2,1)S(1)}, bf16[2,64,4,768]{3,2,1,0:T(4,128)(2,1)S(1)}) custom-call(bf16[1,64,32,768]{3,2,1,0:T(8,128)(2,1)} %g_hbm.1), custom_call_target="tpu_custom_call" | custom-call | tf_op jit(solution)/shard_map/split_rows/pallas_call | solution.py:81
  2.8 1.9 %collective-permute-start.1 = (bf16[2,64,4,768]{3,2,1,0:T(4,128)(2,1)S(1)}, bf16[2,64,4,768]{3,2,1,0:T(4,128)(2,1)S(1)}, u32[]{:S(2)}, u32[]{:S(2)}) collective-permute-start(bf16[2,64,4,768]{3,2,1,0:T(4,128)(2,1)S(1)} %get-tuple-element.22), channel_id=1, source_target_pairs={{0,64},{64,0},{128,192},{192,128},{256,320},{320,256},{384,448},{4... | collective-permute-start | bytes 2359304 | tf_op jit(solution)/shard_map/ppermute | solution.py:253
  4.7 2.4 %collective-permute-start = (bf16[2,64,4,768]{3,2,1,0:T(4,128)(2,1)S(1)}, bf16[2,64,4,768]{3,2,1,0:T(4,128)(2,1)S(1)}, u32[]{:S(2)}, u32[]{:S(2)}) collective-permute-start(bf16[2,64,4,768]{3,2,1,0:T(4,128)(2,1)S(1)} %get-tuple-element.20), channel_id=1, source_target_pairs={{0,64},{64,0},{128,192},{192,128},{256,320},{320,256},{384,448},{4... | collective-permute-start | bytes 2359304 | tf_op jit(solution)/shard_map/ppermute | solution.py:253
  7.1 0.0 collective-permute-done.1
  7.1 0.4 fusion.2
  7.5 3.5 %collective-permute-start.3 = (bf16[64,4,768]{2,1,0:T(4,128)(2,1)S(1)}, bf16[64,4,768]{2,1,0:T(4,128)(2,1)S(1)}, u32[]{:S(2)}, u32[]{:S(2)}) collective-permute-start(bf16[64,4,768]{2,1,0:T(4,128)(2,1)S(1)} %get-tuple-element.36), channel_id=1, source_target_pairs={{0,128},{64,448},{128,0},{192,320},{256,384},{320,192},{384,256},{... | collective-permute-start | bytes 1179656 | tf_op jit(solution)/shard_map/ppermute | solution.py:262
  11.0 2.4 %collective-permute-start.2 = (bf16[64,4,768]{2,1,0:T(4,128)(2,1)S(1)}, bf16[64,4,768]{2,1,0:T(4,128)(2,1)S(1)}, u32[]{:S(2)}, u32[]{:S(2)}) collective-permute-start(bf16[64,4,768]{2,1,0:T(4,128)(2,1)S(1)} %get-tuple-element.37), channel_id=1, source_target_pairs={{0,128},{64,448},{128,0},{192,320},{256,384},{320,192},{384,256},{... | collective-permute-start | bytes 1179656 | tf_op jit(solution)/shard_map/ppermute | solution.py:262
  13.4 0.0 collective-permute-done.swapped
  13.4 3.8 %collective-permute-done.3 = bf16[64,4,768]{2,1,0:T(4,128)(2,1)S(1)} collective-permute-done((bf16[64,4,768]{2,1,0:T(4,128)(2,1)S(1)}, bf16[64,4,768]{2,1,0:T(4,128)(2,1)S(1)}, u32[]{:S(2)}, u32[]{:S(2)}) %collective-permute-start.3) | collective-permute-done | bytes 393248 | tf_op jit(solution)/shard_map/ppermute | solution.py:262
  17.2 0.3 fusion
  17.5 4.9 %collective-permute-start.4 = (bf16[64,4,768]{2,1,0:T(4,128)(2,1)S(1)}, bf16[64,4,768]{2,1,0:T(4,128)(2,1)S(1)}, u32[]{:S(2)}, u32[]{:S(2)}) collective-permute-start(bf16[64,4,768]{2,1,0:T(4,128)(2,1)S(1)} %fusion), channel_id=1, source_target_pairs={{0,384},{64,192},{128,256},{192,64},{256,128},{320,448},{384,0},{4... | collective-permute-start | bytes 1179656 | tf_op jit(solution)/shard_map/ppermute | solution.py:262
  22.4 0.0 collective-permute-done.2.first
  22.4 5.9 %collective-permute-done.4.second = bf16[64,4,768]{2,1,0:T(4,128)(2,1)S(1)} collective-permute-done((bf16[64,4,768]{2,1,0:T(4,128)(2,1)S(1)}, bf16[64,4,768]{2,1,0:T(4,128)(2,1)S(1)}, u32[]{:S(2)}, u32[]{:S(2)}) %collective-permute-start.4) | collective-permute-done | bytes 393248 | tf_op jit(solution)/shard_map/ppermute | solution.py:262
  28.4 0.0 copy-done.1
  28.4 0.0 copy-done
  28.4 1.0 nesterov.1
  29.4 43.1 %all_to_all.10.a_ref = bf16[64,4,768]{2,1,0:T(4,128)(2,1)S(1)} all-to-all(bf16[64,4,768]{2,1,0:T(4,128)(2,1)S(1)} %nesterov.1), channel_id=1, replica_groups=mesh['dp'=8,'fsdp'=64] {'fsdp'}, dimensions={0} | all-to-all | bytes 786432 | tf_op jit(solution)/shard_map/all_to_all | solution.py:266
  72.5 0.6 partial_gram.1
  73.2 1.9 %collective-permute-start.5 = (bf16[11,64,128]{2,1,0:T(8,128)(2,1)S(1)}, bf16[11,64,128]{2,1,0:T(8,128)(2,1)S(1)}, u32[]{:S(2)}, u32[]{:S(2)}) collective-permute-start(bf16[11,64,128]{2,1,0:T(8,128)(2,1)S(1)} %get-tuple-element.26), channel_id=1, source_target_pairs={{0,64},{64,0},{128,192},{192,128},{256,320},{320,256},{384,448},{4... | collective-permute-start | bytes 540680 | tf_op jit(solution)/shard_map/ppermute | solution.py:253
  75.1 2.4 %collective-permute-start.8 = (bf16[10,64,128]{2,1,0:T(8,128)(2,1)S(1)}, bf16[10,64,128]{2,1,0:T(8,128)(2,1)S(1)}, u32[]{:S(2)}, u32[]{:S(2)}) collective-permute-start(bf16[10,64,128]{2,1,0:T(8,128)(2,1)S(1)} %get-tuple-element.28), channel_id=1, source_target_pairs={{0,64},{64,0},{128,192},{192,128},{256,320},{320,256},{384,448},{4... | collective-permute-start | bytes 491528 | tf_op jit(solution)/shard_map/ppermute | solution.py:253
  77.5 0.0 collective-permute-done.5
  77.6 2.7 %collective-permute-start.6 = (bf16[11,64,128]{2,1,0:T(8,128)(2,1)S(1)}, bf16[11,64,128]{2,1,0:T(8,128)(2,1)S(1)}, u32[]{:S(2)}, u32[]{:S(2)}) collective-permute-start(bf16[11,64,128]{2,1,0:T(8,128)(2,1)S(1)} %fusion.3), channel_id=1, source_target_pairs={{0,128},{64,448},{128,0},{192,320},{256,384},{320,192},{384,256},{... | collective-permute-start | bytes 540680 | tf_op jit(solution)/shard_map/ppermute | solution.py:262
  80.3 0.0 collective-permute-done.8
  80.4 3.1 %collective-permute-start.9 = (bf16[10,64,128]{2,1,0:T(8,128)(2,1)S(1)}, bf16[10,64,128]{2,1,0:T(8,128)(2,1)S(1)}, u32[]{:S(2)}, u32[]{:S(2)}) collective-permute-start(bf16[10,64,128]{2,1,0:T(8,128)(2,1)S(1)} %fusion.4), channel_id=1, source_target_pairs={{0,128},{64,448},{128,0},{192,320},{256,384},{320,192},{384,256},{... | collective-permute-start | bytes 491528 | tf_op jit(solution)/shard_map/ppermute | solution.py:262
  83.5 1.5 %collective-permute-done.6 = bf16[11,64,128]{2,1,0:T(8,128)(2,1)S(1)} collective-permute-done((bf16[11,64,128]{2,1,0:T(8,128)(2,1)S(1)}, bf16[11,64,128]{2,1,0:T(8,128)(2,1)S(1)}, u32[]{:S(2)}, u32[]{:S(2)}) %collective-permute-start.6) | collective-permute-done | bytes 180256 | tf_op jit(solution)/shard_map/ppermute | solution.py:262
  85.0 0.1 fusion.5
  85.0 4.8 %collective-permute-start.7 = (bf16[11,64,128]{2,1,0:T(8,128)(2,1)S(1)}, bf16[11,64,128]{2,1,0:T(8,128)(2,1)S(1)}, u32[]{:S(2)}, u32[]{:S(2)}) collective-permute-start(bf16[11,64,128]{2,1,0:T(8,128)(2,1)S(1)} %fusion.5), channel_id=1, source_target_pairs={{0,384},{64,192},{128,256},{192,64},{256,128},{320,448},{384,0},{4... | collective-permute-start | bytes 540680 | tf_op jit(solution)/shard_map/ppermute | solution.py:262
  89.9 0.0 collective-permute-done.9
  89.9 0.1 fusion.6
  90.0 2.2 %collective-permute-start.10 = (bf16[10,64,128]{2,1,0:T(8,128)(2,1)S(1)}, bf16[10,64,128]{2,1,0:T(8,128)(2,1)S(1)}, u32[]{:S(2)}, u32[]{:S(2)}) collective-permute-start(bf16[10,64,128]{2,1,0:T(8,128)(2,1)S(1)} %fusion.6), channel_id=1, source_target_pairs={{0,384},{64,192},{128,256},{192,64},{256,128},{320,448},{384,0},{4... | collective-permute-start | bytes 491528 | tf_op jit(solution)/shard_map/ppermute | solution.py:262
  92.2 1.5 %collective-permute-done.7 = bf16[11,64,128]{2,1,0:T(8,128)(2,1)S(1)} collective-permute-done((bf16[11,64,128]{2,1,0:T(8,128)(2,1)S(1)}, bf16[11,64,128]{2,1,0:T(8,128)(2,1)S(1)}, u32[]{:S(2)}, u32[]{:S(2)}) %collective-permute-start.7) | collective-permute-done | bytes 180256 | tf_op jit(solution)/shard_map/ppermute | solution.py:262
  93.6 0.1 add_convert_fusion.2.own_a
  93.7 1.9 %collective-permute-start.11 = (bf16[11,64,128]{2,1,0:T(8,128)(2,1)S(1)}, bf16[11,64,128]{2,1,0:T(8,128)(2,1)S(1)}, u32[]{:S(2)}, u32[]{:S(2)}) collective-permute-start(bf16[11,64,128]{2,1,0:T(8,128)(2,1)S(1)} %add_convert_fusion.2.own_a), channel_id=1, source_target_pairs={{0,64},{64,0},{128,192},{192,128},{256,320},{320,256},{384,448},{4... | collective-permute-start | bytes 540680 | tf_op jit(solution)/shard_map/ppermute | solution.py:253
  95.6 2.7 %collective-permute-done.10 = bf16[10,64,128]{2,1,0:T(8,128)(2,1)S(1)} collective-permute-done((bf16[10,64,128]{2,1,0:T(8,128)(2,1)S(1)}, bf16[10,64,128]{2,1,0:T(8,128)(2,1)S(1)}, u32[]{:S(2)}, u32[]{:S(2)}) %collective-permute-start.10) | collective-permute-done | bytes 163872 | tf_op jit(solution)/shard_map/ppermute | solution.py:262
  98.4 0.1 add_convert_fusion.3.own_b
  98.5 1.9 %collective-permute-start.12 = (bf16[10,64,128]{2,1,0:T(8,128)(2,1)S(1)}, bf16[10,64,128]{2,1,0:T(8,128)(2,1)S(1)}, u32[]{:S(2)}, u32[]{:S(2)}) collective-permute-start(bf16[10,64,128]{2,1,0:T(8,128)(2,1)S(1)} %add_convert_fusion.3.own_b), channel_id=1, source_target_pairs={{0,64},{64,0},{128,192},{192,128},{256,320},{320,256},{384,448},{4... | collective-permute-start | bytes 491528 | tf_op jit(solution)/shard_map/ppermute | solution.py:253
  100.4 1.4 collective-permute-done.12.other_b
  101.8 0.0 collective-permute-done.11.other_a
  101.8 5.2 %polish.1 = bf16[64,4,768]{2,1,0:T(4,128)(2,1)} custom-call(bf16[11,64,128]{2,1,0:T(8,128)(2,1)S(1)} %add_convert_fusion.2.own_a, bf16[10,64,128]{2,1,0:T(8,128)(2,1)S(1)} %add_convert_fusion.3.own_b, bf16[11,64,128]{2,1,0:T(8,128)(2,1)S(1)} %collective-permute-done.11.other_a, bf16[10,64,128]{2,1,0:T(8,128)(2,1)S(1)} %collective-permute-done.12.other_b, ...), custom_call_target="tpu_custom_call" | custom-call | tf_op jit(solution)/shard_map/polish/pallas_call | solution.py:235
  107.0 6.7 %all-to-all-start.1 = ((bf16[64,4,768]{2,1,0:T(4,128)(2,1)}), bf16[64,4,768]{2,1,0:T(4,128)(2,1)S(1)}, u32[]{:S(2)}, u32[]{:S(2)}) async-start(bf16[64,4,768]{2,1,0:T(4,128)(2,1)} %polish.1), calls=%async_computation.1 | async-start | bytes 786432 | tf_op jit(solution)/shard_map/all_to_all | solution.py:266
  113.7 1.7 %new_momentum.1 = f32[64,4,768]{2,1,0:T(4,128)} custom-call(s32[64]{0:T(128)S(1)} %copy-done.1, bf16[2,64,4,768]{3,2,1,0:T(4,128)(2,1)S(1)} %get-tuple-element.31.keep, bf16[2,64,4,768]{3,2,1,0:T(4,128)(2,1)S(1)} %collective-permute-done.swapped, bf16[64,4,768]{2,1,0:T(4,128)(2,1)S(1)} %collective-permute-done.2.first, ...), custom_call_target="tpu_custom_call" | custom-call | flops 1179648 | bytes 3145728 | tf_op jit(solution)/shard_map/new_momentum/pallas_call | solution.py:125
  115.4 24.8 %all-to-all-done.1 = bf16[64,4,768]{2,1,0:T(4,128)(2,1)S(1)} async-done(((bf16[64,4,768]{2,1,0:T(4,128)(2,1)}), bf16[64,4,768]{2,1,0:T(4,128)(2,1)S(1)}, u32[]{:S(2)}, u32[]{:S(2)}) %all-to-all-start.1) | async-done | bytes 393248 | tf_op jit(solution)/shard_map/all_to_all | solution.py:266
  140.2 0.7 copy.6
  (2 shorter events, 0.1 us)
Async XLA Ops:
  0.6 27.8 %copy-start.1 = (s32[64]{0:T(128)S(1)}, s32[64]{0:T(128)}, u32[]{:S(2)}) copy-start(s32[64]{0:T(128)} %slots.2) | copy-start | bytes 772
  0.6 27.8 %copy-start = (f32[64,4,768]{2,1,0:T(4,128)S(1)}, f32[64,4,768]{2,1,0:T(4,128)}, u32[]{:S(2)}) copy-start(f32[64,4,768]{2,1,0:T(4,128)} %mom.2) | copy-start | bytes 2359300
  2.8 4.3 %collective-permute-start.1 = (bf16[2,64,4,768]{3,2,1,0:T(4,128)(2,1)S(1)}, bf16[2,64,4,768]{3,2,1,0:T(4,128)(2,1)S(1)}, u32[]{:S(2)}, u32[]{:S(2)}) collective-permute-start(bf16[2,64,4,768]{3,2,1,0:T(4,128)(2,1)S(1)} %get-tuple-element.22), channel_id=1, source_target_pairs={{0,64},{64,0},{128,192},{192,128},{256,320},{320,256},{384,448},{4... | collective-permute-start | bytes 2359304 | tf_op jit(solution)/shard_map/ppermute | solution.py:253
  4.7 8.7 %collective-permute-start = (bf16[2,64,4,768]{3,2,1,0:T(4,128)(2,1)S(1)}, bf16[2,64,4,768]{3,2,1,0:T(4,128)(2,1)S(1)}, u32[]{:S(2)}, u32[]{:S(2)}) collective-permute-start(bf16[2,64,4,768]{3,2,1,0:T(4,128)(2,1)S(1)} %get-tuple-element.20), channel_id=1, source_target_pairs={{0,64},{64,0},{128,192},{192,128},{256,320},{320,256},{384,448},{4... | collective-permute-start | bytes 2359304 | tf_op jit(solution)/shard_map/ppermute | solution.py:253
  7.5 9.7 %collective-permute-start.3 = (bf16[64,4,768]{2,1,0:T(4,128)(2,1)S(1)}, bf16[64,4,768]{2,1,0:T(4,128)(2,1)S(1)}, u32[]{:S(2)}, u32[]{:S(2)}) collective-permute-start(bf16[64,4,768]{2,1,0:T(4,128)(2,1)S(1)} %get-tuple-element.36), channel_id=1, source_target_pairs={{0,128},{64,448},{128,0},{192,320},{256,384},{320,192},{384,256},{... | collective-permute-start | bytes 1179656 | tf_op jit(solution)/shard_map/ppermute | solution.py:262
  11.0 11.4 %collective-permute-start.2 = (bf16[64,4,768]{2,1,0:T(4,128)(2,1)S(1)}, bf16[64,4,768]{2,1,0:T(4,128)(2,1)S(1)}, u32[]{:S(2)}, u32[]{:S(2)}) collective-permute-start(bf16[64,4,768]{2,1,0:T(4,128)(2,1)S(1)} %get-tuple-element.37), channel_id=1, source_target_pairs={{0,128},{64,448},{128,0},{192,320},{256,384},{320,192},{384,256},{... | collective-permute-start | bytes 1179656 | tf_op jit(solution)/shard_map/ppermute | solution.py:262
  17.5 10.9 %collective-permute-start.4 = (bf16[64,4,768]{2,1,0:T(4,128)(2,1)S(1)}, bf16[64,4,768]{2,1,0:T(4,128)(2,1)S(1)}, u32[]{:S(2)}, u32[]{:S(2)}) collective-permute-start(bf16[64,4,768]{2,1,0:T(4,128)(2,1)S(1)} %fusion), channel_id=1, source_target_pairs={{0,384},{64,192},{128,256},{192,64},{256,128},{320,448},{384,0},{4... | collective-permute-start | bytes 1179656 | tf_op jit(solution)/shard_map/ppermute | solution.py:262
  73.2 4.3 %collective-permute-start.5 = (bf16[11,64,128]{2,1,0:T(8,128)(2,1)S(1)}, bf16[11,64,128]{2,1,0:T(8,128)(2,1)S(1)}, u32[]{:S(2)}, u32[]{:S(2)}) collective-permute-start(bf16[11,64,128]{2,1,0:T(8,128)(2,1)S(1)} %get-tuple-element.26), channel_id=1, source_target_pairs={{0,64},{64,0},{128,192},{192,128},{256,320},{320,256},{384,448},{4... | collective-permute-start | bytes 540680 | tf_op jit(solution)/shard_map/ppermute | solution.py:253
  75.1 5.2 %collective-permute-start.8 = (bf16[10,64,128]{2,1,0:T(8,128)(2,1)S(1)}, bf16[10,64,128]{2,1,0:T(8,128)(2,1)S(1)}, u32[]{:S(2)}, u32[]{:S(2)}) collective-permute-start(bf16[10,64,128]{2,1,0:T(8,128)(2,1)S(1)} %get-tuple-element.28), channel_id=1, source_target_pairs={{0,64},{64,0},{128,192},{192,128},{256,320},{320,256},{384,448},{4... | collective-permute-start | bytes 491528 | tf_op jit(solution)/shard_map/ppermute | solution.py:253
  77.6 7.4 %collective-permute-start.6 = (bf16[11,64,128]{2,1,0:T(8,128)(2,1)S(1)}, bf16[11,64,128]{2,1,0:T(8,128)(2,1)S(1)}, u32[]{:S(2)}, u32[]{:S(2)}) collective-permute-start(bf16[11,64,128]{2,1,0:T(8,128)(2,1)S(1)} %fusion.3), channel_id=1, source_target_pairs={{0,128},{64,448},{128,0},{192,320},{256,384},{320,192},{384,256},{... | collective-permute-start | bytes 540680 | tf_op jit(solution)/shard_map/ppermute | solution.py:262
  80.4 9.5 %collective-permute-start.9 = (bf16[10,64,128]{2,1,0:T(8,128)(2,1)S(1)}, bf16[10,64,128]{2,1,0:T(8,128)(2,1)S(1)}, u32[]{:S(2)}, u32[]{:S(2)}) collective-permute-start(bf16[10,64,128]{2,1,0:T(8,128)(2,1)S(1)} %fusion.4), channel_id=1, source_target_pairs={{0,128},{64,448},{128,0},{192,320},{256,384},{320,192},{384,256},{... | collective-permute-start | bytes 491528 | tf_op jit(solution)/shard_map/ppermute | solution.py:262
  85.0 8.6 %collective-permute-start.7 = (bf16[11,64,128]{2,1,0:T(8,128)(2,1)S(1)}, bf16[11,64,128]{2,1,0:T(8,128)(2,1)S(1)}, u32[]{:S(2)}, u32[]{:S(2)}) collective-permute-start(bf16[11,64,128]{2,1,0:T(8,128)(2,1)S(1)} %fusion.5), channel_id=1, source_target_pairs={{0,384},{64,192},{128,256},{192,64},{256,128},{320,448},{384,0},{4... | collective-permute-start | bytes 540680 | tf_op jit(solution)/shard_map/ppermute | solution.py:262
  90.0 8.4 %collective-permute-start.10 = (bf16[10,64,128]{2,1,0:T(8,128)(2,1)S(1)}, bf16[10,64,128]{2,1,0:T(8,128)(2,1)S(1)}, u32[]{:S(2)}, u32[]{:S(2)}) collective-permute-start(bf16[10,64,128]{2,1,0:T(8,128)(2,1)S(1)} %fusion.6), channel_id=1, source_target_pairs={{0,384},{64,192},{128,256},{192,64},{256,128},{320,448},{384,0},{4... | collective-permute-start | bytes 491528 | tf_op jit(solution)/shard_map/ppermute | solution.py:262
  93.7 8.0 %collective-permute-start.11 = (bf16[11,64,128]{2,1,0:T(8,128)(2,1)S(1)}, bf16[11,64,128]{2,1,0:T(8,128)(2,1)S(1)}, u32[]{:S(2)}, u32[]{:S(2)}) collective-permute-start(bf16[11,64,128]{2,1,0:T(8,128)(2,1)S(1)} %add_convert_fusion.2.own_a), channel_id=1, source_target_pairs={{0,64},{64,0},{128,192},{192,128},{256,320},{320,256},{384,448},{4... | collective-permute-start | bytes 540680 | tf_op jit(solution)/shard_map/ppermute | solution.py:253
  98.5 3.3 %collective-permute-start.12 = (bf16[10,64,128]{2,1,0:T(8,128)(2,1)S(1)}, bf16[10,64,128]{2,1,0:T(8,128)(2,1)S(1)}, u32[]{:S(2)}, u32[]{:S(2)}) collective-permute-start(bf16[10,64,128]{2,1,0:T(8,128)(2,1)S(1)} %add_convert_fusion.3.own_b), channel_id=1, source_target_pairs={{0,64},{64,0},{128,192},{192,128},{256,320},{320,256},{384,448},{4... | collective-permute-start | bytes 491528 | tf_op jit(solution)/shard_map/ppermute | solution.py:253
  107.0 33.2 %all-to-all-start.1 = ((bf16[64,4,768]{2,1,0:T(4,128)(2,1)}), bf16[64,4,768]{2,1,0:T(4,128)(2,1)S(1)}, u32[]{:S(2)}, u32[]{:S(2)}) async-start(bf16[64,4,768]{2,1,0:T(4,128)(2,1)} %polish.1), calls=%async_computation.1 | async-start | bytes 786432 | tf_op jit(solution)/shard_map/all_to_all | solution.py:266

commit v9 on v6

--- a/solution.py
+++ b/solution.py
@@ -286,7 +286,7 @@
     gram = gram + y_swap(gram.astype(BF), 0).astype(F32)
     gram = gram + y_swap(gram.astype(BF), 1).astype(F32)
     own = gram.astype(BF)
-    other = core_swap(own)
+    other, new_momentum = lax.optimization_barrier((core_swap(own), new_momentum))
 
     update = polish(math.sqrt(max(n_rows, cols)), own, other, rows)
     return (exchange(update), new_momentum)

time: 140 us -> 139 us (level)
  blocking collectives: 43.1 us -> 76.6 us
  waiting for transfers between devices: 49.7 us -> 23.3 us
  starting transfers between devices: 33.2 us -> 26.5 us
    all_to_all x1 -> x2, blocking collectives: 43.1 us -> 76.6 us  [exchange(): return lax.all_to_all(v, 'fsdp', split_axis=0, concat_axis=0, tiled=True)]
    all_to_all x1 -> x0, waiting for transfers between devices: 24.8 us -> none  [exchange(): return lax.all_to_all(v, 'fsdp', split_axis=0, concat_axis=0, tiled=True)]
    all_to_all x1 -> x0, starting transfers between devices: 6.66 us -> none  [exchange(): return lax.all_to_all(v, 'fsdp', split_axis=0, concat_axis=0, tiled=True)]
    ppermute x4, waiting for transfers between devices: 3.24 us -> 1.63 us  [core_swap(): return lax.ppermute(v, 'dp', [(i, i ^ 1) for i in range(2 * NY)])]
  transfers between devices with their start and end apart: 10 -> 9, of which waited for: 7 -> 5; matrix products, arithmetic and copies ran while one was open for 1% -> 1% of each run, Pallas kernels for 1% -> 1%
where the time goes in v9:
time: 139 us
  blocking collectives  76.6 us (55%)
  starting transfers between devices  26.5 us (19%)
  waiting for transfers between devices  23.3 us (17%)
  Pallas kernels  9.91 us (7%)
    all_to_all x2, blocking collectives, exchange(): return lax.all_to_all(v, 'fsdp', split_axis=0, concat_axis=0, tiled=True)  76.6 us
    ppermute x5, waiting for transfers between devices, y_swap(): return lax.ppermute(v, 'dp', perm)  21.6 us
    ppermute x5, starting transfers between devices, y_swap(): return lax.ppermute(v, 'dp', perm)  18.3 us
    ppermute x4, starting transfers between devices, core_swap(): return lax.ppermute(v, 'dp', [(i, i ^ 1) for i in range(2 * NY)])  8.17 us
    pallas_call x1, Pallas kernels, polish(): pl.pallas_call(functools.partial(polish_kernel, scale), in_specs=whole(3)...  4.48 us
  transfers between devices with their start and end apart: 9, of which 5 were waited for; matrix products, arithmetic and copies ran while one was open for 1% of the time, Pallas kernels for 1%

profile of v9, /device:TPU:6, one launch (start us, length us, event | category | flops | bytes accessed | tf_op | source)
XLA Modules:
  0.0 139.0 jit_solution(11632631429548095519)
XLA Ops:
  0.6 0.0 copy-start.1
  0.6 0.0 copy-start
  0.6 2.1 %split_rows.1 = (bf16[2,64,4,768]{3,2,1,0:T(4,128)(2,1)S(1)}, bf16[2,64,4,768]{3,2,1,0:T(4,128)(2,1)S(1)}, bf16[2,64,4,768]{3,2,1,0:T(4,128)(2,1)S(1)}, bf16[2,64,4,768]{3,2,1,0:T(4,128)(2,1)S(1)}) custom-call(bf16[1,64,32,768]{3,2,1,0:T(8,128)(2,1)} %g_hbm.1), custom_call_target="tpu_custom_call" | custom-call | tf_op jit(solution)/shard_map/split_rows/pallas_call | solution.py:81
  2.8 1.9 %collective-permute-start.1 = (bf16[2,64,4,768]{3,2,1,0:T(4,128)(2,1)S(1)}, bf16[2,64,4,768]{3,2,1,0:T(4,128)(2,1)S(1)}, u32[]{:S(2)}, u32[]{:S(2)}) collective-permute-start(bf16[2,64,4,768]{3,2,1,0:T(4,128)(2,1)S(1)} %get-tuple-element.21), channel_id=1, source_target_pairs={{0,64},{64,0},{128,192},{192,128},{256,320},{320,256},{384,448},{4... | collective-permute-start | bytes 2359304 | tf_op jit(solution)/shard_map/ppermute | solution.py:250
  4.7 2.4 %collective-permute-start = (bf16[2,64,4,768]{3,2,1,0:T(4,128)(2,1)S(1)}, bf16[2,64,4,768]{3,2,1,0:T(4,128)(2,1)S(1)}, u32[]{:S(2)}, u32[]{:S(2)}) collective-permute-start(bf16[2,64,4,768]{3,2,1,0:T(4,128)(2,1)S(1)} %get-tuple-element.19), channel_id=1, source_target_pairs={{0,64},{64,0},{128,192},{192,128},{256,320},{320,256},{384,448},{4... | collective-permute-start | bytes 2359304 | tf_op jit(solution)/shard_map/ppermute | solution.py:250
  7.1 0.0 collective-permute-done.1
  7.1 0.4 fusion.3
  7.5 3.5 %collective-permute-start.3 = (bf16[64,4,768]{2,1,0:T(4,128)(2,1)S(1)}, bf16[64,4,768]{2,1,0:T(4,128)(2,1)S(1)}, u32[]{:S(2)}, u32[]{:S(2)}) collective-permute-start(bf16[64,4,768]{2,1,0:T(4,128)(2,1)S(1)} %get-tuple-element.34), channel_id=1, source_target_pairs={{0,128},{64,448},{128,0},{192,320},{256,384},{320,192},{384,256},{... | collective-permute-start | bytes 1179656 | tf_op jit(solution)/shard_map/ppermute | solution.py:259
  11.0 2.4 %collective-permute-start.2 = (bf16[64,4,768]{2,1,0:T(4,128)(2,1)S(1)}, bf16[64,4,768]{2,1,0:T(4,128)(2,1)S(1)}, u32[]{:S(2)}, u32[]{:S(2)}) collective-permute-start(bf16[64,4,768]{2,1,0:T(4,128)(2,1)S(1)} %get-tuple-element.35), channel_id=1, source_target_pairs={{0,128},{64,448},{128,0},{192,320},{256,384},{320,192},{384,256},{... | collective-permute-start | bytes 1179656 | tf_op jit(solution)/shard_map/ppermute | solution.py:259
  13.4 0.0 collective-permute-done.swapped
  13.4 3.8 %collective-permute-done.3 = bf16[64,4,768]{2,1,0:T(4,128)(2,1)S(1)} collective-permute-done((bf16[64,4,768]{2,1,0:T(4,128)(2,1)S(1)}, bf16[64,4,768]{2,1,0:T(4,128)(2,1)S(1)}, u32[]{:S(2)}, u32[]{:S(2)}) %collective-permute-start.3) | collective-permute-done | bytes 393248 | tf_op jit(solution)/shard_map/ppermute | solution.py:259
  17.2 0.3 fusion
  17.5 4.9 %collective-permute-start.4 = (bf16[64,4,768]{2,1,0:T(4,128)(2,1)S(1)}, bf16[64,4,768]{2,1,0:T(4,128)(2,1)S(1)}, u32[]{:S(2)}, u32[]{:S(2)}) collective-permute-start(bf16[64,4,768]{2,1,0:T(4,128)(2,1)S(1)} %fusion), channel_id=1, source_target_pairs={{0,384},{64,192},{128,256},{192,64},{256,128},{320,448},{384,0},{4... | collective-permute-start | bytes 1179656 | tf_op jit(solution)/shard_map/ppermute | solution.py:259
  22.4 0.0 collective-permute-done.2.first
  22.4 5.9 %collective-permute-done.4.second = bf16[64,4,768]{2,1,0:T(4,128)(2,1)S(1)} collective-permute-done((bf16[64,4,768]{2,1,0:T(4,128)(2,1)S(1)}, bf16[64,4,768]{2,1,0:T(4,128)(2,1)S(1)}, u32[]{:S(2)}, u32[]{:S(2)}) %collective-permute-start.4) | collective-permute-done | bytes 393248 | tf_op jit(solution)/shard_map/ppermute | solution.py:259
  28.4 0.0 copy-done.1
  28.4 0.0 copy-done
  28.4 1.0 nesterov.1
  29.4 43.1 %all_to_all.10.a_ref = bf16[64,4,768]{2,1,0:T(4,128)(2,1)S(1)} all-to-all(bf16[64,4,768]{2,1,0:T(4,128)(2,1)S(1)} %nesterov.1), channel_id=1, replica_groups=mesh['dp'=8,'fsdp'=64] {'fsdp'}, dimensions={0} | all-to-all | bytes 786432 | tf_op jit(solution)/shard_map/all_to_all | solution.py:263
  72.5 0.6 partial_gram.1
  73.2 1.9 %collective-permute-start.5 = (bf16[21,64,128]{2,1,0:T(8,128)(2,1)S(1)}, bf16[21,64,128]{2,1,0:T(8,128)(2,1)S(1)}, u32[]{:S(2)}, u32[]{:S(2)}) collective-permute-start(bf16[21,64,128]{2,1,0:T(8,128)(2,1)S(1)} %get-tuple-element.24), channel_id=1, source_target_pairs={{0,64},{64,0},{128,192},{192,128},{256,320},{320,256},{384,448},{4... | collective-permute-start | bytes 1032200 | tf_op jit(solution)/shard_map/ppermute | solution.py:250
  75.1 1.6 %collective-permute-done.5 = bf16[21,64,128]{2,1,0:T(8,128)(2,1)S(1)} collective-permute-done((bf16[21,64,128]{2,1,0:T(8,128)(2,1)S(1)}, bf16[21,64,128]{2,1,0:T(8,128)(2,1)S(1)}, u32[]{:S(2)}, u32[]{:S(2)}) %collective-permute-start.5) | collective-permute-done | bytes 344096 | tf_op jit(solution)/shard_map/ppermute | solution.py:250
  76.7 0.1 fusion.1
  76.8 2.7 %collective-permute-start.6 = (bf16[21,64,128]{2,1,0:T(8,128)(2,1)S(1)}, bf16[21,64,128]{2,1,0:T(8,128)(2,1)S(1)}, u32[]{:S(2)}, u32[]{:S(2)}) collective-permute-start(bf16[21,64,128]{2,1,0:T(8,128)(2,1)S(1)} %fusion.1), channel_id=1, source_target_pairs={{0,128},{64,448},{128,0},{192,320},{256,384},{320,192},{384,256},{... | collective-permute-start | bytes 1032200 | tf_op jit(solution)/shard_map/ppermute | solution.py:259
  79.5 6.4 %collective-permute-done.6 = bf16[21,64,128]{2,1,0:T(8,128)(2,1)S(1)} collective-permute-done((bf16[21,64,128]{2,1,0:T(8,128)(2,1)S(1)}, bf16[21,64,128]{2,1,0:T(8,128)(2,1)S(1)}, u32[]{:S(2)}, u32[]{:S(2)}) %collective-permute-start.6) | collective-permute-done | bytes 344096 | tf_op jit(solution)/shard_map/ppermute | solution.py:259
  86.0 0.1 fusion.4
  86.1 4.9 %collective-permute-start.7 = (bf16[21,64,128]{2,1,0:T(8,128)(2,1)S(1)}, bf16[21,64,128]{2,1,0:T(8,128)(2,1)S(1)}, u32[]{:S(2)}, u32[]{:S(2)}) collective-permute-start(bf16[21,64,128]{2,1,0:T(8,128)(2,1)S(1)} %fusion.4), channel_id=1, source_target_pairs={{0,384},{64,192},{128,256},{192,64},{256,128},{320,448},{384,0},{4... | collective-permute-start | bytes 1032200 | tf_op jit(solution)/shard_map/ppermute | solution.py:259
  91.0 5.5 %collective-permute-done.7 = bf16[21,64,128]{2,1,0:T(8,128)(2,1)S(1)} collective-permute-done((bf16[21,64,128]{2,1,0:T(8,128)(2,1)S(1)}, bf16[21,64,128]{2,1,0:T(8,128)(2,1)S(1)}, u32[]{:S(2)}, u32[]{:S(2)}) %collective-permute-start.7) | collective-permute-done | bytes 344096 | tf_op jit(solution)/shard_map/ppermute | solution.py:259
  96.5 0.2 add_convert_fusion.2.own
  96.7 1.9 %collective-permute-start.8 = (bf16[21,64,128]{2,1,0:T(8,128)(2,1)S(1)}, bf16[21,64,128]{2,1,0:T(8,128)(2,1)S(1)}, u32[]{:S(2)}, u32[]{:S(2)}) collective-permute-start(bf16[21,64,128]{2,1,0:T(8,128)(2,1)S(1)} %add_convert_fusion.2.own), channel_id=1, source_target_pairs={{0,64},{64,0},{128,192},{192,128},{256,320},{320,256},{384,448},{4... | collective-permute-start | bytes 1032200 | tf_op jit(solution)/shard_map/ppermute | solution.py:250
  98.6 1.7 %new_momentum.1 = f32[64,4,768]{2,1,0:T(4,128)} custom-call(s32[64]{0:T(128)S(1)} %copy-done.1, bf16[2,64,4,768]{3,2,1,0:T(4,128)(2,1)S(1)} %get-tuple-element.26.keep, bf16[2,64,4,768]{3,2,1,0:T(4,128)(2,1)S(1)} %collective-permute-done.swapped, bf16[64,4,768]{2,1,0:T(4,128)(2,1)S(1)} %collective-permute-done.2.first, ...), custom_call_target="tpu_custom_call" | custom-call | flops 1179648 | bytes 3145728 | tf_op jit(solution)/shard_map/new_momentum/pallas_call | solution.py:125
  100.3 0.0 collective-permute-done.8.other
  100.3 4.5 %polish.1 = bf16[64,4,768]{2,1,0:T(4,128)(2,1)S(1)} custom-call(bf16[21,64,128]{2,1,0:T(8,128)(2,1)S(1)} %add_convert_fusion.2.own, bf16[21,64,128]{2,1,0:T(8,128)(2,1)S(1)} %collective-permute-done.8.other, bf16[256,768]{1,0:T(8,128)(2,1)S(1)} %get-tuple-element.32.rows_ref), custom_call_target="tpu_custom_call" | custom-call | tf_op jit(solution)/shard_map/polish/pallas_call | solution.py:232
  104.8 33.4 %all_to_all.11 = bf16[64,4,768]{2,1,0:T(4,128)(2,1)S(1)} all-to-all(bf16[64,4,768]{2,1,0:T(4,128)(2,1)S(1)} %polish.1), channel_id=1, replica_groups=mesh['dp'=8,'fsdp'=64] {'fsdp'}, dimensions={0} | all-to-all | bytes 786432 | tf_op jit(solution)/shard_map/all_to_all | solution.py:263
  138.2 0.7 copy.6
Async XLA Ops:
  0.6 27.8 %copy-start.1 = (s32[64]{0:T(128)S(1)}, s32[64]{0:T(128)}, u32[]{:S(2)}) copy-start(s32[64]{0:T(128)} %slots.2) | copy-start | bytes 772
  0.6 27.8 %copy-start = (f32[64,4,768]{2,1,0:T(4,128)S(1)}, f32[64,4,768]{2,1,0:T(4,128)}, u32[]{:S(2)}) copy-start(f32[64,4,768]{2,1,0:T(4,128)} %mom.2) | copy-start | bytes 2359300
  2.8 4.3 %collective-permute-start.1 = (bf16[2,64,4,768]{3,2,1,0:T(4,128)(2,1)S(1)}, bf16[2,64,4,768]{3,2,1,0:T(4,128)(2,1)S(1)}, u32[]{:S(2)}, u32[]{:S(2)}) collective-permute-start(bf16[2,64,4,768]{3,2,1,0:T(4,128)(2,1)S(1)} %get-tuple-element.21), channel_id=1, source_target_pairs={{0,64},{64,0},{128,192},{192,128},{256,320},{320,256},{384,448},{4... | collective-permute-start | bytes 2359304 | tf_op jit(solution)/shard_map/ppermute | solution.py:250
  4.7 8.7 %collective-permute-start = (bf16[2,64,4,768]{3,2,1,0:T(4,128)(2,1)S(1)}, bf16[2,64,4,768]{3,2,1,0:T(4,128)(2,1)S(1)}, u32[]{:S(2)}, u32[]{:S(2)}) collective-permute-start(bf16[2,64,4,768]{3,2,1,0:T(4,128)(2,1)S(1)} %get-tuple-element.19), channel_id=1, source_target_pairs={{0,64},{64,0},{128,192},{192,128},{256,320},{320,256},{384,448},{4... | collective-permute-start | bytes 2359304 | tf_op jit(solution)/shard_map/ppermute | solution.py:250
  7.5 9.7 %collective-permute-start.3 = (bf16[64,4,768]{2,1,0:T(4,128)(2,1)S(1)}, bf16[64,4,768]{2,1,0:T(4,128)(2,1)S(1)}, u32[]{:S(2)}, u32[]{:S(2)}) collective-permute-start(bf16[64,4,768]{2,1,0:T(4,128)(2,1)S(1)} %get-tuple-element.34), channel_id=1, source_target_pairs={{0,128},{64,448},{128,0},{192,320},{256,384},{320,192},{384,256},{... | collective-permute-start | bytes 1179656 | tf_op jit(solution)/shard_map/ppermute | solution.py:259
  11.0 11.4 %collective-permute-start.2 = (bf16[64,4,768]{2,1,0:T(4,128)(2,1)S(1)}, bf16[64,4,768]{2,1,0:T(4,128)(2,1)S(1)}, u32[]{:S(2)}, u32[]{:S(2)}) collective-permute-start(bf16[64,4,768]{2,1,0:T(4,128)(2,1)S(1)} %get-tuple-element.35), channel_id=1, source_target_pairs={{0,128},{64,448},{128,0},{192,320},{256,384},{320,192},{384,256},{... | collective-permute-start | bytes 1179656 | tf_op jit(solution)/shard_map/ppermute | solution.py:259
  17.5 10.9 %collective-permute-start.4 = (bf16[64,4,768]{2,1,0:T(4,128)(2,1)S(1)}, bf16[64,4,768]{2,1,0:T(4,128)(2,1)S(1)}, u32[]{:S(2)}, u32[]{:S(2)}) collective-permute-start(bf16[64,4,768]{2,1,0:T(4,128)(2,1)S(1)} %fusion), channel_id=1, source_target_pairs={{0,384},{64,192},{128,256},{192,64},{256,128},{320,448},{384,0},{4... | collective-permute-start | bytes 1179656 | tf_op jit(solution)/shard_map/ppermute | solution.py:259
  73.2 3.5 %collective-permute-start.5 = (bf16[21,64,128]{2,1,0:T(8,128)(2,1)S(1)}, bf16[21,64,128]{2,1,0:T(8,128)(2,1)S(1)}, u32[]{:S(2)}, u32[]{:S(2)}) collective-permute-start(bf16[21,64,128]{2,1,0:T(8,128)(2,1)S(1)} %get-tuple-element.24), channel_id=1, source_target_pairs={{0,64},{64,0},{128,192},{192,128},{256,320},{320,256},{384,448},{4... | collective-permute-start | bytes 1032200 | tf_op jit(solution)/shard_map/ppermute | solution.py:250
  76.8 9.1 %collective-permute-start.6 = (bf16[21,64,128]{2,1,0:T(8,128)(2,1)S(1)}, bf16[21,64,128]{2,1,0:T(8,128)(2,1)S(1)}, u32[]{:S(2)}, u32[]{:S(2)}) collective-permute-start(bf16[21,64,128]{2,1,0:T(8,128)(2,1)S(1)} %fusion.1), channel_id=1, source_target_pairs={{0,128},{64,448},{128,0},{192,320},{256,384},{320,192},{384,256},{... | collective-permute-start | bytes 1032200 | tf_op jit(solution)/shard_map/ppermute | solution.py:259
  86.1 10.4 %collective-permute-start.7 = (bf16[21,64,128]{2,1,0:T(8,128)(2,1)S(1)}, bf16[21,64,128]{2,1,0:T(8,128)(2,1)S(1)}, u32[]{:S(2)}, u32[]{:S(2)}) collective-permute-start(bf16[21,64,128]{2,1,0:T(8,128)(2,1)S(1)} %fusion.4), channel_id=1, source_target_pairs={{0,384},{64,192},{128,256},{192,64},{256,128},{320,448},{384,0},{4... | collective-permute-start | bytes 1032200 | tf_op jit(solution)/shard_map/ppermute | solution.py:259
  96.7 3.6 %collective-permute-start.8 = (bf16[21,64,128]{2,1,0:T(8,128)(2,1)S(1)}, bf16[21,64,128]{2,1,0:T(8,128)(2,1)S(1)}, u32[]{:S(2)}, u32[]{:S(2)}) collective-permute-start(bf16[21,64,128]{2,1,0:T(8,128)(2,1)S(1)} %add_convert_fusion.2.own), channel_id=1, source_target_pairs={{0,64},{64,0},{128,192},{192,128},{256,320},{320,256},{384,448},{4... | collective-permute-start | bytes 1032200 | tf_op jit(solution)/shard_map/ppermute | solution.py:250

commit v10 on v9

--- a/solution.py
+++ b/solution.py
@@ -259,6 +259,13 @@
     return lax.ppermute(v, "dp", perm)
 
 
+def y_cross(v):
+    perm = []
+    for y in range(NY):
+        perm += [(2 * y, 2 * (NY - 1 - y) + 1), (2 * y + 1, 2 * (y ^ 1))]
+    return lax.ppermute(v, "dp", perm)
+
+
 def exchange(v):
     return lax.all_to_all(v, "fsdp", split_axis=0, concat_axis=0, tiled=True)
 
@@ -284,9 +291,10 @@
     new_momentum = momentum_call(momentum_kernel, F32, "new_momentum", *parts)
     gram = gram_keep + core_swap(gram_send).astype(F32)
     gram = gram + y_swap(gram.astype(BF), 0).astype(F32)
-    gram = gram + y_swap(gram.astype(BF), 1).astype(F32)
-    own = gram.astype(BF)
-    other, new_momentum = lax.optimization_barrier((core_swap(own), new_momentum))
+    low = gram.astype(BF)
+    other = (core_swap(low).astype(F32) + y_cross(low).astype(F32)).astype(BF)
+    own = (low.astype(F32) + y_swap(low, 1).astype(F32)).astype(BF)
+    other, new_momentum = lax.optimization_barrier((other, new_momentum))
 
     update = polish(math.sqrt(max(n_rows, cols)), own, other, rows)
     return (exchange(update), new_momentum)

time: 139 us -> 140 us (level)
  starting transfers between devices: 26.5 us -> 28.8 us
  blocking collectives: 76.6 us -> 74.5 us
    ppermute x0 -> x1, starting transfers between devices: none -> 4.65 us  [y_cross(): return lax.ppermute(v, 'dp', perm)]
    ppermute x5, starting transfers between devices: 18.3 us -> 16 us  [y_swap(): return lax.ppermute(v, 'dp', perm)]
    all_to_all x2, blocking collectives: 76.6 us -> 74.5 us  [exchange(): return lax.all_to_all(v, 'fsdp', split_axis=0, concat_axis=0, tiled=True)]
  transfers between devices with their start and end apart: 9 -> 10, of which waited for: 5 -> 5; matrix products, arithmetic and copies ran while one was open for 1% -> 1% of each run, Pallas kernels for 1% -> 1%
where the time goes in v10:
time: 140 us
  blocking collectives  74.5 us (53%)
  starting transfers between devices  28.8 us (21%)
  waiting for transfers between devices  23.8 us (17%)
  Pallas kernels  9.92 us (7%)
    all_to_all x2, blocking collectives, exchange(): return lax.all_to_all(v, 'fsdp', split_axis=0, concat_axis=0, tiled=True)  74.5 us
    ppermute x5, waiting for transfers between devices, y_swap(): return lax.ppermute(v, 'dp', perm)  22.2 us
    ppermute x5, starting transfers between devices, y_swap(): return lax.ppermute(v, 'dp', perm)  16 us
    ppermute x4, starting transfers between devices, core_swap(): return lax.ppermute(v, 'dp', [(i, i ^ 1) for i in range(2 * NY)])  8.17 us
    ppermute x1, starting transfers between devices, y_cross(): return lax.ppermute(v, 'dp', perm)  4.65 us
    pallas_call x1, Pallas kernels, polish(): pl.pallas_call(functools.partial(polish_kernel, scale), in_specs=whole(3)...  4.49 us
  transfers between devices with their start and end apart: 10, of which 5 were waited for; matrix products, arithmetic and copies ran while one was open for 1% of the time, Pallas kernels for 1%

profile of v10, /device:TPU:6, one launch (start us, length us, event | category | flops | bytes accessed | tf_op | source)
XLA Modules:
  0.0 139.8 jit_solution(2583385023090388990)
XLA Ops:
  0.6 0.0 copy-start.1
  0.6 0.0 copy-start
  0.6 2.1 %split_rows.1 = (bf16[2,64,4,768]{3,2,1,0:T(4,128)(2,1)S(1)}, bf16[2,64,4,768]{3,2,1,0:T(4,128)(2,1)S(1)}, bf16[2,64,4,768]{3,2,1,0:T(4,128)(2,1)S(1)}, bf16[2,64,4,768]{3,2,1,0:T(4,128)(2,1)S(1)}) custom-call(bf16[1,64,32,768]{3,2,1,0:T(8,128)(2,1)} %g_hbm.1), custom_call_target="tpu_custom_call" | custom-call | tf_op jit(solution)/shard_map/split_rows/pallas_call | solution.py:81
  2.8 1.9 %collective-permute-start.1 = (bf16[2,64,4,768]{3,2,1,0:T(4,128)(2,1)S(1)}, bf16[2,64,4,768]{3,2,1,0:T(4,128)(2,1)S(1)}, u32[]{:S(2)}, u32[]{:S(2)}) collective-permute-start(bf16[2,64,4,768]{3,2,1,0:T(4,128)(2,1)S(1)} %get-tuple-element.21), channel_id=1, source_target_pairs={{0,64},{64,0},{128,192},{192,128},{256,320},{320,256},{384,448},{4... | collective-permute-start | bytes 2359304 | tf_op jit(solution)/shard_map/ppermute | solution.py:250
  4.7 2.4 %collective-permute-start = (bf16[2,64,4,768]{3,2,1,0:T(4,128)(2,1)S(1)}, bf16[2,64,4,768]{3,2,1,0:T(4,128)(2,1)S(1)}, u32[]{:S(2)}, u32[]{:S(2)}) collective-permute-start(bf16[2,64,4,768]{3,2,1,0:T(4,128)(2,1)S(1)} %get-tuple-element.19), channel_id=1, source_target_pairs={{0,64},{64,0},{128,192},{192,128},{256,320},{320,256},{384,448},{4... | collective-permute-start | bytes 2359304 | tf_op jit(solution)/shard_map/ppermute | solution.py:250
  7.1 0.0 collective-permute-done.1
  7.1 0.4 fusion.3
  7.5 3.5 %collective-permute-start.3 = (bf16[64,4,768]{2,1,0:T(4,128)(2,1)S(1)}, bf16[64,4,768]{2,1,0:T(4,128)(2,1)S(1)}, u32[]{:S(2)}, u32[]{:S(2)}) collective-permute-start(bf16[64,4,768]{2,1,0:T(4,128)(2,1)S(1)} %get-tuple-element.34), channel_id=1, source_target_pairs={{0,128},{64,448},{128,0},{192,320},{256,384},{320,192},{384,256},{... | collective-permute-start | bytes 1179656 | tf_op jit(solution)/shard_map/ppermute | solution.py:259
  11.0 2.4 %collective-permute-start.2 = (bf16[64,4,768]{2,1,0:T(4,128)(2,1)S(1)}, bf16[64,4,768]{2,1,0:T(4,128)(2,1)S(1)}, u32[]{:S(2)}, u32[]{:S(2)}) collective-permute-start(bf16[64,4,768]{2,1,0:T(4,128)(2,1)S(1)} %get-tuple-element.35), channel_id=1, source_target_pairs={{0,128},{64,448},{128,0},{192,320},{256,384},{320,192},{384,256},{... | collective-permute-start | bytes 1179656 | tf_op jit(solution)/shard_map/ppermute | solution.py:259
  13.4 0.0 collective-permute-done.swapped
  13.4 3.8 %collective-permute-done.3 = bf16[64,4,768]{2,1,0:T(4,128)(2,1)S(1)} collective-permute-done((bf16[64,4,768]{2,1,0:T(4,128)(2,1)S(1)}, bf16[64,4,768]{2,1,0:T(4,128)(2,1)S(1)}, u32[]{:S(2)}, u32[]{:S(2)}) %collective-permute-start.3) | collective-permute-done | bytes 393248 | tf_op jit(solution)/shard_map/ppermute | solution.py:259
  17.2 0.3 fusion
  17.5 4.9 %collective-permute-start.4 = (bf16[64,4,768]{2,1,0:T(4,128)(2,1)S(1)}, bf16[64,4,768]{2,1,0:T(4,128)(2,1)S(1)}, u32[]{:S(2)}, u32[]{:S(2)}) collective-permute-start(bf16[64,4,768]{2,1,0:T(4,128)(2,1)S(1)} %fusion), channel_id=1, source_target_pairs={{0,384},{64,192},{128,256},{192,64},{256,128},{320,448},{384,0},{4... | collective-permute-start | bytes 1179656 | tf_op jit(solution)/shard_map/ppermute | solution.py:259
  22.4 0.0 collective-permute-done.2.first
  22.4 5.9 %collective-permute-done.4.second = bf16[64,4,768]{2,1,0:T(4,128)(2,1)S(1)} collective-permute-done((bf16[64,4,768]{2,1,0:T(4,128)(2,1)S(1)}, bf16[64,4,768]{2,1,0:T(4,128)(2,1)S(1)}, u32[]{:S(2)}, u32[]{:S(2)}) %collective-permute-start.4) | collective-permute-done | bytes 393248 | tf_op jit(solution)/shard_map/ppermute | solution.py:259
  28.4 0.0 copy-done.1
  28.4 0.0 copy-done
  28.4 1.0 nesterov.1
  29.4 43.1 %all_to_all.10.a_ref = bf16[64,4,768]{2,1,0:T(4,128)(2,1)S(1)} all-to-all(bf16[64,4,768]{2,1,0:T(4,128)(2,1)S(1)} %nesterov.1), channel_id=1, replica_groups=mesh['dp'=8,'fsdp'=64] {'fsdp'}, dimensions={0} | all-to-all | bytes 786432 | tf_op jit(solution)/shard_map/all_to_all | solution.py:270
  72.5 0.6 partial_gram.1
  73.2 1.9 %collective-permute-start.5 = (bf16[21,64,128]{2,1,0:T(8,128)(2,1)S(1)}, bf16[21,64,128]{2,1,0:T(8,128)(2,1)S(1)}, u32[]{:S(2)}, u32[]{:S(2)}) collective-permute-start(bf16[21,64,128]{2,1,0:T(8,128)(2,1)S(1)} %get-tuple-element.24), channel_id=1, source_target_pairs={{0,64},{64,0},{128,192},{192,128},{256,320},{320,256},{384,448},{4... | collective-permute-start | bytes 1032200 | tf_op jit(solution)/shard_map/ppermute | solution.py:250
  75.1 1.6 %collective-permute-done.5 = bf16[21,64,128]{2,1,0:T(8,128)(2,1)S(1)} collective-permute-done((bf16[21,64,128]{2,1,0:T(8,128)(2,1)S(1)}, bf16[21,64,128]{2,1,0:T(8,128)(2,1)S(1)}, u32[]{:S(2)}, u32[]{:S(2)}) %collective-permute-start.5) | collective-permute-done | bytes 344096 | tf_op jit(solution)/shard_map/ppermute | solution.py:250
  76.7 0.1 fusion.1
  76.8 2.7 %collective-permute-start.6 = (bf16[21,64,128]{2,1,0:T(8,128)(2,1)S(1)}, bf16[21,64,128]{2,1,0:T(8,128)(2,1)S(1)}, u32[]{:S(2)}, u32[]{:S(2)}) collective-permute-start(bf16[21,64,128]{2,1,0:T(8,128)(2,1)S(1)} %fusion.1), channel_id=1, source_target_pairs={{0,128},{64,448},{128,0},{192,320},{256,384},{320,192},{384,256},{... | collective-permute-start | bytes 1032200 | tf_op jit(solution)/shard_map/ppermute | solution.py:259
  79.6 6.4 %collective-permute-done.6 = bf16[21,64,128]{2,1,0:T(8,128)(2,1)S(1)} collective-permute-done((bf16[21,64,128]{2,1,0:T(8,128)(2,1)S(1)}, bf16[21,64,128]{2,1,0:T(8,128)(2,1)S(1)}, u32[]{:S(2)}, u32[]{:S(2)}) %collective-permute-start.6) | collective-permute-done | bytes 344096 | tf_op jit(solution)/shard_map/ppermute | solution.py:259
  86.0 0.1 add_convert_fusion.4
  86.1 4.7 %collective-permute-start.9 = (bf16[21,64,128]{2,1,0:T(8,128)(2,1)S(1)}, bf16[21,64,128]{2,1,0:T(8,128)(2,1)S(1)}, u32[]{:S(2)}, u32[]{:S(2)}) collective-permute-start(bf16[21,64,128]{2,1,0:T(8,128)(2,1)S(1)} %add_convert_fusion.4), channel_id=1, source_target_pairs={{0,448},{64,128},{128,320},{192,0},{256,192},{320,384},{384,64},{4... | collective-permute-start | bytes 1032200 | tf_op jit(solution)/shard_map/ppermute | solution.py:266
  90.8 1.9 %collective-permute-start.8 = (bf16[21,64,128]{2,1,0:T(8,128)(2,1)S(1)}, bf16[21,64,128]{2,1,0:T(8,128)(2,1)S(1)}, u32[]{:S(2)}, u32[]{:S(2)}) collective-permute-start(bf16[21,64,128]{2,1,0:T(8,128)(2,1)S(1)} %add_convert_fusion.4), channel_id=1, source_target_pairs={{0,64},{64,0},{128,192},{192,128},{256,320},{320,256},{384,448},{4... | collective-permute-start | bytes 1032200 | tf_op jit(solution)/shard_map/ppermute | solution.py:250
  92.7 2.5 %collective-permute-start.7 = (bf16[21,64,128]{2,1,0:T(8,128)(2,1)S(1)}, bf16[21,64,128]{2,1,0:T(8,128)(2,1)S(1)}, u32[]{:S(2)}, u32[]{:S(2)}) collective-permute-start(bf16[21,64,128]{2,1,0:T(8,128)(2,1)S(1)} %add_convert_fusion.4), channel_id=1, source_target_pairs={{0,384},{64,192},{128,256},{192,64},{256,128},{320,448},{384,0},{4... | collective-permute-start | bytes 1032200 | tf_op jit(solution)/shard_map/ppermute | solution.py:259
  95.2 1.7 %new_momentum.1 = f32[64,4,768]{2,1,0:T(4,128)} custom-call(s32[64]{0:T(128)S(1)} %copy-done.1, bf16[2,64,4,768]{3,2,1,0:T(4,128)(2,1)S(1)} %get-tuple-element.26.keep, bf16[2,64,4,768]{3,2,1,0:T(4,128)(2,1)S(1)} %collective-permute-done.swapped, bf16[64,4,768]{2,1,0:T(4,128)(2,1)S(1)} %collective-permute-done.2.first, ...), custom_call_target="tpu_custom_call" | custom-call | flops 1179648 | bytes 3145728 | tf_op jit(solution)/shard_map/new_momentum/pallas_call | solution.py:125
  96.9 0.0 collective-permute-done.9
  96.9 0.0 collective-permute-done.8
  96.9 0.1 add_convert_fusion.2.other
  97.0 6.0 %collective-permute-done.7 = bf16[21,64,128]{2,1,0:T(8,128)(2,1)S(1)} collective-permute-done((bf16[21,64,128]{2,1,0:T(8,128)(2,1)S(1)}, bf16[21,64,128]{2,1,0:T(8,128)(2,1)S(1)}, u32[]{:S(2)}, u32[]{:S(2)}) %collective-permute-start.7) | collective-permute-done | bytes 344096 | tf_op jit(solution)/shard_map/ppermute | solution.py:259
  103.0 0.1 add_convert_fusion.3.own
  103.2 4.5 %polish.1 = bf16[64,4,768]{2,1,0:T(4,128)(2,1)S(1)} custom-call(bf16[21,64,128]{2,1,0:T(8,128)(2,1)S(1)} %add_convert_fusion.3.own, bf16[21,64,128]{2,1,0:T(8,128)(2,1)S(1)} %add_convert_fusion.2.other, bf16[256,768]{1,0:T(8,128)(2,1)S(1)} %get-tuple-element.32.rows_ref), custom_call_target="tpu_custom_call" | custom-call | tf_op jit(solution)/shard_map/polish/pallas_call | solution.py:232
  107.6 31.4 %all_to_all.11 = bf16[64,4,768]{2,1,0:T(4,128)(2,1)S(1)} all-to-all(bf16[64,4,768]{2,1,0:T(4,128)(2,1)S(1)} %polish.1), channel_id=1, replica_groups=mesh['dp'=8,'fsdp'=64] {'fsdp'}, dimensions={0} | all-to-all | bytes 786432 | tf_op jit(solution)/shard_map/all_to_all | solution.py:270
  139.0 0.7 copy.6
Async XLA Ops:
  0.6 27.8 %copy-start.1 = (s32[64]{0:T(128)S(1)}, s32[64]{0:T(128)}, u32[]{:S(2)}) copy-start(s32[64]{0:T(128)} %slots.2) | copy-start | bytes 772
  0.6 27.8 %copy-start = (f32[64,4,768]{2,1,0:T(4,128)S(1)}, f32[64,4,768]{2,1,0:T(4,128)}, u32[]{:S(2)}) copy-start(f32[64,4,768]{2,1,0:T(4,128)} %mom.2) | copy-start | bytes 2359300
  2.8 4.3 %collective-permute-start.1 = (bf16[2,64,4,768]{3,2,1,0:T(4,128)(2,1)S(1)}, bf16[2,64,4,768]{3,2,1,0:T(4,128)(2,1)S(1)}, u32[]{:S(2)}, u32[]{:S(2)}) collective-permute-start(bf16[2,64,4,768]{3,2,1,0:T(4,128)(2,1)S(1)} %get-tuple-element.21), channel_id=1, source_target_pairs={{0,64},{64,0},{128,192},{192,128},{256,320},{320,256},{384,448},{4... | collective-permute-start | bytes 2359304 | tf_op jit(solution)/shard_map/ppermute | solution.py:250
  4.7 8.7 %collective-permute-start = (bf16[2,64,4,768]{3,2,1,0:T(4,128)(2,1)S(1)}, bf16[2,64,4,768]{3,2,1,0:T(4,128)(2,1)S(1)}, u32[]{:S(2)}, u32[]{:S(2)}) collective-permute-start(bf16[2,64,4,768]{3,2,1,0:T(4,128)(2,1)S(1)} %get-tuple-element.19), channel_id=1, source_target_pairs={{0,64},{64,0},{128,192},{192,128},{256,320},{320,256},{384,448},{4... | collective-permute-start | bytes 2359304 | tf_op jit(solution)/shard_map/ppermute | solution.py:250
  7.5 9.7 %collective-permute-start.3 = (bf16[64,4,768]{2,1,0:T(4,128)(2,1)S(1)}, bf16[64,4,768]{2,1,0:T(4,128)(2,1)S(1)}, u32[]{:S(2)}, u32[]{:S(2)}) collective-permute-start(bf16[64,4,768]{2,1,0:T(4,128)(2,1)S(1)} %get-tuple-element.34), channel_id=1, source_target_pairs={{0,128},{64,448},{128,0},{192,320},{256,384},{320,192},{384,256},{... | collective-permute-start | bytes 1179656 | tf_op jit(solution)/shard_map/ppermute | solution.py:259
  11.0 11.4 %collective-permute-start.2 = (bf16[64,4,768]{2,1,0:T(4,128)(2,1)S(1)}, bf16[64,4,768]{2,1,0:T(4,128)(2,1)S(1)}, u32[]{:S(2)}, u32[]{:S(2)}) collective-permute-start(bf16[64,4,768]{2,1,0:T(4,128)(2,1)S(1)} %get-tuple-element.35), channel_id=1, source_target_pairs={{0,128},{64,448},{128,0},{192,320},{256,384},{320,192},{384,256},{... | collective-permute-start | bytes 1179656 | tf_op jit(solution)/shard_map/ppermute | solution.py:259
  17.5 10.9 %collective-permute-start.4 = (bf16[64,4,768]{2,1,0:T(4,128)(2,1)S(1)}, bf16[64,4,768]{2,1,0:T(4,128)(2,1)S(1)}, u32[]{:S(2)}, u32[]{:S(2)}) collective-permute-start(bf16[64,4,768]{2,1,0:T(4,128)(2,1)S(1)} %fusion), channel_id=1, source_target_pairs={{0,384},{64,192},{128,256},{192,64},{256,128},{320,448},{384,0},{4... | collective-permute-start | bytes 1179656 | tf_op jit(solution)/shard_map/ppermute | solution.py:259
  73.2 3.5 %collective-permute-start.5 = (bf16[21,64,128]{2,1,0:T(8,128)(2,1)S(1)}, bf16[21,64,128]{2,1,0:T(8,128)(2,1)S(1)}, u32[]{:S(2)}, u32[]{:S(2)}) collective-permute-start(bf16[21,64,128]{2,1,0:T(8,128)(2,1)S(1)} %get-tuple-element.24), channel_id=1, source_target_pairs={{0,64},{64,0},{128,192},{192,128},{256,320},{320,256},{384,448},{4... | collective-permute-start | bytes 1032200 | tf_op jit(solution)/shard_map/ppermute | solution.py:250
  76.8 9.1 %collective-permute-start.6 = (bf16[21,64,128]{2,1,0:T(8,128)(2,1)S(1)}, bf16[21,64,128]{2,1,0:T(8,128)(2,1)S(1)}, u32[]{:S(2)}, u32[]{:S(2)}) collective-permute-start(bf16[21,64,128]{2,1,0:T(8,128)(2,1)S(1)} %fusion.1), channel_id=1, source_target_pairs={{0,128},{64,448},{128,0},{192,320},{256,384},{320,192},{384,256},{... | collective-permute-start | bytes 1032200 | tf_op jit(solution)/shard_map/ppermute | solution.py:259
  86.1 10.8 %collective-permute-start.9 = (bf16[21,64,128]{2,1,0:T(8,128)(2,1)S(1)}, bf16[21,64,128]{2,1,0:T(8,128)(2,1)S(1)}, u32[]{:S(2)}, u32[]{:S(2)}) collective-permute-start(bf16[21,64,128]{2,1,0:T(8,128)(2,1)S(1)} %add_convert_fusion.4), channel_id=1, source_target_pairs={{0,448},{64,128},{128,320},{192,0},{256,192},{320,384},{384,64},{4... | collective-permute-start | bytes 1032200 | tf_op jit(solution)/shard_map/ppermute | solution.py:266
  90.8 6.1 %collective-permute-start.8 = (bf16[21,64,128]{2,1,0:T(8,128)(2,1)S(1)}, bf16[21,64,128]{2,1,0:T(8,128)(2,1)S(1)}, u32[]{:S(2)}, u32[]{:S(2)}) collective-permute-start(bf16[21,64,128]{2,1,0:T(8,128)(2,1)S(1)} %add_convert_fusion.4), channel_id=1, source_target_pairs={{0,64},{64,0},{128,192},{192,128},{256,320},{320,256},{384,448},{4... | collective-permute-start | bytes 1032200 | tf_op jit(solution)/shard_map/ppermute | solution.py:250
  92.7 10.4 %collective-permute-start.7 = (bf16[21,64,128]{2,1,0:T(8,128)(2,1)S(1)}, bf16[21,64,128]{2,1,0:T(8,128)(2,1)S(1)}, u32[]{:S(2)}, u32[]{:S(2)}) collective-permute-start(bf16[21,64,128]{2,1,0:T(8,128)(2,1)S(1)} %add_convert_fusion.4), channel_id=1, source_target_pairs={{0,384},{64,192},{128,256},{192,64},{256,128},{320,448},{384,0},{4... | collective-permute-start | bytes 1032200 | tf_op jit(solution)/shard_map/ppermute | solution.py:259
